TPU v7x, 32 devices: a whole 2x2x4 slice. The times are simulated.
32 devices in a mesh: seg: 2 (over y), bundle: 16 (over z, x, core).
Axes of the slice: x: 2, y: 2, z: 4, core: 2. Of those that a mesh axis runs over, the one named last changes fastest.
Arguments:
- conc: float32 [64, 16, 1024], P('bundle', None, 'seg'), may hold values from -6 to 6
- slowness: float32 [64, 1024], P('bundle', 'seg'), may hold values from 0 to 3
- retard: float32 [16], replicated, may hold values from 0.05 to 30.72
- taps: float32 [16, 33], replicated, may hold values from -0.12 to 0.12
- inlet: float32 [64, 16], P('bundle'), may hold values from -6 to 6
- grid: float32 [16, 65536], P(None, ('seg', 'bundle')), may hold values from -6 to 6
- kappa: float32 [65536], P(('seg', 'bundle')), may hold values from 0.05 to 0.5
- owners: int32 [2, 64, 4, 1], P('seg', 'bundle'), may hold values from 0 to 15; in each aligned block of 16 rows (0 to 15, 16 to 31, ..., all dimensions but the last counted through in order) at most 2 rows name the same one
- cells: int32 [64, 1024], P('bundle', 'seg'), may hold values from 0 to 2047
Outputs:
- conc_out: float32 [64, 16, 1024], P('bundle', None, 'seg')
- grid_out: float32 [16, 65536], P(None, ('seg', 'bundle'))
Inputs may be any that keep to these rules, and one draw needn't show every extreme that they name: `owners`: among the node blocks of one device (one segment of 4 streamlines), at most 2 name the same owner.
All inputs are finite; a program needn't handle non-finite values.
Results may differ from a plain program's by a relative error of at most 0.00022.
Values sent between devices are 32-bit elements; how exact they have to be, the bound alone decides.
No kernel may reach another device: no remote copies, remote signals or barrier semaphores. Data moves between devices by JAX's collectives and lax.ppermute only.
A program may use at most 128 MiB of HBM per device.

v0:
```python
import functools

import jax
import jax.numpy as jnp
from jax import lax
from jax.experimental import pallas as pl
from jax.experimental.pallas import tpu as pltpu
from jax.sharding import PartitionSpec as P

STEPS = 4
LANES = 128
HALF = 16
F32 = jnp.float32
BF16 = jnp.bfloat16

VMEM = pl.BlockSpec(memory_space=pltpu.VMEM)
SMEM = pl.BlockSpec(memory_space=pltpu.SMEM)


def call(kernel, outs, ins, out_specs=None, scratch=(), flops=100_000):
    args = [a for a, _ in ins]
    size = sum(a.size * 4 for a in args) + sum(o.size * 4 for o in outs)
    return pl.pallas_call(
        kernel,
        out_shape=outs,
        in_specs=[s for _, s in ins],
        out_specs=out_specs or [VMEM] * len(outs),
        scratch_shapes=list(scratch),
        cost_estimate=pl.CostEstimate(flops=flops, bytes_accessed=size, transcendentals=0),
        compiler_params=pltpu.CompilerParams(vmem_limit_bytes=40 * 1024 * 1024),
    )(*args)


def sds(shape, dtype=F32):
    return jax.ShapeDtypeStruct(shape, dtype)


def route_kernel(groups, cap, owners, cells, slot, send, count):
    blocks = slot.shape[0]
    owners_total = send.shape[0]
    send[...] = jnp.full(send.shape, -1, jnp.int32)
    for o in range(owners_total):
        count[o] = 0
    for b in range(blocks):
        line, group = b // groups, b % groups
        owner = owners[b]
        rank = count[owner]
        count[owner] = rank + 1
        slot[b] = owner * cap + rank
        send[owner, pl.ds(rank, 1), :] = cells[
            pl.ds(line, 1), group * LANES : (group + 1) * LANES
        ]


def where_slot(slot, b, cap):
    s = slot[b]
    return s // cap, s % cap


def block_scan(retain, value, lane):
    factor, offset = retain, (1.0 - retain) * value
    shift = 1
    while shift < LANES:
        inside = lane >= shift
        offset = offset + jnp.where(inside, factor * pltpu.roll(offset, shift, 1), 0.0)
        factor = jnp.where(inside, factor * pltpu.roll(factor, shift, 1), factor)
        shift *= 2
    return factor, offset


def last_lane(x):
    return jnp.broadcast_to(x[:, LANES - 1 : LANES], x.shape)


def scan_line(retains, values, lane):
    factors, offsets = [], []
    for retain, value in zip(retains, values):
        factor, offset = block_scan(retain, value, lane)
        if factors:
            offset = offset + factor * last_lane(offsets[-1])
            factor = factor * last_lane(factors[-1])
        factors.append(factor)
        offsets.append(offset)
    return factors, offsets


def column(ref_at, rows):
    row = lax.broadcasted_iota(jnp.int32, (rows, LANES), 0)
    out = jnp.zeros((rows, LANES), F32)
    for k in range(rows):
        out = jnp.where(row == k, ref_at(k), out)
    return out


def tile(ref, line, comps, group):
    return ref[pl.ds(line * comps, comps), group * LANES : (group + 1) * LANES]


def put(ref, line, comps, group, value):
    ref[pl.ds(line * comps, comps), group * LANES : (group + 1) * LANES] = value


def first_kernel(lines, comps, groups, conc, slowness, retard, retain, offset, factor, ends):
    lane = lax.broadcasted_iota(jnp.int32, (comps, LANES), 1)
    slow_by = column(lambda k: retard[k], comps)
    for line in range(lines):
        retains, values = [], []
        for group in range(groups):
            s = slowness[pl.ds(line, 1), group * LANES : (group + 1) * LANES]
            r = 1.0 / (1.0 + slow_by * s)
            put(retain, line, comps, group, r)
            retains.append(r)
            values.append(conc[line, :, group * LANES : (group + 1) * LANES])
        factors, offsets = scan_line(retains, values, lane)
        for group in range(groups):
            put(factor, line, comps, group, factors[group])
            put(offset, line, comps, group, offsets[group])
        ends[0, pl.ds(line * comps, comps), :] = jnp.where(lane < 64, offsets[0], offsets[-1])
        ends[1, pl.ds(line * comps, comps), :] = jnp.where(lane < 64, factors[0], factors[-1])


def spread_kernel(
    lines, comps, groups, cap, segs, has_gather,
    offset, factor, end_offset, end_factor, other_offset, other_factor, taps, inlet, slot, spread, send,
):
    taps_total = taps.shape[1]
    me = lax.axis_index("seg")
    lane = lax.broadcasted_iota(jnp.int32, (comps, LANES), 1)
    columns = [jnp.broadcast_to(taps[:, t : t + 1], (comps, LANES)) for t in range(taps_total)]
    for line in range(lines):
        rows = pl.ds(line * comps, comps)

        def part(s):
            if has_gather:
                return other_offset[s, rows, :], other_factor[s, rows, :]
            mine = me == s
            return (
                jnp.where(mine, end_offset[0, rows, :], other_offset[0, rows, :]),
                jnp.where(mine, end_factor[1, rows, :], other_factor[1, rows, :]),
            )

        flow = column(lambda k: inlet[line, k], comps)
        zero = jnp.zeros((comps, LANES), F32)
        left, right, inflow = zero, zero, zero
        for s in range(segs):
            inflow = jnp.where(me == s, flow, inflow)
            off, fac = part(s)
            edge = off + fac * flow
            left = jnp.where(me == s + 1, edge, left)
            right = jnp.where(me == s - 1, edge, right)
            flow = last_lane(edge)
        up = [left]
        for group in range(groups):
            up.append(tile(offset, line, comps, group) + tile(factor, line, comps, group) * inflow)
        up.append(right)
        for group in range(groups):
            before, here, after = up[group], up[group + 1], up[group + 2]
            total = here + columns[HALF] * here
            for d in range(1, HALF + 1):
                low = pltpu.roll(jnp.where(lane >= LANES - d, before, here), d, 1)
                high = pltpu.roll(jnp.where(lane < d, after, here), LANES - d, 1)
                total = total + columns[HALF - d] * low + columns[HALF + d] * high
            put(spread, line, comps, group, total)
            owner, rank = where_slot(slot, line * groups + group, cap)
            send[owner, pl.ds(pl.multiple_of(rank * comps, 8), comps), :] = total


def conc_kernel(lines, comps, groups, cap, first, last, spread, got, coupling, retain, slot, *outs):
    lane = lax.broadcasted_iota(jnp.int32, (comps, LANES), 1)
    outs = list(outs)
    coupling_out = outs.pop() if first else None
    for line in range(lines):
        values, retains = [], []
        for group in range(groups):
            b = line * groups + group
            owner, rank = where_slot(slot, b, cap)
            looked = got[owner, pl.ds(pl.multiple_of(rank * comps, 8), comps), :]
            if first:
                rate = got[owner, pl.ds(cap * comps + rank, 1), :]
                coupling_out[pl.ds(b, 1), :] = rate
            else:
                rate = coupling[pl.ds(b, 1), :]
            s = tile(spread, line, comps, group)
            value = s + rate * (looked - s)
            if last:
                outs[0][line, :, group * LANES : (group + 1) * LANES] = value
            values.append(value)
            if not last:
                retains.append(tile(retain, line, comps, group))
        if last:
            continue
        _, offsets = scan_line(retains, values, lane)
        for group in range(groups):
            put(outs[0], line, comps, group, offsets[group])
        outs[1][0, pl.ds(line * comps, comps), :] = jnp.where(lane < 64, offsets[0], offsets[-1])


def gather_cells(grid, cell, comps, high_total):
    low = jnp.broadcast_to(cell & (LANES - 1), (comps, LANES))
    high = jnp.broadcast_to(cell >> 7, (comps, LANES))
    out = jnp.zeros((comps, LANES), F32)
    for h in range(high_total):
        g = jnp.take_along_axis(
            grid[:, h * LANES : (h + 1) * LANES], low, axis=1, mode="promise_in_bounds"
        )
        out = jnp.where(high == h, g, out)
    return out


def look_first_kernel(cap, cells, grid, kappa, send, rates):
    comps = grid.shape[0]
    high_total = grid.shape[1] // LANES
    row = lax.broadcasted_iota(jnp.int32, (high_total, LANES), 0)

    def one(owner, carry):
        for rank in range(cap):
            cell = cells[owner, pl.ds(rank, 1), :]
            valid = cell >= 0
            cell = jnp.maximum(cell, 0)
            send[owner, rank * comps : (rank + 1) * comps, :] = gather_cells(
                grid, cell, comps, high_total
            )
            low = jnp.broadcast_to(cell & (LANES - 1), (high_total, LANES))
            k = jnp.take_along_axis(kappa[...], low, axis=1, mode="promise_in_bounds")
            rate = jnp.sum(jnp.where(row == (cell >> 7), k, 0.0), axis=0, keepdims=True)
            rate = jnp.where(valid, rate, 0.0)
            rates[owner, pl.ds(rank, 1), :] = rate
            send[owner, pl.ds(cap * comps + rank, 1), :] = rate
        return carry

    lax.fori_loop(0, cells.shape[0], one, 0, unroll=4)


def update_kernel(cap, chunk, last, cells, arrived, looked, rates, grid, *rest):
    if last:
        grid_out, masked, onehot = rest
    else:
        grid_out, send, masked, onehot = rest
    comps = grid.shape[0]
    high_total = grid.shape[1] // LANES
    owners_total = cells.shape[0]
    rows = high_total * comps
    lane_row = lax.broadcasted_iota(jnp.int32, (LANES, LANES), 0).astype(F32)
    total = None
    for start in range(0, owners_total, chunk):

        for i in range(chunk):
            owner = start + i
            for rank in range(cap):
                at = (i * cap + rank) * LANES
                cell = cells[owner, rank : rank + 1, :]
                valid = jnp.broadcast_to(cell, (comps, LANES)) >= 0
                cell = jnp.maximum(cell, 0)
                rate = rates[owner, rank : rank + 1, :]
                span = slice(rank * comps, (rank + 1) * comps)
                flux = jnp.where(valid, rate * (looked[owner, span, :] - arrived[owner, span, :]), 0.0)
                coarse = flux.astype(BF16)
                fine = (flux - coarse.astype(F32)).astype(BF16)
                high = jnp.broadcast_to((cell >> 7).astype(F32), (comps, LANES)).astype(BF16)
                for h in range(high_total):
                    hit = high == jnp.asarray(h, BF16)
                    masked[h * comps : (h + 1) * comps, at : at + LANES] = jnp.where(
                        hit, coarse, jnp.zeros_like(coarse)
                    )
                    masked[rows + h * comps : rows + (h + 1) * comps, at : at + LANES] = jnp.where(
                        hit, fine, jnp.zeros_like(fine)
                    )
                low = (cell & (LANES - 1)).astype(F32)
                onehot[:, at : at + LANES] = jnp.where(lane_row == low, 1.0, 0.0).astype(BF16)
        part = lax.dot_general(
            masked[...], onehot[...], (((1,), (1,)), ((), ())), preferred_element_type=F32
        )
        total = part if total is None else total + part
    for h in range(high_total):
        span = slice(h * LANES, (h + 1) * LANES)
        at = slice(h * comps, (h + 1) * comps)
        at2 = slice(rows + h * comps, rows + (h + 1) * comps)
        grid_out[:, span] = grid[:, span] - 0.25 * (total[at, :] + total[at2, :])
    if last:
        return

    def one(owner, carry):
        for rank in range(cap):
            cell = jnp.maximum(cells[owner, pl.ds(rank, 1), :], 0)
            send[owner, rank * comps : (rank + 1) * comps, :] = gather_cells(
                grid_out, cell, comps, high_total
            )
        return carry

    lax.fori_loop(0, owners_total, one, 0, unroll=4)


def swap(x, segs):
    if segs == 2:
        return lax.ppermute(x, "seg", [(0, 1), (1, 0)])
    return lax.all_gather(x, "seg")


def exchange(x):
    return lax.all_to_all(x, "bundle", split_axis=0, concat_axis=0, tiled=True)


def per_device(conc, slowness, retard, taps, inlet, grid, kappa, owners, cells):
    lines, comps, nodes = conc.shape
    groups = nodes // LANES
    blocks = lines * groups
    segs = lax.axis_size("seg")
    owners_total = lax.axis_size("bundle")
    cap = max(2, 2 * blocks // owners_total)
    rows = lines * comps
    cell_count = grid.shape[1]
    chunk = 16 if owners_total % 16 == 0 else owners_total

    slot, cell_send = call(
        functools.partial(route_kernel, groups, cap),
        [sds((blocks,), jnp.int32), sds((owners_total, cap, LANES), jnp.int32)],
        [(owners.reshape(blocks), SMEM), (cells, VMEM)],
        out_specs=[SMEM, VMEM],
        scratch=[pltpu.SMEM((owners_total,), jnp.int32)],
    )
    cell_recv = exchange(cell_send)

    retain, offset, factor, ends = call(
        functools.partial(first_kernel, lines, comps, groups),
        [sds((rows, nodes))] * 3 + [sds((2, rows, LANES))],
        [(conc, VMEM), (slowness, VMEM), (retard, SMEM)],
    )
    first_ends = ends
    other = swap(ends, segs)
    if segs == 2:
        other_offset = other_factor = other
    else:
        other_offset, other_factor = other[:, 0], other[:, 1]

    looked, rates = call(
        functools.partial(look_first_kernel, cap),
        [sds((owners_total, cap * comps + 8 * (-(-cap // 8)), LANES)), sds((owners_total, cap, LANES))],
        [(cell_recv, VMEM), (grid, VMEM), (kappa.reshape(cell_count // LANES, LANES), VMEM)],
    )
    coupling = None
    for step in range(STEPS):
        last = step == STEPS - 1
        spread, send = call(
            functools.partial(spread_kernel, lines, comps, groups, cap, segs, segs != 2),
            [sds((rows, nodes)), sds((owners_total, cap * comps, LANES))],
            [
                (offset, VMEM), (factor, VMEM), (ends, VMEM), (first_ends, VMEM),
                (other_offset, VMEM), (other_factor, VMEM), (taps, VMEM), (inlet, SMEM), (slot, SMEM),
            ],
        )
        arrived = exchange(send)
        got = exchange(looked)
        outs = [sds(conc.shape)] if last else [sds((rows, nodes)), sds((1, rows, LANES))]
        if step == 0:
            outs.append(sds((blocks, LANES)))
        result = call(
            functools.partial(conc_kernel, lines, comps, groups, cap, step == 0, last),
            outs,
            [
                (spread, VMEM), (got, VMEM), (slowness if step == 0 else coupling, VMEM),
                (retain, VMEM), (slot, SMEM),
            ],
        )
        if step == 0:
            coupling = result[-1]
        if last:
            conc_out = result[0]
        else:
            offset, ends = result[0], result[1]
            got_ends = swap(ends, segs)
            other_offset = got_ends if segs == 2 else got_ends[:, 0]
        outs = [sds(grid.shape)]
        if not last:
            outs.append(sds((owners_total, cap * comps, LANES)))
        result = call(
            functools.partial(update_kernel, cap, chunk, last),
            outs,
            [(cell_recv, VMEM), (arrived, VMEM), (looked, VMEM), (rates, VMEM), (grid, VMEM)],
            scratch=[
                pltpu.VMEM((2 * (cell_count // LANES) * comps, chunk * cap * LANES), BF16),
                pltpu.VMEM((LANES, chunk * cap * LANES), BF16),
            ],
        )
        grid = result[0]
        if not last:
            looked = result[1]
    return (conc_out, grid)


def solution(mesh):
    return jax.shard_map(
        per_device,
        mesh=mesh,
        in_specs=(
            P("bundle", None, "seg"),
            P("bundle", "seg"),
            P(),
            P(),
            P("bundle", None),
            P(None, ("seg", "bundle")),
            P(("seg", "bundle")),
            P("seg", "bundle", None, None),
            P("bundle", "seg"),
        ),
        out_specs=(P("bundle", None, "seg"), P(None, ("seg", "bundle"))),
        check_vma=False,
    )
```

profile of v0, /device:TPU:0, one launch (start us, length us, event | category | flops | bytes accessed | tf_op | source)
XLA Modules:
  0.0 137.9 jit_solution(6996332665963782108)
XLA Ops:
  0.6 0.9 copy-done.2
  1.5 0.7 copy-done.4
  2.2 0.7 copy-done.8
  2.9 1.5 %shard_map.104 = (f32[64,512]{1,0:T(8,128)S(1)}, f32[64,512]{1,0:T(8,128)S(1)}, f32[64,512]{1,0:T(8,128)S(1)}, f32[2,64,128]{2,1,0:T(8,128)S(1)}) custom-call(f32[4,16,512]{2,1,0:T(8,128)S(1)} %copy-done.2, f32[4,512]{1,0:T(4,128)S(1)} %copy-done.4, f32[16]{0:T(128)S(1)} %copy-done.8), custom_call_target="tpu_custom_call" | custom-call | flops 100000 | bytes 598080 | tf_op jit(solution)/shard_map/pallas_call | solution.py:23
  4.4 0.0 copy-start.7
  4.4 3.0 %collective-permute-start = (f32[2,64,128]{2,1,0:T(8,128)S(1)}, f32[2,64,128]{2,1,0:T(8,128)S(1)}, u32[]{:S(2)}, u32[]{:S(2)}) collective-permute-start(f32[2,64,128]{2,1,0:T(8,128)S(1)} %get-tuple-element.33.end_offset.end_factor), channel_id=1, source_target_pairs={{0,16},{16,0},{1,17},{17,1},{2,18},{18,2},{3,19},{19,3},{4,20},{20... | collective-permute-start | bytes 196616 | tf_op jit(solution)/shard_map/ppermute | solution.py:295
  7.4 0.5 broadcast.3
  7.9 0.7 reduce.3
  8.6 0.1 reshape.10.owners
  8.7 1.2 shard_map.105
  9.9 5.9 %all-to-all-start = ((s32[16,2,128]{2,1,0:T(2,128)}), s32[16,2,128]{2,1,0:T(2,128)S(1)}, u32[]{:S(2)}, u32[]{:S(2)}) async-start(s32[16,2,128]{2,1,0:T(2,128)} %get-tuple-element.36), calls=%async_computation | async-start | bytes 32768 | tf_op jit(solution)/shard_map/all_to_all | solution.py:300
  15.9 0.7 copy-done.3
  16.5 2.9 %shard_map.106 = (f32[64,512]{1,0:T(8,128)S(1)}, f32[16,32,128]{2,1,0:T(8,128)}) custom-call(f32[64,512]{1,0:T(8,128)S(1)} %get-tuple-element.31.offset, f32[64,512]{1,0:T(8,128)S(1)} %get-tuple-element.32.factor, f32[2,64,128]{2,1,0:T(8,128)S(1)} %get-tuple-element.33.end_offset.end_factor, f32[2,64,128]{2,1,0:T(8,128)S(1)} %get-tuple-element.33.end_offset.end_factor, ...), custom_call_target="tpu_custom_call" | custom-call | flops 100000 | bytes 919936 | tf_op jit(solution)/shard_map/pallas_call | solution.py:23
  19.4 2.9 %all-to-all-done.cells = s32[16,2,128]{2,1,0:T(2,128)S(1)} async-done(((s32[16,2,128]{2,1,0:T(2,128)}), s32[16,2,128]{2,1,0:T(2,128)S(1)}, u32[]{:S(2)}, u32[]{:S(2)}) %all-to-all-start) | async-done | bytes 16416 | tf_op jit(solution)/shard_map/all_to_all | solution.py:300
  22.3 3.7 %all-to-all-start.2 = ((f32[16,32,128]{2,1,0:T(8,128)}), f32[16,32,128]{2,1,0:T(8,128)S(1)}, u32[]{:S(2)}, u32[]{:S(2)}) async-start(f32[16,32,128]{2,1,0:T(8,128)} %get-tuple-element.42), calls=%async_computation.2 | async-start | bytes 524288 | tf_op jit(solution)/shard_map/all_to_all | solution.py:300
  26.0 2.3 %shard_map.107 = (f32[16,40,128]{2,1,0:T(8,128)}, f32[16,2,128]{2,1,0:T(2,128)S(1)}) custom-call(s32[16,2,128]{2,1,0:T(2,128)S(1)} %all-to-all-done.cells, f32[16,2048]{1,0:T(8,128)S(1)} %copy-done, f32[16,128]{1,0:T(8,128)S(1)} %bitcast.2), custom_call_target="tpu_custom_call" | custom-call | flops 100000 | bytes 499712 | tf_op jit(solution)/shard_map/pallas_call | solution.py:23
  28.3 7.7 %all-to-all-done.2.arrived = f32[16,32,128]{2,1,0:T(8,128)S(1)} async-done(((f32[16,32,128]{2,1,0:T(8,128)}), f32[16,32,128]{2,1,0:T(8,128)S(1)}, u32[]{:S(2)}, u32[]{:S(2)}) %all-to-all-start.2) | async-done | bytes 262176 | tf_op jit(solution)/shard_map/all_to_all | solution.py:300
  36.0 3.5 %all-to-all-start.1 = ((f32[16,40,128]{2,1,0:T(8,128)}), f32[16,40,128]{2,1,0:T(8,128)S(1)}, u32[]{:S(2)}, u32[]{:S(2)}) async-start(f32[16,40,128]{2,1,0:T(8,128)} %get-tuple-element.37.looked), calls=%async_computation.1 | async-start | bytes 655360 | tf_op jit(solution)/shard_map/all_to_all | solution.py:300
  39.6 4.6 %shard_map.110 = (f32[16,2048]{1,0:T(8,128)S(1)}, f32[16,32,128]{2,1,0:T(8,128)}) custom-call(s32[16,2,128]{2,1,0:T(2,128)S(1)} %all-to-all-done.cells, f32[16,32,128]{2,1,0:T(8,128)S(1)} %all-to-all-done.2.arrived, f32[16,40,128]{2,1,0:T(8,128)} %get-tuple-element.37.looked, f32[16,2,128]{2,1,0:T(2,128)S(1)} %get-tuple-element.43.rates, f32[16,2048]{1,0:T(8,128)S(1)} %copy-done), custom_call_target="tpu_custom_call" | custom-call | flops 100000 | bytes 1146880 | tf_op jit(solution)/shard_map/pallas_call | solution.py:23
  44.2 6.4 %all-to-all-done.1.got = f32[16,40,128]{2,1,0:T(8,128)S(1)} async-done(((f32[16,40,128]{2,1,0:T(8,128)}), f32[16,40,128]{2,1,0:T(8,128)S(1)}, u32[]{:S(2)}, u32[]{:S(2)}) %all-to-all-start.1) | async-done | bytes 327712 | tf_op jit(solution)/shard_map/all_to_all | solution.py:300
  50.6 3.7 %all-to-all-start.3 = ((f32[16,32,128]{2,1,0:T(8,128)}), f32[16,32,128]{2,1,0:T(8,128)S(1)}, u32[]{:S(2)}, u32[]{:S(2)}) async-start(f32[16,32,128]{2,1,0:T(8,128)} %get-tuple-element.44.looked), calls=%async_computation.3 | async-start | bytes 524288 | tf_op jit(solution)/shard_map/all_to_all | solution.py:300
  54.3 1.5 %shard_map.108 = (f32[64,512]{1,0:T(8,128)S(1)}, f32[1,64,128]{2,1,0:T(8,128)S(1)}, f32[16,128]{1,0:T(8,128)S(1)}) custom-call(f32[64,512]{1,0:T(8,128)S(1)} %get-tuple-element.35.spread, f32[16,40,128]{2,1,0:T(8,128)S(1)} %all-to-all-done.1.got, f32[4,512]{1,0:T(4,128)S(1)} %copy-done.5, f32[64,512]{1,0:T(8,128)S(1)} %get-tuple-element.38.retain, ...), custom_call_target="tpu_custom_call" | custom-call | flops 100000 | bytes 770112 | tf_op jit(solution)/shard_map/pallas_call | solution.py:23
  55.8 0.6 collective-permute-start.1
  56.4 3.4 %collective-permute-done.1.other_offset = f32[1,64,128]{2,1,0:T(8,128)S(1)} collective-permute-done((f32[1,64,128]{2,1,0:T(8,128)S(1)}, f32[1,64,128]{2,1,0:T(8,128)S(1)}, u32[]{:S(2)}, u32[]{:S(2)}) %collective-permute-start.1) | collective-permute-done | bytes 32800 | tf_op jit(solution)/shard_map/ppermute | solution.py:295
  59.8 2.9 %shard_map.109 = (f32[64,512]{1,0:T(8,128)S(1)}, f32[16,32,128]{2,1,0:T(8,128)}) custom-call(f32[64,512]{1,0:T(8,128)S(1)} %get-tuple-element.39.offset, f32[64,512]{1,0:T(8,128)S(1)} %get-tuple-element.32.factor, f32[1,64,128]{2,1,0:T(8,128)S(1)} %get-tuple-element.40.end_offset, f32[2,64,128]{2,1,0:T(8,128)S(1)} %get-tuple-element.33.end_offset.end_factor, ...), custom_call_target="tpu_custom_call" | custom-call | flops 100000 | bytes 854400 | tf_op jit(solution)/shard_map/pallas_call | solution.py:23
  62.7 1.6 %all-to-all-done.3.got = f32[16,32,128]{2,1,0:T(8,128)S(1)} async-done(((f32[16,32,128]{2,1,0:T(8,128)}), f32[16,32,128]{2,1,0:T(8,128)S(1)}, u32[]{:S(2)}, u32[]{:S(2)}) %all-to-all-start.3) | async-done | bytes 262176 | tf_op jit(solution)/shard_map/all_to_all | solution.py:300
  64.3 4.4 %all-to-all-start.4 = ((f32[16,32,128]{2,1,0:T(8,128)}), f32[16,32,128]{2,1,0:T(8,128)S(1)}, u32[]{:S(2)}, u32[]{:S(2)}) async-start(f32[16,32,128]{2,1,0:T(8,128)} %get-tuple-element.49), calls=%async_computation.4 | async-start | bytes 524288 | tf_op jit(solution)/shard_map/all_to_all | solution.py:300
  68.7 1.5 %shard_map.111 = (f32[64,512]{1,0:T(8,128)S(1)}, f32[1,64,128]{2,1,0:T(8,128)S(1)}) custom-call(f32[64,512]{1,0:T(8,128)S(1)} %get-tuple-element.41.spread, f32[16,32,128]{2,1,0:T(8,128)S(1)} %all-to-all-done.3.got, f32[16,128]{1,0:T(8,128)S(1)} %get-tuple-element.45.coupling, f32[64,512]{1,0:T(8,128)S(1)} %get-tuple-element.38.retain, ...), custom_call_target="tpu_custom_call" | custom-call | flops 100000 | bytes 696384 | tf_op jit(solution)/shard_map/pallas_call | solution.py:23
  70.2 0.6 collective-permute-start.2
  70.8 3.4 %collective-permute-done.2.other_offset = f32[1,64,128]{2,1,0:T(8,128)S(1)} collective-permute-done((f32[1,64,128]{2,1,0:T(8,128)S(1)}, f32[1,64,128]{2,1,0:T(8,128)S(1)}, u32[]{:S(2)}, u32[]{:S(2)}) %collective-permute-start.2) | collective-permute-done | bytes 32800 | tf_op jit(solution)/shard_map/ppermute | solution.py:295
  74.2 2.9 %shard_map.112 = (f32[64,512]{1,0:T(8,128)S(1)}, f32[16,32,128]{2,1,0:T(8,128)}) custom-call(f32[64,512]{1,0:T(8,128)S(1)} %get-tuple-element.46.offset, f32[64,512]{1,0:T(8,128)S(1)} %get-tuple-element.32.factor, f32[1,64,128]{2,1,0:T(8,128)S(1)} %get-tuple-element.47.end_offset, f32[2,64,128]{2,1,0:T(8,128)S(1)} %get-tuple-element.33.end_offset.end_factor, ...), custom_call_target="tpu_custom_call" | custom-call | flops 100000 | bytes 854400 | tf_op jit(solution)/shard_map/pallas_call | solution.py:23
  77.1 1.7 %all-to-all-done.4.arrived = f32[16,32,128]{2,1,0:T(8,128)S(1)} async-done(((f32[16,32,128]{2,1,0:T(8,128)}), f32[16,32,128]{2,1,0:T(8,128)S(1)}, u32[]{:S(2)}, u32[]{:S(2)}) %all-to-all-start.4) | async-done | bytes 262176 | tf_op jit(solution)/shard_map/all_to_all | solution.py:300
  78.8 4.4 %all-to-all-start.6 = ((f32[16,32,128]{2,1,0:T(8,128)}), f32[16,32,128]{2,1,0:T(8,128)S(1)}, u32[]{:S(2)}, u32[]{:S(2)}) async-start(f32[16,32,128]{2,1,0:T(8,128)} %get-tuple-element.55), calls=%async_computation.6 | async-start | bytes 524288 | tf_op jit(solution)/shard_map/all_to_all | solution.py:300
  83.1 4.6 %shard_map.113 = (f32[16,2048]{1,0:T(8,128)S(1)}, f32[16,32,128]{2,1,0:T(8,128)}) custom-call(s32[16,2,128]{2,1,0:T(2,128)S(1)} %all-to-all-done.cells, f32[16,32,128]{2,1,0:T(8,128)S(1)} %all-to-all-done.4.arrived, f32[16,32,128]{2,1,0:T(8,128)} %get-tuple-element.44.looked, f32[16,2,128]{2,1,0:T(2,128)S(1)} %get-tuple-element.43.rates, ...), custom_call_target="tpu_custom_call" | custom-call | flops 100000 | bytes 1081344 | tf_op jit(solution)/shard_map/pallas_call | solution.py:23
  87.7 5.5 %all-to-all-done.6.arrived = f32[16,32,128]{2,1,0:T(8,128)S(1)} async-done(((f32[16,32,128]{2,1,0:T(8,128)}), f32[16,32,128]{2,1,0:T(8,128)S(1)}, u32[]{:S(2)}, u32[]{:S(2)}) %all-to-all-start.6) | async-done | bytes 262176 | tf_op jit(solution)/shard_map/all_to_all | solution.py:300
  93.2 3.7 %all-to-all-start.5 = ((f32[16,32,128]{2,1,0:T(8,128)}), f32[16,32,128]{2,1,0:T(8,128)S(1)}, u32[]{:S(2)}, u32[]{:S(2)}) async-start(f32[16,32,128]{2,1,0:T(8,128)} %get-tuple-element.51.looked), calls=%async_computation.5 | async-start | bytes 524288 | tf_op jit(solution)/shard_map/all_to_all | solution.py:300
  96.9 4.6 %shard_map.116 = (f32[16,2048]{1,0:T(8,128)S(1)}, f32[16,32,128]{2,1,0:T(8,128)}) custom-call(s32[16,2,128]{2,1,0:T(2,128)S(1)} %all-to-all-done.cells, f32[16,32,128]{2,1,0:T(8,128)S(1)} %all-to-all-done.6.arrived, f32[16,32,128]{2,1,0:T(8,128)} %get-tuple-element.51.looked, f32[16,2,128]{2,1,0:T(2,128)S(1)} %get-tuple-element.43.rates, ...), custom_call_target="tpu_custom_call" | custom-call | flops 100000 | bytes 1081344 | tf_op jit(solution)/shard_map/pallas_call | solution.py:23
  101.5 5.4 %all-to-all-done.5.got = f32[16,32,128]{2,1,0:T(8,128)S(1)} async-done(((f32[16,32,128]{2,1,0:T(8,128)}), f32[16,32,128]{2,1,0:T(8,128)S(1)}, u32[]{:S(2)}, u32[]{:S(2)}) %all-to-all-start.5) | async-done | bytes 262176 | tf_op jit(solution)/shard_map/all_to_all | solution.py:300
  106.9 3.5 %all-to-all-start.7 = ((f32[16,32,128]{2,1,0:T(8,128)}), f32[16,32,128]{2,1,0:T(8,128)S(1)}, u32[]{:S(2)}, u32[]{:S(2)}) async-start(f32[16,32,128]{2,1,0:T(8,128)} %get-tuple-element.57.looked), calls=%async_computation.7 | async-start | bytes 524288 | tf_op jit(solution)/shard_map/all_to_all | solution.py:300
  110.4 1.5 %shard_map.114 = (f32[64,512]{1,0:T(8,128)S(1)}, f32[1,64,128]{2,1,0:T(8,128)S(1)}) custom-call(f32[64,512]{1,0:T(8,128)S(1)} %get-tuple-element.48.spread, f32[16,32,128]{2,1,0:T(8,128)S(1)} %all-to-all-done.5.got, f32[16,128]{1,0:T(8,128)S(1)} %get-tuple-element.45.coupling, f32[64,512]{1,0:T(8,128)S(1)} %get-tuple-element.38.retain, ...), custom_call_target="tpu_custom_call" | custom-call | flops 100000 | bytes 696384 | tf_op jit(solution)/shard_map/pallas_call | solution.py:23
  111.9 0.6 collective-permute-start.3
  112.5 3.4 %collective-permute-done.3.other_offset = f32[1,64,128]{2,1,0:T(8,128)S(1)} collective-permute-done((f32[1,64,128]{2,1,0:T(8,128)S(1)}, f32[1,64,128]{2,1,0:T(8,128)S(1)}, u32[]{:S(2)}, u32[]{:S(2)}) %collective-permute-start.3) | collective-permute-done | bytes 32800 | tf_op jit(solution)/shard_map/ppermute | solution.py:295
  115.9 2.9 %shard_map.115 = (f32[64,512]{1,0:T(8,128)S(1)}, f32[16,32,128]{2,1,0:T(8,128)}) custom-call(f32[64,512]{1,0:T(8,128)S(1)} %get-tuple-element.52.offset, f32[64,512]{1,0:T(8,128)S(1)} %get-tuple-element.32.factor, f32[1,64,128]{2,1,0:T(8,128)S(1)} %get-tuple-element.53.end_offset, f32[2,64,128]{2,1,0:T(8,128)S(1)} %get-tuple-element.33.end_offset.end_factor, ...), custom_call_target="tpu_custom_call" | custom-call | flops 100000 | bytes 854400 | tf_op jit(solution)/shard_map/pallas_call | solution.py:23
  118.8 1.6 %all-to-all-done.7.got = f32[16,32,128]{2,1,0:T(8,128)S(1)} async-done(((f32[16,32,128]{2,1,0:T(8,128)}), f32[16,32,128]{2,1,0:T(8,128)S(1)}, u32[]{:S(2)}, u32[]{:S(2)}) %all-to-all-start.7) | async-done | bytes 262176 | tf_op jit(solution)/shard_map/all_to_all | solution.py:300
  120.4 4.4 %all-to-all-start.8 = ((f32[16,32,128]{2,1,0:T(8,128)}), f32[16,32,128]{2,1,0:T(8,128)S(1)}, u32[]{:S(2)}, u32[]{:S(2)}) async-start(f32[16,32,128]{2,1,0:T(8,128)} %get-tuple-element.58), calls=%async_computation.8 | async-start | bytes 524288 | tf_op jit(solution)/shard_map/all_to_all | solution.py:300
  124.8 1.3 shard_map.117
  126.1 8.7 %all-to-all-done.8.arrived = f32[16,32,128]{2,1,0:T(8,128)S(1)} async-done(((f32[16,32,128]{2,1,0:T(8,128)}), f32[16,32,128]{2,1,0:T(8,128)S(1)}, u32[]{:S(2)}, u32[]{:S(2)}) %all-to-all-start.8) | async-done | bytes 262176 | tf_op jit(solution)/shard_map/all_to_all | solution.py:300
  134.9 3.1 %shard_map.118 = f32[16,2048]{1,0:T(8,128)} custom-call(s32[16,2,128]{2,1,0:T(2,128)S(1)} %all-to-all-done.cells, f32[16,32,128]{2,1,0:T(8,128)S(1)} %all-to-all-done.8.arrived, f32[16,32,128]{2,1,0:T(8,128)} %get-tuple-element.57.looked, f32[16,2,128]{2,1,0:T(2,128)S(1)} %get-tuple-element.43.rates, f32[16,2048]{1,0:T(8,128)S(1)} %get-tuple-element.59.grid), custom_call_target="tpu_custom_call" | custom-call | flops 100000 | bytes 819200 | tf_op jit(solution)/shard_map/pallas_call | solution.py:23
  (16 shorter events, 0.0 us)
Async XLA Ops:
  0.6 0.9 copy-start.2
  1.5 0.7 copy-start.4
  2.2 0.7 copy-start.8
  2.9 5.0 %copy-start.9 = (s32[1,4,4,1]{2,3,1,0:T(1,128)S(1)}, s32[1,4,4,1]{2,3,1,0:T(1,128)}, u32[]{:S(2)}) copy-start(s32[1,4,4,1]{2,3,1,0:T(1,128)} %param.16) | copy-start | bytes 196
  4.4 4.3 %copy-start.7 = (s32[4,512]{1,0:T(4,128)S(1)}, s32[4,512]{1,0:T(4,128)}, u32[]{:S(2)}) copy-start(s32[4,512]{1,0:T(4,128)} %cells.1) | copy-start | bytes 24580
  4.4 11.5 %collective-permute-start = (f32[2,64,128]{2,1,0:T(8,128)S(1)}, f32[2,64,128]{2,1,0:T(8,128)S(1)}, u32[]{:S(2)}, u32[]{:S(2)}) collective-permute-start(f32[2,64,128]{2,1,0:T(8,128)S(1)} %get-tuple-element.33.end_offset.end_factor), channel_id=1, source_target_pairs={{0,16},{16,0},{1,17},{17,1},{2,18},{18,2},{3,19},{19,3},{4,20},{20... | collective-permute-start | bytes 196616 | tf_op jit(solution)/shard_map/ppermute | solution.py:295
  9.9 6.0 %copy-start.1 = (f32[16,33]{1,0:T(8,128)S(1)}, f32[16,33]{1,0:T(8,128)}, u32[]{:S(2)}) copy-start(f32[16,33]{1,0:T(8,128)} %taps.7) | copy-start | bytes 6340
  9.9 12.4 %all-to-all-start = ((s32[16,2,128]{2,1,0:T(2,128)}), s32[16,2,128]{2,1,0:T(2,128)S(1)}, u32[]{:S(2)}, u32[]{:S(2)}) async-start(s32[16,2,128]{2,1,0:T(2,128)} %get-tuple-element.36), calls=%async_computation | async-start | bytes 32768 | tf_op jit(solution)/shard_map/all_to_all | solution.py:300
  15.9 0.7 copy-start.3
  22.3 3.7 %copy-start = (f32[16,2048]{1,0:T(8,128)S(1)}, f32[16,2048]{1,0:T(8,128)}, u32[]{:S(2)}) copy-start(f32[16,2048]{1,0:T(8,128)} %grid.3) | copy-start | bytes 393220
  22.3 3.7 %copy-start.6 = (f32[2048]{0:T(1024)S(1)}, f32[2048]{0:T(1024)}, u32[]{:S(2)}) copy-start(f32[2048]{0:T(1024)} %param.15) | copy-start | bytes 24580
  22.3 13.7 %all-to-all-start.2 = ((f32[16,32,128]{2,1,0:T(8,128)}), f32[16,32,128]{2,1,0:T(8,128)S(1)}, u32[]{:S(2)}, u32[]{:S(2)}) async-start(f32[16,32,128]{2,1,0:T(8,128)} %get-tuple-element.42), calls=%async_computation.2 | async-start | bytes 524288 | tf_op jit(solution)/shard_map/all_to_all | solution.py:300
  36.0 14.6 %all-to-all-start.1 = ((f32[16,40,128]{2,1,0:T(8,128)}), f32[16,40,128]{2,1,0:T(8,128)S(1)}, u32[]{:S(2)}, u32[]{:S(2)}) async-start(f32[16,40,128]{2,1,0:T(8,128)} %get-tuple-element.37.looked), calls=%async_computation.1 | async-start | bytes 655360 | tf_op jit(solution)/shard_map/all_to_all | solution.py:300
  50.6 3.7 %copy-start.5 = (f32[4,512]{1,0:T(4,128)S(1)}, f32[4,512]{1,0:T(4,128)}, u32[]{:S(2)}) copy-start(f32[4,512]{1,0:T(4,128)} %coupling.1) | copy-start | bytes 24580
  50.6 13.7 %all-to-all-start.3 = ((f32[16,32,128]{2,1,0:T(8,128)}), f32[16,32,128]{2,1,0:T(8,128)S(1)}, u32[]{:S(2)}, u32[]{:S(2)}) async-start(f32[16,32,128]{2,1,0:T(8,128)} %get-tuple-element.44.looked), calls=%async_computation.3 | async-start | bytes 524288 | tf_op jit(solution)/shard_map/all_to_all | solution.py:300
  55.8 4.0 %collective-permute-start.1 = (f32[1,64,128]{2,1,0:T(8,128)S(1)}, f32[1,64,128]{2,1,0:T(8,128)S(1)}, u32[]{:S(2)}, u32[]{:S(2)}) collective-permute-start(f32[1,64,128]{2,1,0:T(8,128)S(1)} %get-tuple-element.40.end_offset), channel_id=1, source_target_pairs={{0,16},{16,0},{1,17},{17,1},{2,18},{18,2},{3,19},{19,3},{4,20},{20... | collective-permute-start | bytes 98312 | tf_op jit(solution)/shard_map/ppermute | solution.py:295
  64.3 14.4 %all-to-all-start.4 = ((f32[16,32,128]{2,1,0:T(8,128)}), f32[16,32,128]{2,1,0:T(8,128)S(1)}, u32[]{:S(2)}, u32[]{:S(2)}) async-start(f32[16,32,128]{2,1,0:T(8,128)} %get-tuple-element.49), calls=%async_computation.4 | async-start | bytes 524288 | tf_op jit(solution)/shard_map/all_to_all | solution.py:300
  70.2 4.0 %collective-permute-start.2 = (f32[1,64,128]{2,1,0:T(8,128)S(1)}, f32[1,64,128]{2,1,0:T(8,128)S(1)}, u32[]{:S(2)}, u32[]{:S(2)}) collective-permute-start(f32[1,64,128]{2,1,0:T(8,128)S(1)} %get-tuple-element.47.end_offset), channel_id=1, source_target_pairs={{0,16},{16,0},{1,17},{17,1},{2,18},{18,2},{3,19},{19,3},{4,20},{20... | collective-permute-start | bytes 98312 | tf_op jit(solution)/shard_map/ppermute | solution.py:295
  78.8 14.4 %all-to-all-start.6 = ((f32[16,32,128]{2,1,0:T(8,128)}), f32[16,32,128]{2,1,0:T(8,128)S(1)}, u32[]{:S(2)}, u32[]{:S(2)}) async-start(f32[16,32,128]{2,1,0:T(8,128)} %get-tuple-element.55), calls=%async_computation.6 | async-start | bytes 524288 | tf_op jit(solution)/shard_map/all_to_all | solution.py:300
  93.2 13.7 %all-to-all-start.5 = ((f32[16,32,128]{2,1,0:T(8,128)}), f32[16,32,128]{2,1,0:T(8,128)S(1)}, u32[]{:S(2)}, u32[]{:S(2)}) async-start(f32[16,32,128]{2,1,0:T(8,128)} %get-tuple-element.51.looked), calls=%async_computation.5 | async-start | bytes 524288 | tf_op jit(solution)/shard_map/all_to_all | solution.py:300
  106.9 13.5 %all-to-all-start.7 = ((f32[16,32,128]{2,1,0:T(8,128)}), f32[16,32,128]{2,1,0:T(8,128)S(1)}, u32[]{:S(2)}, u32[]{:S(2)}) async-start(f32[16,32,128]{2,1,0:T(8,128)} %get-tuple-element.57.looked), calls=%async_computation.7 | async-start | bytes 524288 | tf_op jit(solution)/shard_map/all_to_all | solution.py:300
  111.9 4.0 %collective-permute-start.3 = (f32[1,64,128]{2,1,0:T(8,128)S(1)}, f32[1,64,128]{2,1,0:T(8,128)S(1)}, u32[]{:S(2)}, u32[]{:S(2)}) collective-permute-start(f32[1,64,128]{2,1,0:T(8,128)S(1)} %get-tuple-element.53.end_offset), channel_id=1, source_target_pairs={{0,16},{16,0},{1,17},{17,1},{2,18},{18,2},{3,19},{19,3},{4,20},{20... | collective-permute-start | bytes 98312 | tf_op jit(solution)/shard_map/ppermute | solution.py:295
  120.4 14.4 %all-to-all-start.8 = ((f32[16,32,128]{2,1,0:T(8,128)}), f32[16,32,128]{2,1,0:T(8,128)S(1)}, u32[]{:S(2)}, u32[]{:S(2)}) async-start(f32[16,32,128]{2,1,0:T(8,128)} %get-tuple-element.58), calls=%async_computation.8 | async-start | bytes 524288 | tf_op jit(solution)/shard_map/all_to_all | solution.py:300
where the time goes:
time: 139 us; the launch traced here: 138 us
  waiting for transfers between devices  51.7 us (37%)
  starting transfers between devices  41.9 us (30%)
  Pallas kernels  39.3 us (28%)
  local copies, waits for them, and re-layouts  3.54 us (3%)
    all_to_all x9, waiting for transfers between devices, exchange(): return lax.all_to_all(x, 'bundle', split_axis=0, concat_axis=0, tiled=True)  41.5 us
    pallas_call x15, Pallas kernels, call(): pl.pallas_call(kernel, out_shape=outs, in_specs=[s for _, s in ins], out_...  39.3 us
    all_to_all x9, starting transfers between devices, exchange(): return lax.all_to_all(x, 'bundle', split_axis=0, concat_axis=0, tiled=True)  37.1 us
    ppermute x4, waiting for transfers between devices, swap(): return lax.ppermute(x, 'seg', [(0, 1), (1, 0)])  10.2 us
    ppermute x4, starting transfers between devices, swap(): return lax.ppermute(x, 'seg', [(0, 1), (1, 0)])  4.75 us
    unnamed x21, local copies, waits for them, and re-layouts  3.45 us
  transfers between devices with their start and end apart: 13, of which 12 were waited for; matrix products, arithmetic and copies ran while one was open for 1% of the time, Pallas kernels for 25%

commit v1 on v0

v1 whole, which is shorter than its diff:
```python
import functools

import jax
import jax.numpy as jnp
from jax import lax
from jax.experimental import pallas as pl
from jax.experimental.pallas import tpu as pltpu
from jax.sharding import PartitionSpec as P

STEPS = 4
LANES = 128
HALF = 16
RADIX = 4
F32 = jnp.float32
BF16 = jnp.bfloat16

VMEM = pl.BlockSpec(memory_space=pltpu.VMEM)
SMEM = pl.BlockSpec(memory_space=pltpu.SMEM)
ANY = pl.BlockSpec(memory_space=pl.ANY)


def call(kernel, outs, ins, out_specs=None, scratch=(), flops=100_000, aliases=None):
    args = [a for a, _ in ins]
    size = sum(a.size * 4 for a in args) + sum(o.size * 4 for o in outs)
    return pl.pallas_call(
        kernel,
        out_shape=outs,
        in_specs=[s for _, s in ins],
        out_specs=out_specs or [VMEM] * len(outs),
        scratch_shapes=list(scratch),
        input_output_aliases=aliases or {},
        cost_estimate=pl.CostEstimate(flops=flops, bytes_accessed=size, transcendentals=0),
        compiler_params=pltpu.CompilerParams(vmem_limit_bytes=40 * 1024 * 1024),
    )(*args)


def sds(shape, dtype=F32):
    return jax.ShapeDtypeStruct(shape, dtype)


def route_kernel(groups, cap, owners, cells, slot, send, count):
    blocks = slot.shape[0]
    owners_total = send.shape[0]
    send[...] = jnp.full(send.shape, -1, jnp.int32)
    for o in range(owners_total):
        count[o] = 0
    for b in range(blocks):
        line, group = b // groups, b % groups
        owner = owners[0, line, 0, group]
        rank = count[owner]
        count[owner] = rank + 1
        slot[b] = owner * cap + rank
        send[owner, pl.ds(rank, 1), :] = cells[
            pl.ds(line, 1), group * LANES : (group + 1) * LANES
        ]


def where_slot(slot, b, cap):
    s = slot[b]
    return s // cap, s % cap


def last_lane(x):
    return jnp.broadcast_to(x[:, LANES - 1 : LANES], x.shape)


def column(ref_at, rows):
    row = lax.broadcasted_iota(jnp.int32, (rows, LANES), 0)
    out = jnp.zeros((rows, LANES), F32)
    for k in range(rows):
        out = jnp.where(row == k, ref_at(k), out)
    return out


def tile(ref, line, comps, group):
    return ref[pl.ds(line * comps, comps), group * LANES : (group + 1) * LANES]


def put(ref, line, comps, group, value):
    ref[pl.ds(line * comps, comps), group * LANES : (group + 1) * LANES] = value


def level_rows(levels, level, line, comps, group):
    return levels[level, pl.ds(line * comps, comps), group * LANES : (group + 1) * LANES]


LEVELS = 7


def scan_line(levels, retain, values, line, comps, groups):
    offsets = []
    for group in range(groups):
        offset = (1.0 - tile(retain, line, comps, group)) * values[group]
        for level in range(LEVELS):
            offset = offset + level_rows(levels, level, line, comps, group) * pltpu.roll(
                offset, 1 << level, 1
            )
        offsets.append(offset)
    carry = last_lane(offsets[0])
    done = [offsets[0]]
    for group in range(1, groups):
        done.append(offsets[group] + level_rows(levels, LEVELS, line, comps, group) * carry)
        if group < groups - 1:
            carry = (
                last_lane(offsets[group])
                + level_rows(levels, LEVELS + 1, line, comps, group) * carry
            )
    return done


def tap_columns(taps, comps):
    return [jnp.broadcast_to(taps[:, t : t + 1], (comps, LANES)) for t in range(taps.shape[1])]


def correlate(tiles, columns, lane):
    count = len(tiles)
    shifted = [tiles]
    for b in range(1, RADIX):
        row = []
        for j in range(count):
            x = tiles[j]
            y = jnp.where(lane < b, tiles[j + 1] if j + 1 < count else 0.0, x)
            row.append(pltpu.roll(y, LANES - b, 1))
        shifted.append(row)
    early = [None] + [
        jnp.where(lane >= LANES - b, pltpu.roll(tiles[0], LANES - b, 1), 0.0) for b in range(1, RADIX)
    ]

    def mix(a, values):
        total = None
        for b in range(RADIX):
            t = RADIX * a + b + HALF
            if t < len(columns) and values[b] is not None:
                term = columns[t] * values[b]
                total = term if total is None else total + term
        return total

    spans = range(-(HALF // RADIX), HALF // RADIX + 1)
    outs = [None] * count
    for a in spans:
        parts = [mix(a, [shifted[b][j] for b in range(RADIX)]) for j in range(count)]
        for j in range(count):
            if a == 0:
                y = parts[j]
            elif a > 0:
                after = parts[j + 1] if j + 1 < count else 0.0
                y = pltpu.roll(jnp.where(lane < RADIX * a, after, parts[j]), LANES - RADIX * a, 1)
            else:
                before = parts[j - 1] if j else mix(a, early)
                y = pltpu.roll(
                    jnp.where(lane >= LANES + RADIX * a, before, parts[j]), -RADIX * a, 1
                )
            outs[j] = y if outs[j] is None else outs[j] + y
    return outs


def correlate_ring(x, columns):
    shifted = [x] + [pltpu.roll(x, LANES - b, 1) for b in range(1, RADIX)]
    out = None
    for a in range(-(HALF // RADIX), HALF // RADIX + 1):
        total = None
        for b in range(RADIX):
            t = RADIX * a + b + HALF
            if t < len(columns):
                term = columns[t] * shifted[b]
                total = term if total is None else total + term
        if a:
            total = pltpu.roll(total, (-RADIX * a) % LANES, 1)
        out = total if out is None else out + total
    return out


def first_kernel(
    lines, comps, groups, conc, slowness, retard, order, retain, levels, offset, factor, ends
):
    lane = lax.broadcasted_iota(jnp.int32, (comps, LANES), 1)
    slow_by = column(lambda k: retard[k], comps)
    for line in range(lines):
        values, whole = [], []
        for group in range(groups):
            s = slowness[pl.ds(line, 1), group * LANES : (group + 1) * LANES]
            r = 1.0 / (1.0 + slow_by * s)
            put(retain, line, comps, group, r)
            rows = pl.ds(line * comps, comps)
            span = slice(group * LANES, (group + 1) * LANES)
            f = r
            for level in range(LEVELS):
                inside = lane >= (1 << level)
                levels[level, rows, span] = jnp.where(inside, f, 0.0)
                f = jnp.where(inside, f * pltpu.roll(f, 1 << level, 1), f)
            levels[LEVELS, rows, span] = f
            end = last_lane(f)
            levels[LEVELS + 1, rows, span] = end
            if group:
                f = f * carry
                carry = carry * end
            else:
                carry = end
            put(factor, line, comps, group, f)
            whole.append(f)
            values.append(conc[line, :, span])
        offsets = scan_line(levels, retain, values, line, comps, groups)
        for group in range(groups):
            put(offset, line, comps, group, offsets[group])
        ends[0, pl.ds(line * comps, comps), :] = jnp.where(lane < 64, offsets[0], offsets[-1])
        ends[1, pl.ds(line * comps, comps), :] = jnp.where(lane < 64, whole[0], whole[-1])


def taps_kernel(lines, comps, groups, sources, taps, *refs):
    lane = lax.broadcasted_iota(jnp.int32, (comps, LANES), 1)
    columns = tap_columns(taps, comps)
    for source, out in zip(refs[:sources], refs[sources:]):
        for line in range(lines):
            tiles = [tile(source, line, comps, group) for group in range(groups)]
            sums = correlate(tiles, columns, lane)
            for group in range(groups):
                put(out, line, comps, group, tiles[group] + sums[group])


def finish_kernel(
    lines, comps, groups, cap, segs, has_gather, aliased,
    local, carried, end_offset, end_factor, other_offset, other_factor, taps, inlet, slot, *rest,
):
    if aliased:
        rest = rest[1:]
    spread, send, done = rest
    me = lax.axis_index("seg")
    lane = lax.broadcasted_iota(jnp.int32, (comps, LANES), 1)
    columns = tap_columns(taps, comps)
    copies = []
    for line in range(lines):
        rows = pl.ds(line * comps, comps)

        def part(s):
            if has_gather:
                return other_offset[s, rows, :], other_factor[s, rows, :]
            mine = me == s
            return (
                jnp.where(mine, end_offset[0, rows, :], other_offset[0, rows, :]),
                jnp.where(mine, end_factor[1, rows, :], other_factor[1, rows, :]),
            )

        flow = column(lambda k: inlet[line, k], comps)
        zero = jnp.zeros((comps, LANES), F32)
        left, right, inflow = zero, zero, zero
        for s in range(segs):
            inflow = jnp.where(me == s, flow, inflow)
            off, fac = part(s)
            edge = off + fac * flow
            left = jnp.where(me == s + 1, edge, left)
            right = jnp.where(me == s - 1, edge, right)
            if s < segs - 1:
                flow = last_lane(edge)
        ring = jnp.where(lane >= LANES - HALF, left, 0.0)
        ring = jnp.where((lane >= 48) & (lane < 48 + HALF), pltpu.roll(right, 48, 1), ring)
        ring = correlate_ring(ring, columns)
        for group in range(groups):
            total = tile(local, line, comps, group) + tile(carried, line, comps, group) * inflow
            if group == 0:
                total = total + jnp.where(lane < HALF, ring, 0.0)
            if group == groups - 1:
                total = total + jnp.where(lane >= LANES - HALF, pltpu.roll(ring, 80, 1), 0.0)
            put(spread, line, comps, group, total)
            b = line * groups + group
            owner, rank = where_slot(slot, b, cap)
            copy = pltpu.make_async_copy(
                spread.at[pl.ds(line * comps, comps), group * LANES : (group + 1) * LANES],
                send.at[owner, pl.ds(pl.multiple_of((cap + rank) * comps, 8), comps), :],
                done.at[b],
            )
            copy.start()
            copies.append(copy)
    for copy in copies:
        copy.wait()


def conc_kernel(lines, comps, groups, cap, first, last, spread, got, coupling, retain, levels, slot, *outs):
    lane = lax.broadcasted_iota(jnp.int32, (comps, LANES), 1)
    outs = list(outs)
    coupling_out = outs.pop() if first else None
    for line in range(lines):
        values = []
        for group in range(groups):
            b = line * groups + group
            owner, rank = where_slot(slot, b, cap)
            looked = got[owner, pl.ds(pl.multiple_of(rank * comps, 8), comps), :]
            if first:
                rate = got[owner, pl.ds(2 * cap * comps + rank, 1), :]
                coupling_out[pl.ds(b, 1), :] = rate
            else:
                rate = coupling[pl.ds(b, 1), :]
            s = tile(spread, line, comps, group)
            value = s + rate * (looked - s)
            if last:
                outs[0][line, :, group * LANES : (group + 1) * LANES] = value
            values.append(value)
        if last:
            continue
        offsets = scan_line(levels, retain, values, line, comps, groups)
        for group in range(groups):
            put(outs[0], line, comps, group, offsets[group])
        outs[1][0, pl.ds(line * comps, comps), :] = jnp.where(lane < 64, offsets[0], offsets[-1])


def gather_cells(grid, cell, comps, high_total):
    low = jnp.broadcast_to(cell & (LANES - 1), (comps, LANES))
    high = jnp.broadcast_to(cell >> 7, (comps, LANES))
    out = jnp.zeros((comps, LANES), F32)
    for h in range(high_total):
        g = jnp.take_along_axis(
            grid[:, h * LANES : (h + 1) * LANES], low, axis=1, mode="promise_in_bounds"
        )
        out = jnp.where(high == h, g, out)
    return out


def look_first_kernel(cap, cells, grid, kappa, send_in, looked, rates, send, extra, done):
    comps = grid.shape[0]
    high_total = grid.shape[1] // LANES
    row = lax.broadcasted_iota(jnp.int32, (high_total, LANES), 0)

    def one(owner, carry):
        for rank in range(cap):
            cell = cells[owner, pl.ds(rank, 1), :]
            valid = cell >= 0
            cell = jnp.maximum(cell, 0)
            looked[owner, rank * comps : (rank + 1) * comps, :] = gather_cells(
                grid, cell, comps, high_total
            )
            low = jnp.broadcast_to(cell & (LANES - 1), (high_total, LANES))
            k = jnp.take_along_axis(kappa[...], low, axis=1, mode="promise_in_bounds")
            rate = jnp.sum(jnp.where(row == (cell >> 7), k, 0.0), axis=0, keepdims=True)
            rate = jnp.where(valid, rate, 0.0)
            rates[owner, pl.ds(rank, 1), :] = rate
            extra[owner, pl.ds(rank, 1), :] = rate
        return carry

    lax.fori_loop(0, cells.shape[0], one, 0, unroll=4)
    width = cap * comps
    copies = [
        pltpu.make_async_copy(looked, send.at[:, 0:width, :], done.at[0]),
        pltpu.make_async_copy(extra, send.at[:, 2 * width : 2 * width + extra.shape[1], :], done.at[1]),
    ]
    for copy in copies:
        copy.start()
    for copy in copies:
        copy.wait()


def onehot_kernel(cap, cells, onehot):
    wide = onehot.shape[1]
    row = lax.broadcasted_iota(jnp.int32, (wide, LANES), 0)

    def one(owner, carry):
        for rank in range(cap):
            cell = cells[owner, pl.ds(rank, 1), :]
            hit = jnp.where(row == (cell & (wide - 1)), 1.0, 0.0).astype(F32)
            at = pl.multiple_of((owner * cap + rank) * LANES, LANES)
            onehot[pl.ds(at, LANES), :] = hit.T.astype(BF16)
        return carry

    lax.fori_loop(0, cells.shape[0], one, 0)


def update_kernel(cap, chunk, last, cells, got, looked, rates, onehot, grid, *rest):
    if last:
        grid_out, masked = rest
    else:
        grid_out, looked_out, send, masked, done = rest
    comps = grid.shape[0]
    wide = onehot.shape[1]
    bits = wide.bit_length() - 1
    high_total = grid.shape[1] // wide
    owners_total = cells.shape[0]
    rows = high_total * comps
    width = chunk * cap * LANES
    total = None
    for start in range(0, owners_total, chunk):
        turn = (start // chunk) % masked.shape[0]
        for i in range(chunk):
            owner = start + i
            for rank in range(cap):
                at = (i * cap + rank) * LANES
                cell = cells[owner, rank : rank + 1, :]
                valid = jnp.broadcast_to(cell, (comps, LANES)) >= 0
                cell = jnp.maximum(cell, 0)
                rate = rates[owner, rank : rank + 1, :]
                span = slice(rank * comps, (rank + 1) * comps)
                came = slice((cap + rank) * comps, (cap + rank + 1) * comps)
                flux = jnp.where(valid, rate * (looked[owner, span, :] - got[owner, came, :]), 0.0)
                coarse = flux.astype(BF16)
                fine = (flux - coarse.astype(F32)).astype(BF16)
                high = jnp.broadcast_to((cell >> bits).astype(F32), (comps, LANES)).astype(BF16)
                for h in range(high_total):
                    hit = high == jnp.asarray(h, BF16)
                    masked[turn, h * comps : (h + 1) * comps, at : at + LANES] = jnp.where(
                        hit, coarse, jnp.zeros_like(coarse)
                    )
                    masked[turn, rows + h * comps : rows + (h + 1) * comps, at : at + LANES] = (
                        jnp.where(hit, fine, jnp.zeros_like(fine))
                    )
        first = start * cap * LANES
        part = jnp.dot(
            masked[turn], onehot[first : first + width, :], preferred_element_type=F32
        )
        total = part if total is None else total + part
    for h in range(high_total):
        span = slice(h * wide, (h + 1) * wide)
        at = slice(h * comps, (h + 1) * comps)
        at2 = slice(rows + h * comps, rows + (h + 1) * comps)
        grid_out[:, span] = grid[:, span] - 0.25 * (total[at, :] + total[at2, :])
    if last:
        return

    def one(owner, carry):
        for rank in range(cap):
            cell = jnp.maximum(cells[owner, pl.ds(rank, 1), :], 0)
            looked_out[owner, rank * comps : (rank + 1) * comps, :] = gather_cells(
                grid_out, cell, comps, grid.shape[1] // LANES
            )
        return carry

    lax.fori_loop(0, owners_total, one, 0, unroll=4)
    copy = pltpu.make_async_copy(looked_out, send.at[:, 0 : cap * comps, :], done.at[0])
    copy.start()
    copy.wait()


def swap(x, segs):
    if segs == 2:
        return lax.ppermute(x, "seg", [(0, 1), (1, 0)])
    return lax.all_gather(x, "seg")


def exchange(x):
    return lax.all_to_all(x, "bundle", split_axis=0, concat_axis=0, tiled=True)


def per_device(conc, slowness, retard, taps, inlet, grid, kappa, owners, cells):
    lines, comps, nodes = conc.shape
    groups = nodes // LANES
    blocks = lines * groups
    segs = lax.axis_size("seg")
    owners_total = lax.axis_size("bundle")
    cap = max(2, 2 * blocks // owners_total)
    rows = lines * comps
    cell_count = grid.shape[1]
    chunk = 4 if owners_total % 4 == 0 else owners_total
    half = cap * comps
    extra = 8 * (-(-cap // 8))

    slot, cell_send = call(
        functools.partial(route_kernel, groups, cap),
        [sds((blocks,), jnp.int32), sds((owners_total, cap, LANES), jnp.int32)],
        [(jnp.swapaxes(owners, 2, 3), SMEM), (cells, VMEM)],
        out_specs=[SMEM, VMEM],
        scratch=[pltpu.SMEM((owners_total,), jnp.int32)],
    )
    cell_recv = exchange(cell_send)

    retain, levels, offset, factor, ends = call(
        functools.partial(first_kernel, lines, comps, groups),
        [
            sds((rows, nodes)), sds((LEVELS + 2, rows, nodes)), sds((rows, nodes)),
            sds((rows, nodes)), sds((2, rows, LANES)),
        ],
        [(conc, VMEM), (slowness, VMEM), (retard, SMEM), (slot, SMEM)],
    )
    first_ends = ends
    other = swap(ends, segs)
    if segs == 2:
        other_offset = other_factor = other
    else:
        other_offset, other_factor = other[:, 0], other[:, 1]
    local, carried = call(
        functools.partial(taps_kernel, lines, comps, groups, 2),
        [sds((rows, nodes))] * 2,
        [(taps, VMEM), (offset, VMEM), (factor, VMEM)],
    )

    def finish(send, size):
        ins = [
            (local, VMEM), (carried, VMEM), (ends, VMEM), (first_ends, VMEM),
            (other_offset, VMEM), (other_factor, VMEM), (taps, VMEM), (inlet, SMEM), (slot, SMEM),
        ]
        aliases = {}
        if send is not None:
            aliases = {len(ins): 1}
            ins.append((send, ANY))
        return call(
            functools.partial(
                finish_kernel, lines, comps, groups, cap, segs, segs != 2, send is not None
            ),
            [sds((rows, nodes)), sds((owners_total, size, LANES))],
            ins,
            out_specs=[VMEM, ANY],
            scratch=[pltpu.SemaphoreType.DMA((blocks,))],
            aliases=aliases,
        )

    spread, send = finish(None, 2 * half + extra)
    looked, rates, send = call(
        functools.partial(look_first_kernel, cap),
        [
            sds((owners_total, half, LANES)), sds((owners_total, cap, LANES)),
            sds((owners_total, 2 * half + extra, LANES)),
        ],
        [
            (cell_recv, VMEM), (grid, VMEM),
            (kappa.reshape(cell_count // LANES, LANES), VMEM), (send, ANY),
        ],
        out_specs=[VMEM, VMEM, ANY],
        scratch=[pltpu.VMEM((owners_total, extra, LANES), F32), pltpu.SemaphoreType.DMA((2,))],
        aliases={3: 2},
    )
    wide = 256 if cell_count % 256 == 0 else LANES
    (onehot,) = call(
        functools.partial(onehot_kernel, cap),
        [sds((owners_total * cap * LANES, wide), BF16)],
        [(cell_recv, VMEM)],
    )
    coupling = slowness
    for step in range(STEPS):
        last = step == STEPS - 1
        got = exchange(send)
        outs = [sds(conc.shape)] if last else [sds((rows, nodes)), sds((1, rows, LANES))]
        if step == 0:
            outs.append(sds((blocks, LANES)))
        result = call(
            functools.partial(conc_kernel, lines, comps, groups, cap, step == 0, last),
            outs,
            [
                (spread, VMEM), (got, VMEM), (coupling, VMEM), (retain, VMEM), (levels, VMEM),
                (slot, SMEM),
            ],
        )
        if step == 0:
            coupling = result[-1]
        if last:
            conc_out = result[0]
        else:
            offset, ends = result[0], result[1]
            got_ends = swap(ends, segs)
            other_offset = got_ends if segs == 2 else got_ends[:, 0]
        outs, specs = [sds(grid.shape)], [VMEM]
        scratch = [pltpu.VMEM((min(4, owners_total // chunk), 2 * (cell_count // wide) * comps, chunk * cap * LANES), BF16)]
        if not last:
            outs += [sds((owners_total, half, LANES)), sds((owners_total, 2 * half, LANES))]
            specs += [VMEM, ANY]
            scratch.append(pltpu.SemaphoreType.DMA((1,)))
        result = call(
            functools.partial(update_kernel, cap, chunk, last),
            outs,
            [
                (cell_recv, VMEM), (got, VMEM), (looked, VMEM), (rates, VMEM), (onehot, VMEM),
                (grid, VMEM),
            ],
            out_specs=specs,
            scratch=scratch,
        )
        grid = result[0]
        if not last:
            looked, send = result[1], result[2]
            (local,) = call(
                functools.partial(taps_kernel, lines, comps, groups, 1),
                [sds((rows, nodes))],
                [(taps, VMEM), (offset, VMEM)],
            )
            spread, send = finish(send, 2 * half)
    return (conc_out, grid)


def solution(mesh):
    return jax.shard_map(
        per_device,
        mesh=mesh,
        in_specs=(
            P("bundle", None, "seg"),
            P("bundle", "seg"),
            P(),
            P(),
            P("bundle", None),
            P(None, ("seg", "bundle")),
            P(("seg", "bundle")),
            P("seg", "bundle", None, None),
            P("bundle", "seg"),
        ),
        out_specs=(P("bundle", None, "seg"), P(None, ("seg", "bundle"))),
        check_vma=False,
    )
```

time: 139 us -> 130 us (0.935)
  blocking collectives: 0 us -> 75.9 us
  waiting for transfers between devices: 51.7 us -> 1.2 us
  starting transfers between devices: 41.9 us -> 12 us
  Pallas kernels: 39.3 us -> 32.8 us
  local copies, waits for them, and re-layouts: 3.54 us -> 6.62 us
    all_to_all x0 -> x4, blocking collectives: none -> 75.9 us  [exchange(): return lax.all_to_all(x, 'bundle', split_axis=0, concat_axis=0, tiled=True)]
    all_to_all x9 -> x1, waiting for transfers between devices: 41.5 us -> 1.18 us  [exchange(): return lax.all_to_all(x, 'bundle', split_axis=0, concat_axis=0, tiled=True)]
    all_to_all x9 -> x1, starting transfers between devices: 37.1 us -> 5.91 us  [exchange(): return lax.all_to_all(x, 'bundle', split_axis=0, concat_axis=0, tiled=True)]
    ppermute x4, waiting for transfers between devices: 10.2 us -> 0.02 us  [swap(): return lax.ppermute(x, 'seg', [(0, 1), (1, 0)])]
    pallas_call x15 -> x20, Pallas kernels: 39.3 us -> 32.8 us  [call(): pl.pallas_call(kernel, out_shape=outs, in_specs=[s for _, s in ins], out_...]
    unnamed x21 -> x26, local copies, waits for them, and re-layouts: 3.45 us -> 6.62 us
  transfers between devices with their start and end apart: 13 -> 5, of which waited for: 12 -> 1; matrix products, arithmetic and copies ran while one was open for 1% -> 0% of each run, Pallas kernels for 25% -> 12%
where the time goes in v1:
time: 130 us; the launch traced here: 129 us
  blocking collectives  75.9 us (58%)
  Pallas kernels  32.8 us (25%)
  starting transfers between devices  12 us (9%)
  local copies, waits for them, and re-layouts  6.62 us (5%)
    all_to_all x4, blocking collectives, exchange(): return lax.all_to_all(x, 'bundle', split_axis=0, concat_axis=0, tiled=True)  75.9 us
    pallas_call x20, Pallas kernels, call(): pl.pallas_call(kernel, out_shape=outs, in_specs=[s for _, s in ins], out_...  32.8 us
    unnamed x26, local copies, waits for them, and re-layouts  6.62 us
    ppermute x4, starting transfers between devices, swap(): return lax.ppermute(x, 'seg', [(0, 1), (1, 0)])  6.05 us
    all_to_all x1, starting transfers between devices, exchange(): return lax.all_to_all(x, 'bundle', split_axis=0, concat_axis=0, tiled=True)  5.91 us
  transfers between devices with their start and end apart: 5, of which 1 were waited for; matrix products, arithmetic and copies ran while one was open for 0% of the time, Pallas kernels for 12%

profile of v1, /device:TPU:0, one launch (start us, length us, event | category | flops | bytes accessed | tf_op | source)
XLA Modules:
  0.0 129.4 jit_solution(7513507176913555629)
XLA Ops:
  0.6 0.0 copy-start.8
  0.7 0.7 copy-done.10
  1.3 0.7 copy-done.11
  2.0 1.3 shard_map.104
  3.3 0.0 copy-start.4
  3.3 0.9 copy-done.4
  4.2 0.7 copy-done.7
  4.9 0.7 copy-done.12
  5.6 1.4 %shard_map.105 = (f32[64,512]{1,0:T(8,128)S(1)}, f32[9,64,512]{2,1,0:T(8,128)S(1)}, f32[64,512]{1,0:T(8,128)S(1)}, f32[64,512]{1,0:T(8,128)S(1)}, f32[2,64,128]{2,1,0:T(8,128)S(1)}) custom-call(f32[4,16,512]{2,1,0:T(8,128)S(1)} %copy-done.4, f32[4,512]{1,0:T(4,128)S(1)} %copy-done.7, f32[16]{0:T(128)S(1)} %copy-done.12, s32[16]{0:T(128)S(1)} %get-tuple-element.38.order.slot), custom_call_target="tpu_custom_call" | custom-call | flops 100000 | bytes 1777792 | tf_op jit(solution)/shard_map/pallas_call | solution.py:25
  6.9 3.0 %collective-permute-start = (f32[2,64,128]{2,1,0:T(8,128)S(1)}, f32[2,64,128]{2,1,0:T(8,128)S(1)}, u32[]{:S(2)}, u32[]{:S(2)}) collective-permute-start(f32[2,64,128]{2,1,0:T(8,128)S(1)} %get-tuple-element.43.end_offset.end_factor), channel_id=1, source_target_pairs={{0,16},{16,0},{1,17},{17,1},{2,18},{18,2},{3,19},{19,3},{4,20},{20... | collective-permute-start | bytes 196616 | tf_op jit(solution)/shard_map/ppermute | solution.py:431
  10.0 5.9 %all-to-all-start = ((s32[16,2,128]{2,1,0:T(2,128)}), s32[16,2,128]{2,1,0:T(2,128)S(1)}, u32[]{:S(2)}, u32[]{:S(2)}) async-start(s32[16,2,128]{2,1,0:T(2,128)} %get-tuple-element.45), calls=%async_computation | async-start | bytes 32768 | tf_op jit(solution)/shard_map/all_to_all | solution.py:436
  15.9 0.0 copy-start
  15.9 0.7 copy-done
  16.6 1.5 %shard_map.106 = (f32[64,512]{1,0:T(8,128)S(1)}, f32[64,512]{1,0:T(8,128)S(1)}) custom-call(f32[16,33]{1,0:T(8,128)S(1)} %copy-done, f32[64,512]{1,0:T(8,128)S(1)} %get-tuple-element.39.refs_0_, f32[64,512]{1,0:T(8,128)S(1)} %get-tuple-element.40.refs_1_), custom_call_target="tpu_custom_call" | custom-call | flops 100000 | bytes 526400 | tf_op jit(solution)/shard_map/pallas_call | solution.py:25
  18.1 0.0 collective-permute-done.other_offset.other_factor
  18.1 0.0 copy-start.5
  18.1 0.7 copy-done.5
  18.8 2.4 %shard_map.107 = (f32[64,512]{1,0:T(8,128)S(1)}, f32[16,72,128]{2,1,0:T(8,128)S(1)}) custom-call(f32[64,512]{1,0:T(8,128)S(1)} %get-tuple-element.41.local, f32[64,512]{1,0:T(8,128)S(1)} %get-tuple-element.42.carried, f32[2,64,128]{2,1,0:T(8,128)S(1)} %get-tuple-element.43.end_offset.end_factor, f32[2,64,128]{2,1,0:T(8,128)S(1)} %get-tuple-element.43.end_offset.end_factor, ...), custom_call_target="tpu_custom_call" | custom-call | flops 100000 | bytes 1247616 | tf_op jit(solution)/shard_map/pallas_call | solution.py:25
  21.2 1.2 all-to-all-done.cells
  22.4 0.9 copy-done.2
  23.3 0.7 copy-done.9
  24.0 1.6 %shard_map.108 = (f32[16,32,128]{2,1,0:T(8,128)S(1)}, f32[16,2,128]{2,1,0:T(2,128)S(1)}, f32[16,72,128]{2,1,0:T(8,128)S(1)}) custom-call(s32[16,2,128]{2,1,0:T(2,128)S(1)} %all-to-all-done.cells, f32[16,2048]{1,0:T(8,128)S(1)} %copy-done.2, f32[16,128]{1,0:T(8,128)S(1)} %bitcast.4, ...), custom_call_target="tpu_custom_call", output_to_operand_aliasing={{2}: (3, {})} | custom-call | flops 100000 | bytes 1613824 | tf_op jit(solution)/shard_map/pallas_call | solution.py:25
  25.6 21.9 %all_to_all.25.got = f32[16,72,128]{2,1,0:T(8,128)S(1)} all-to-all(f32[16,72,128]{2,1,0:T(8,128)S(1)} %get-tuple-element.47), channel_id=1, replica_groups=mesh['seg'=2,'bundle'=16] {'bundle'}, dimensions={0} | all-to-all | bytes 1179648 | tf_op jit(solution)/shard_map/all_to_all | solution.py:436
  47.5 1.2 shard_map.109
  48.7 0.6 collective-permute-start.1
  49.3 1.8 %shard_map.111.onehot = bf16[4096,256]{1,0:T(8,128)(2,1)S(1)} custom-call(s32[16,2,128]{2,1,0:T(2,128)S(1)} %all-to-all-done.cells), custom_call_target="tpu_custom_call" | custom-call | flops 100000 | bytes 4210688 | tf_op jit(solution)/shard_map/pallas_call | solution.py:25
  51.1 0.0 copy-start.6
  51.1 0.8 shard_map.110.local
  52.0 2.3 %shard_map.112 = (f32[16,2048]{1,0:T(8,128)S(1)}, f32[16,32,128]{2,1,0:T(8,128)S(1)}, f32[16,64,128]{2,1,0:T(8,128)S(1)}) custom-call(s32[16,2,128]{2,1,0:T(2,128)S(1)} %all-to-all-done.cells, f32[16,72,128]{2,1,0:T(8,128)S(1)} %all_to_all.25.got, f32[16,32,128]{2,1,0:T(8,128)S(1)} %get-tuple-element.52.looked, f32[16,2,128]{2,1,0:T(2,128)S(1)} %get-tuple-element.53.rates, ...), custom_call_target="tpu_custom_call" | custom-call | flops 100000 | bytes 6127616 | tf_op jit(solution)/shard_map/pallas_call | solution.py:25
  54.3 0.0 collective-permute-done.1.other_offset
  54.3 2.4 %shard_map.113 = (f32[64,512]{1,0:T(8,128)S(1)}, f32[16,64,128]{2,1,0:T(8,128)S(1)}) custom-call(f32[64,512]{1,0:T(8,128)S(1)} %shard_map.110.local, f32[64,512]{1,0:T(8,128)S(1)} %get-tuple-element.42.carried, f32[1,64,128]{2,1,0:T(8,128)S(1)} %get-tuple-element.51.end_offset, ...), custom_call_target="tpu_custom_call", output_to_operand_aliasing={{1}: (9, {})} | custom-call | flops 100000 | bytes 1640832 | tf_op jit(solution)/shard_map/pallas_call | solution.py:25
  56.7 17.3 %all_to_all.26.got = f32[16,64,128]{2,1,0:T(8,128)S(1)} all-to-all(f32[16,64,128]{2,1,0:T(8,128)S(1)} %get-tuple-element.56), channel_id=1, replica_groups=mesh['seg'=2,'bundle'=16] {'bundle'}, dimensions={0} | all-to-all | bytes 1048576 | tf_op jit(solution)/shard_map/all_to_all | solution.py:436
  73.9 1.2 shard_map.114
  75.2 1.6 %collective-permute-start.2 = (f32[1,64,128]{2,1,0:T(8,128)S(1)}, f32[1,64,128]{2,1,0:T(8,128)S(1)}, u32[]{:S(2)}, u32[]{:S(2)}) collective-permute-start(f32[1,64,128]{2,1,0:T(8,128)S(1)} %get-tuple-element.59.end_offset), channel_id=1, source_target_pairs={{0,16},{16,0},{1,17},{17,1},{2,18},{18,2},{3,19},{19,3},{4,20},{20... | collective-permute-start | bytes 98312 | tf_op jit(solution)/shard_map/ppermute | solution.py:431
  76.8 0.8 shard_map.115.local
  77.6 2.3 %shard_map.116 = (f32[16,2048]{1,0:T(8,128)S(1)}, f32[16,32,128]{2,1,0:T(8,128)S(1)}, f32[16,64,128]{2,1,0:T(8,128)S(1)}) custom-call(s32[16,2,128]{2,1,0:T(2,128)S(1)} %all-to-all-done.cells, f32[16,64,128]{2,1,0:T(8,128)S(1)} %all_to_all.26.got, f32[16,32,128]{2,1,0:T(8,128)S(1)} %get-tuple-element.60.looked, f32[16,2,128]{2,1,0:T(2,128)S(1)} %get-tuple-element.53.rates, ...), custom_call_target="tpu_custom_call" | custom-call | flops 100000 | bytes 6062080 | tf_op jit(solution)/shard_map/pallas_call | solution.py:25
  79.9 0.0 collective-permute-done.2.other_offset
  79.9 2.4 %shard_map.117 = (f32[64,512]{1,0:T(8,128)S(1)}, f32[16,64,128]{2,1,0:T(8,128)S(1)}) custom-call(f32[64,512]{1,0:T(8,128)S(1)} %shard_map.115.local, f32[64,512]{1,0:T(8,128)S(1)} %get-tuple-element.42.carried, f32[1,64,128]{2,1,0:T(8,128)S(1)} %get-tuple-element.59.end_offset, ...), custom_call_target="tpu_custom_call", output_to_operand_aliasing={{1}: (9, {})} | custom-call | flops 100000 | bytes 1640832 | tf_op jit(solution)/shard_map/pallas_call | solution.py:25
  82.3 18.4 %all_to_all.27.got = f32[16,64,128]{2,1,0:T(8,128)S(1)} all-to-all(f32[16,64,128]{2,1,0:T(8,128)S(1)} %get-tuple-element.64), channel_id=1, replica_groups=mesh['seg'=2,'bundle'=16] {'bundle'}, dimensions={0} | all-to-all | bytes 1048576 | tf_op jit(solution)/shard_map/all_to_all | solution.py:436
  100.7 1.2 shard_map.118
  101.9 0.9 collective-permute-start.3
  102.8 0.8 shard_map.119.local
  103.6 2.3 %shard_map.120 = (f32[16,2048]{1,0:T(8,128)S(1)}, f32[16,32,128]{2,1,0:T(8,128)S(1)}, f32[16,64,128]{2,1,0:T(8,128)S(1)}) custom-call(s32[16,2,128]{2,1,0:T(2,128)S(1)} %all-to-all-done.cells, f32[16,64,128]{2,1,0:T(8,128)S(1)} %all_to_all.27.got, f32[16,32,128]{2,1,0:T(8,128)S(1)} %get-tuple-element.67.looked, f32[16,2,128]{2,1,0:T(2,128)S(1)} %get-tuple-element.53.rates, ...), custom_call_target="tpu_custom_call" | custom-call | flops 100000 | bytes 6062080 | tf_op jit(solution)/shard_map/pallas_call | solution.py:25
  105.9 0.0 collective-permute-done.3.other_offset
  105.9 2.4 %shard_map.121 = (f32[64,512]{1,0:T(8,128)S(1)}, f32[16,64,128]{2,1,0:T(8,128)S(1)}) custom-call(f32[64,512]{1,0:T(8,128)S(1)} %shard_map.119.local, f32[64,512]{1,0:T(8,128)S(1)} %get-tuple-element.42.carried, f32[1,64,128]{2,1,0:T(8,128)S(1)} %get-tuple-element.66.end_offset, ...), custom_call_target="tpu_custom_call", output_to_operand_aliasing={{1}: (9, {})} | custom-call | flops 100000 | bytes 1640832 | tf_op jit(solution)/shard_map/pallas_call | solution.py:25
  108.3 18.4 %all_to_all.28.got = f32[16,64,128]{2,1,0:T(8,128)S(1)} all-to-all(f32[16,64,128]{2,1,0:T(8,128)S(1)} %get-tuple-element.71), channel_id=1, replica_groups=mesh['seg'=2,'bundle'=16] {'bundle'}, dimensions={0} | all-to-all | bytes 1048576 | tf_op jit(solution)/shard_map/all_to_all | solution.py:436
  126.7 1.3 %shard_map.122 = f32[4,16,512]{2,1,0:T(8,128)} custom-call(f32[64,512]{1,0:T(8,128)S(1)} %get-tuple-element.70.spread, f32[16,64,128]{2,1,0:T(8,128)S(1)} %all_to_all.28.got, f32[16,128]{1,0:T(8,128)S(1)} %get-tuple-element.57.coupling, f32[64,512]{1,0:T(8,128)S(1)} %get-tuple-element.48.retain, f32[9,64,512]{2,1,0:T(8,128)S(1)} %get-tuple-element.49.levels, ...), custom_call_target="tpu_custom_call" | custom-call | flops 100000 | bytes 2105408 | tf_op jit(solution)/shard_map/pallas_call | solution.py:25
  128.0 1.4 %shard_map.123 = f32[16,2048]{1,0:T(8,128)} custom-call(s32[16,2,128]{2,1,0:T(2,128)S(1)} %all-to-all-done.cells, f32[16,64,128]{2,1,0:T(8,128)S(1)} %all_to_all.28.got, f32[16,32,128]{2,1,0:T(8,128)S(1)} %get-tuple-element.72.looked, f32[16,2,128]{2,1,0:T(2,128)S(1)} %get-tuple-element.53.rates, bf16[4096,256]{1,0:T(8,128)(2,1)S(1)} %shard_map.111.onehot, ...), custom_call_target="tpu_custom_call" | custom-call | flops 100000 | bytes 5275648 | tf_op jit(solution)/shard_map/pallas_call | solution.py:25
  (12 shorter events, 0.0 us)
Async XLA Ops:
  0.6 46.9 %copy-start.8 = (f32[4,512]{1,0:T(4,128)S(1)}, f32[4,512]{1,0:T(4,128)}, u32[]{:S(2)}) copy-start(f32[4,512]{1,0:T(4,128)} %coupling.1) | copy-start | bytes 24580
  0.6 0.7 copy-start.10
  1.3 0.7 copy-start.11
  3.3 0.9 copy-start.4
  4.2 0.7 copy-start.7
  4.9 0.7 copy-start.12
  6.9 11.2 %collective-permute-start = (f32[2,64,128]{2,1,0:T(8,128)S(1)}, f32[2,64,128]{2,1,0:T(8,128)S(1)}, u32[]{:S(2)}, u32[]{:S(2)}) collective-permute-start(f32[2,64,128]{2,1,0:T(8,128)S(1)} %get-tuple-element.43.end_offset.end_factor), channel_id=1, source_target_pairs={{0,16},{16,0},{1,17},{17,1},{2,18},{18,2},{3,19},{19,3},{4,20},{20... | collective-permute-start | bytes 196616 | tf_op jit(solution)/shard_map/ppermute | solution.py:431
  10.0 12.4 %all-to-all-start = ((s32[16,2,128]{2,1,0:T(2,128)}), s32[16,2,128]{2,1,0:T(2,128)S(1)}, u32[]{:S(2)}, u32[]{:S(2)}) async-start(s32[16,2,128]{2,1,0:T(2,128)} %get-tuple-element.45), calls=%async_computation | async-start | bytes 32768 | tf_op jit(solution)/shard_map/all_to_all | solution.py:436
  15.9 0.7 copy-start
  18.1 0.7 copy-start.5
  22.4 0.9 copy-start.2
  23.3 0.7 copy-start.9
  47.5 3.6 %copy-start.1 = (f32[16,33]{1,0:T(8,128)S(1)}, f32[16,33]{1,0:T(8,128)}, u32[]{:S(2)}) copy-start(f32[16,33]{1,0:T(8,128)} %taps.15) | copy-start | bytes 6340
  47.5 4.5 %copy-start.3 = (f32[16,2048]{1,0:T(8,128)S(1)}, f32[16,2048]{1,0:T(8,128)}, u32[]{:S(2)}) copy-start(f32[16,2048]{1,0:T(8,128)} %grid.3) | copy-start | bytes 393220
  48.7 5.5 %collective-permute-start.1 = (f32[1,64,128]{2,1,0:T(8,128)S(1)}, f32[1,64,128]{2,1,0:T(8,128)S(1)}, u32[]{:S(2)}, u32[]{:S(2)}) collective-permute-start(f32[1,64,128]{2,1,0:T(8,128)S(1)} %get-tuple-element.51.end_offset), channel_id=1, source_target_pairs={{0,16},{16,0},{1,17},{17,1},{2,18},{18,2},{3,19},{19,3},{4,20},{20... | collective-permute-start | bytes 98312 | tf_op jit(solution)/shard_map/ppermute | solution.py:431
  51.1 3.2 %copy-start.6 = (f32[4,16]{1,0:T(4,128)S(1)}, f32[4,16]{1,0:T(4,128)}, u32[]{:S(2)}) copy-start(f32[4,16]{1,0:T(4,128)} %inlet.7) | copy-start | bytes 772
  75.2 4.7 %collective-permute-start.2 = (f32[1,64,128]{2,1,0:T(8,128)S(1)}, f32[1,64,128]{2,1,0:T(8,128)S(1)}, u32[]{:S(2)}, u32[]{:S(2)}) collective-permute-start(f32[1,64,128]{2,1,0:T(8,128)S(1)} %get-tuple-element.59.end_offset), channel_id=1, source_target_pairs={{0,16},{16,0},{1,17},{17,1},{2,18},{18,2},{3,19},{19,3},{4,20},{20... | collective-permute-start | bytes 98312 | tf_op jit(solution)/shard_map/ppermute | solution.py:431
  101.9 4.0 %collective-permute-start.3 = (f32[1,64,128]{2,1,0:T(8,128)S(1)}, f32[1,64,128]{2,1,0:T(8,128)S(1)}, u32[]{:S(2)}, u32[]{:S(2)}) collective-permute-start(f32[1,64,128]{2,1,0:T(8,128)S(1)} %get-tuple-element.66.end_offset), channel_id=1, source_target_pairs={{0,16},{16,0},{1,17},{17,1},{2,18},{18,2},{3,19},{19,3},{4,20},{20... | collective-permute-start | bytes 98312 | tf_op jit(solution)/shard_map/ppermute | solution.py:431

commit v2 on v1

--- a/solution.py
+++ b/solution.py
@@ -19,17 +19,15 @@
 ANY = pl.BlockSpec(memory_space=pl.ANY)
 
 
-def call(kernel, outs, ins, out_specs=None, scratch=(), flops=100_000, aliases=None):
+def call(kernel, outs, ins, out_specs=None, scratch=()):
     args = [a for a, _ in ins]
-    size = sum(a.size * 4 for a in args) + sum(o.size * 4 for o in outs)
     return pl.pallas_call(
         kernel,
         out_shape=outs,
         in_specs=[s for _, s in ins],
         out_specs=out_specs or [VMEM] * len(outs),
         scratch_shapes=list(scratch),
-        input_output_aliases=aliases or {},
-        cost_estimate=pl.CostEstimate(flops=flops, bytes_accessed=size, transcendentals=0),
+        cost_estimate=pl.CostEstimate(flops=1, bytes_accessed=1, transcendentals=0),
         compiler_params=pltpu.CompilerParams(vmem_limit_bytes=40 * 1024 * 1024),
     )(*args)
 
@@ -64,12 +62,11 @@
     return jnp.broadcast_to(x[:, LANES - 1 : LANES], x.shape)
 
 
-def column(ref_at, rows):
-    row = lax.broadcasted_iota(jnp.int32, (rows, LANES), 0)
-    out = jnp.zeros((rows, LANES), F32)
-    for k in range(rows):
-        out = jnp.where(row == k, ref_at(k), out)
-    return out
+def column(row, rows):
+    square = (rows, rows)
+    here = lax.broadcasted_iota(jnp.int32, square, 0) == lax.broadcasted_iota(jnp.int32, square, 1)
+    values = jnp.sum(jnp.where(here, jnp.broadcast_to(row, square), 0.0), axis=1, keepdims=True)
+    return jnp.broadcast_to(values, (rows, LANES))
 
 
 def tile(ref, line, comps, group):
@@ -108,8 +105,8 @@
     return done
 
 
-def tap_columns(taps, comps):
-    return [jnp.broadcast_to(taps[:, t : t + 1], (comps, LANES)) for t in range(taps.shape[1])]
+def tap_columns(wide_taps):
+    return [wide_taps[t] for t in range(wide_taps.shape[0])]
 
 
 def correlate(tiles, columns, lane):
@@ -171,10 +168,15 @@
 
 
 def first_kernel(
-    lines, comps, groups, conc, slowness, retard, order, retain, levels, offset, factor, ends
+    lines, comps, groups, conc, slowness, retard, taps, inlet, order,
+    retain, levels, offset, factor, ends, wide_taps, wide_inlet,
 ):
     lane = lax.broadcasted_iota(jnp.int32, (comps, LANES), 1)
-    slow_by = column(lambda k: retard[k], comps)
+    slow_by = column(retard[...], comps)
+    for t in range(taps.shape[1]):
+        wide_taps[t] = jnp.broadcast_to(taps[:, t : t + 1], (comps, LANES))
+    for line in range(lines):
+        wide_inlet[pl.ds(line * comps, comps), :] = column(inlet[line : line + 1, :], comps)
     for line in range(lines):
         values, whole = [], []
         for group in range(groups):
@@ -208,7 +210,7 @@
 
 def taps_kernel(lines, comps, groups, sources, taps, *refs):
     lane = lax.broadcasted_iota(jnp.int32, (comps, LANES), 1)
-    columns = tap_columns(taps, comps)
+    columns = tap_columns(taps)
     for source, out in zip(refs[:sources], refs[sources:]):
         for line in range(lines):
             tiles = [tile(source, line, comps, group) for group in range(groups)]
@@ -217,17 +219,24 @@
                 put(out, line, comps, group, tiles[group] + sums[group])
 
 
+def place(send, slot, b, cap, comps, value):
+    owner, rank = where_slot(slot, b, cap)
+    send[owner, pl.ds(pl.multiple_of((cap + rank) * comps, 8), comps), :] = value
+
+
 def finish_kernel(
-    lines, comps, groups, cap, segs, has_gather, aliased,
-    local, carried, end_offset, end_factor, other_offset, other_factor, taps, inlet, slot, *rest,
+    lines, comps, groups, cap, segs, has_gather, first,
+    local, carried, end_offset, end_factor, other_offset, other_factor, taps, inlet, *rest,
 ):
-    if aliased:
-        rest = rest[1:]
-    spread, send, done = rest
+    if first:
+        (spread,) = rest
+    else:
+        slot_in, looked, spread, send, slot, done = rest
+        copy = pltpu.make_async_copy(slot_in, slot, done)
+        copy.start()
     me = lax.axis_index("seg")
     lane = lax.broadcasted_iota(jnp.int32, (comps, LANES), 1)
-    columns = tap_columns(taps, comps)
-    copies = []
+    columns = tap_columns(taps)
     for line in range(lines):
         rows = pl.ds(line * comps, comps)
 
@@ -240,7 +249,7 @@
                 jnp.where(mine, end_factor[1, rows, :], other_factor[1, rows, :]),
             )
 
-        flow = column(lambda k: inlet[line, k], comps)
+        flow = inlet[rows, :]
         zero = jnp.zeros((comps, LANES), F32)
         left, right, inflow = zero, zero, zero
         for s in range(segs):
@@ -261,17 +270,12 @@
             if group == groups - 1:
                 total = total + jnp.where(lane >= LANES - HALF, pltpu.roll(ring, 80, 1), 0.0)
             put(spread, line, comps, group, total)
-            b = line * groups + group
-            owner, rank = where_slot(slot, b, cap)
-            copy = pltpu.make_async_copy(
-                spread.at[pl.ds(line * comps, comps), group * LANES : (group + 1) * LANES],
-                send.at[owner, pl.ds(pl.multiple_of((cap + rank) * comps, 8), comps), :],
-                done.at[b],
-            )
-            copy.start()
-            copies.append(copy)
-    for copy in copies:
-        copy.wait()
+    if first:
+        return
+    send[:, 0 : cap * comps, :] = looked[...]
+    copy.wait()
+    for b in range(lines * groups):
+        place(send, slot, b, cap, comps, tile(spread, b // groups, comps, b % groups))
 
 
 def conc_kernel(lines, comps, groups, cap, first, last, spread, got, coupling, retain, levels, slot, *outs):
@@ -314,7 +318,7 @@
     return out
 
 
-def look_first_kernel(cap, cells, grid, kappa, send_in, looked, rates, send, extra, done):
+def look_first_kernel(groups, cap, cells, grid, kappa, spread, slot, rates, send):
     comps = grid.shape[0]
     high_total = grid.shape[1] // LANES
     row = lax.broadcasted_iota(jnp.int32, (high_total, LANES), 0)
@@ -324,7 +328,7 @@
             cell = cells[owner, pl.ds(rank, 1), :]
             valid = cell >= 0
             cell = jnp.maximum(cell, 0)
-            looked[owner, rank * comps : (rank + 1) * comps, :] = gather_cells(
+            send[owner, rank * comps : (rank + 1) * comps, :] = gather_cells(
                 grid, cell, comps, high_total
             )
             low = jnp.broadcast_to(cell & (LANES - 1), (high_total, LANES))
@@ -332,19 +336,12 @@
             rate = jnp.sum(jnp.where(row == (cell >> 7), k, 0.0), axis=0, keepdims=True)
             rate = jnp.where(valid, rate, 0.0)
             rates[owner, pl.ds(rank, 1), :] = rate
-            extra[owner, pl.ds(rank, 1), :] = rate
+            send[owner, pl.ds(2 * cap * comps + rank, 1), :] = rate
         return carry
 
     lax.fori_loop(0, cells.shape[0], one, 0, unroll=4)
-    width = cap * comps
-    copies = [
-        pltpu.make_async_copy(looked, send.at[:, 0:width, :], done.at[0]),
-        pltpu.make_async_copy(extra, send.at[:, 2 * width : 2 * width + extra.shape[1], :], done.at[1]),
-    ]
-    for copy in copies:
-        copy.start()
-    for copy in copies:
-        copy.wait()
+    for b in range(slot.shape[0]):
+        place(send, slot, b, cap, comps, tile(spread, b // groups, comps, b % groups))
 
 
 def onehot_kernel(cap, cells, onehot):
@@ -366,7 +363,7 @@
     if last:
         grid_out, masked = rest
     else:
-        grid_out, looked_out, send, masked, done = rest
+        grid_out, looked_out, masked = rest
     comps = grid.shape[0]
     wide = onehot.shape[1]
     bits = wide.bit_length() - 1
@@ -421,9 +418,6 @@
         return carry
 
     lax.fori_loop(0, owners_total, one, 0, unroll=4)
-    copy = pltpu.make_async_copy(looked_out, send.at[:, 0 : cap * comps, :], done.at[0])
-    copy.start()
-    copy.wait()
 
 
 def swap(x, segs):
@@ -451,20 +445,24 @@
 
     slot, cell_send = call(
         functools.partial(route_kernel, groups, cap),
-        [sds((blocks,), jnp.int32), sds((owners_total, cap, LANES), jnp.int32)],
+        [sds((blocks,), jnp.int32), sds((owners_total, 8 * (-(-cap // 8)), LANES), jnp.int32)],
         [(jnp.swapaxes(owners, 2, 3), SMEM), (cells, VMEM)],
         out_specs=[SMEM, VMEM],
         scratch=[pltpu.SMEM((owners_total,), jnp.int32)],
     )
     cell_recv = exchange(cell_send)
 
-    retain, levels, offset, factor, ends = call(
+    retain, levels, offset, factor, ends, taps, inlet = call(
         functools.partial(first_kernel, lines, comps, groups),
         [
             sds((rows, nodes)), sds((LEVELS + 2, rows, nodes)), sds((rows, nodes)),
-            sds((rows, nodes)), sds((2, rows, LANES)),
+            sds((rows, nodes)), sds((2, rows, LANES)), sds((taps.shape[1], comps, LANES)),
+            sds((rows, LANES)),
         ],
-        [(conc, VMEM), (slowness, VMEM), (retard, SMEM), (slot, SMEM)],
+        [
+            (conc, VMEM), (slowness, VMEM), (retard.reshape(1, comps), VMEM), (taps, VMEM),
+            (inlet, VMEM), (slot, ANY),
+        ],
     )
     first_ends = ends
     other = swap(ends, segs)
@@ -478,41 +476,34 @@
         [(taps, VMEM), (offset, VMEM), (factor, VMEM)],
     )
 
-    def finish(send, size):
+    def finish(looked):
+        first = looked is None
         ins = [
             (local, VMEM), (carried, VMEM), (ends, VMEM), (first_ends, VMEM),
-            (other_offset, VMEM), (other_factor, VMEM), (taps, VMEM), (inlet, SMEM), (slot, SMEM),
+            (other_offset, VMEM), (other_factor, VMEM), (taps, VMEM), (inlet, VMEM),
         ]
-        aliases = {}
-        if send is not None:
-            aliases = {len(ins): 1}
-            ins.append((send, ANY))
+        outs, scratch = [sds((rows, nodes))], []
+        if not first:
+            ins += [(slot, VMEM), (looked, VMEM)]
+            outs.append(sds((owners_total, 2 * half, LANES)))
+            scratch = [pltpu.SMEM((blocks,), jnp.int32), pltpu.SemaphoreType.DMA]
         return call(
-            functools.partial(
-                finish_kernel, lines, comps, groups, cap, segs, segs != 2, send is not None
-            ),
-            [sds((rows, nodes)), sds((owners_total, size, LANES))],
-            ins,
-            out_specs=[VMEM, ANY],
-            scratch=[pltpu.SemaphoreType.DMA((blocks,))],
-            aliases=aliases,
+            functools.partial(finish_kernel, lines, comps, groups, cap, segs, segs != 2, first),
+            outs, ins, scratch=scratch,
         )
 
-    spread, send = finish(None, 2 * half + extra)
-    looked, rates, send = call(
-        functools.partial(look_first_kernel, cap),
+    (spread,) = finish(None)
+    rates, send = call(
+        functools.partial(look_first_kernel, groups, cap),
         [
-            sds((owners_total, half, LANES)), sds((owners_total, cap, LANES)),
-            sds((owners_total, 2 * half + extra, LANES)),
+            sds((owners_total, cap, LANES)), sds((owners_total, 2 * half + extra, LANES)),
         ],
         [
-            (cell_recv, VMEM), (grid, VMEM),
-            (kappa.reshape(cell_count // LANES, LANES), VMEM), (send, ANY),
+            (cell_recv, VMEM), (grid, VMEM), (kappa.reshape(cell_count // LANES, LANES), VMEM),
+            (spread, VMEM), (slot, SMEM),
         ],
-        out_specs=[VMEM, VMEM, ANY],
-        scratch=[pltpu.VMEM((owners_total, extra, LANES), F32), pltpu.SemaphoreType.DMA((2,))],
-        aliases={3: 2},
     )
+    looked = send
     wide = 256 if cell_count % 256 == 0 else LANES
     (onehot,) = call(
         functools.partial(onehot_kernel, cap),
@@ -542,12 +533,9 @@
             offset, ends = result[0], result[1]
             got_ends = swap(ends, segs)
             other_offset = got_ends if segs == 2 else got_ends[:, 0]
-        outs, specs = [sds(grid.shape)], [VMEM]
-        scratch = [pltpu.VMEM((min(4, owners_total // chunk), 2 * (cell_count // wide) * comps, chunk * cap * LANES), BF16)]
+        outs = [sds(grid.shape)]
         if not last:
-            outs += [sds((owners_total, half, LANES)), sds((owners_total, 2 * half, LANES))]
-            specs += [VMEM, ANY]
-            scratch.append(pltpu.SemaphoreType.DMA((1,)))
+            outs.append(sds((owners_total, half, LANES)))
         result = call(
             functools.partial(update_kernel, cap, chunk, last),
             outs,
@@ -555,18 +543,26 @@
                 (cell_recv, VMEM), (got, VMEM), (looked, VMEM), (rates, VMEM), (onehot, VMEM),
                 (grid, VMEM),
             ],
-            out_specs=specs,
-            scratch=scratch,
+            scratch=[
+                pltpu.VMEM(
+                    (
+                        min(4, owners_total // chunk),
+                        2 * (cell_count // wide) * comps,
+                        chunk * cap * LANES,
+                    ),
+                    BF16,
+                )
+            ],
         )
         grid = result[0]
         if not last:
-            looked, send = result[1], result[2]
+            looked = result[1]
             (local,) = call(
                 functools.partial(taps_kernel, lines, comps, groups, 1),
                 [sds((rows, nodes))],
                 [(taps, VMEM), (offset, VMEM)],
             )
-            spread, send = finish(send, 2 * half)
+            spread, send = finish(looked)
     return (conc_out, grid)
 
 

time: 130 us -> 126 us (0.969)
  Pallas kernels: 32.8 us -> 26.9 us
    pallas_call x20, Pallas kernels: 32.8 us -> 26.9 us  [call(): pl.pallas_call(kernel, out_shape=outs, in_specs=[s for _, s in ins], out_...]
    ppermute x4, waiting for transfers between devices: 0.02 us -> 1.91 us  [swap(): return lax.ppermute(x, 'seg', [(0, 1), (1, 0)])]
    all_to_all x1, starting transfers between devices: 5.91 us -> 7.37 us  [exchange(): return lax.all_to_all(x, 'bundle', split_axis=0, concat_axis=0, tiled=True)]
    unnamed x26 -> x22, local copies, waits for them, and re-layouts: 6.62 us -> 6.61 us
  transfers between devices with their start and end apart: 5 -> 5, of which waited for: 1 -> 2; matrix products, arithmetic and copies ran while one was open for 0% -> 0% of each run, Pallas kernels for 12% -> 12%
where the time goes in v2:
time: 126 us; the launch traced here: 125 us
  blocking collectives  76.9 us (61%)
  Pallas kernels  26.9 us (21%)
  starting transfers between devices  12.3 us (10%)
  local copies, waits for them, and re-layouts  6.61 us (5%)
  waiting for transfers between devices  1.92 us (2%)
    all_to_all x4, blocking collectives, exchange(): return lax.all_to_all(x, 'bundle', split_axis=0, concat_axis=0, tiled=True)  76.9 us
    pallas_call x20, Pallas kernels, call(): pl.pallas_call(kernel, out_shape=outs, in_specs=[s for _, s in ins], out_...  26.9 us
    all_to_all x1, starting transfers between devices, exchange(): return lax.all_to_all(x, 'bundle', split_axis=0, concat_axis=0, tiled=True)  7.37 us
    unnamed x22, local copies, waits for them, and re-layouts  6.61 us
    ppermute x4, starting transfers between devices, swap(): return lax.ppermute(x, 'seg', [(0, 1), (1, 0)])  4.92 us
  transfers between devices with their start and end apart: 5, of which 2 were waited for; matrix products, arithmetic and copies ran while one was open for 0% of the time, Pallas kernels for 12%

profile of v2, /device:TPU:0, one launch (start us, length us, event | category | flops | bytes accessed | tf_op | source)
XLA Modules:
  0.0 125.4 jit_solution(11338410718634715930)
XLA Ops:
  0.6 0.0 copy-start.4
  0.6 0.0 copy-start.6
  0.7 0.7 copy-done.6
  1.3 0.7 copy-done.9
  2.0 1.3 %shard_map.104 = (s32[16]{0:T(128)S(1)}, s32[16,8,128]{2,1,0:T(8,128)}) custom-call(s32[1,4,1,4]{3,2,1,0:T(1,128)S(1)} %bitcast.6, s32[4,512]{1,0:T(4,128)S(1)} %copy-done.6), custom_call_target="tpu_custom_call" | custom-call | flops 1 | bytes 1 | tf_op jit(solution)/shard_map/pallas_call | solution.py:24
  3.3 7.4 %all-to-all-start = ((s32[16,8,128]{2,1,0:T(8,128)}), s32[16,8,128]{2,1,0:T(8,128)S(1)}, u32[]{:S(2)}, u32[]{:S(2)}) async-start(s32[16,8,128]{2,1,0:T(8,128)} %get-tuple-element.42), calls=%async_computation | async-start | bytes 131072 | tf_op jit(solution)/shard_map/all_to_all | solution.py:430
  10.7 0.0 copy-start.2
  10.7 0.9 copy-done.2
  11.6 0.7 copy-done.3
  12.3 0.7 copy-done.5
  13.0 0.7 copy-done.8
  13.7 0.7 copy-done.10
  14.3 1.9 %shard_map.105 = (f32[64,512]{1,0:T(8,128)S(1)}, f32[9,64,512]{2,1,0:T(8,128)S(1)}, f32[64,512]{1,0:T(8,128)S(1)}, f32[64,512]{1,0:T(8,128)S(1)}, f32[2,64,128]{...) custom-call(f32[4,16,512]{2,1,0:T(8,128)S(1)} %copy-done.2, f32[4,512]{1,0:T(4,128)S(1)} %copy-done.3, ...), custom_call_target="tpu_custom_call" | custom-call | flops 1 | bytes 1 | tf_op jit(solution)/shard_map/pallas_call | solution.py:24
  16.3 1.6 %collective-permute-start = (f32[2,64,128]{2,1,0:T(8,128)S(1)}, f32[2,64,128]{2,1,0:T(8,128)S(1)}, u32[]{:S(2)}, u32[]{:S(2)}) collective-permute-start(f32[2,64,128]{2,1,0:T(8,128)S(1)} %get-tuple-element.40.end_offset.end_factor), channel_id=1, source_target_pairs={{0,16},{16,0},{1,17},{17,1},{2,18},{18,2},{3,19},{19,3},{4,20},{20... | collective-permute-start | bytes 196616 | tf_op jit(solution)/shard_map/ppermute | solution.py:425
  17.8 1.4 %shard_map.106 = (f32[64,512]{1,0:T(8,128)S(1)}, f32[64,512]{1,0:T(8,128)S(1)}) custom-call(f32[33,16,128]{2,1,0:T(8,128)S(1)} %get-tuple-element.35.taps, f32[64,512]{1,0:T(8,128)S(1)} %get-tuple-element.36.refs_0_, f32[64,512]{1,0:T(8,128)S(1)} %get-tuple-element.37.refs_1_), custom_call_target="tpu_custom_call" | custom-call | flops 1 | bytes 1 | tf_op jit(solution)/shard_map/pallas_call | solution.py:24
  19.3 1.5 %collective-permute-done.other_offset.other_factor = f32[2,64,128]{2,1,0:T(8,128)S(1)} collective-permute-done((f32[2,64,128]{2,1,0:T(8,128)S(1)}, f32[2,64,128]{2,1,0:T(8,128)S(1)}, u32[]{:S(2)}, u32[]{:S(2)}) %collective-permute-start) | collective-permute-done | bytes 65568 | tf_op jit(solution)/shard_map/ppermute | solution.py:425
  20.7 0.4 shard_map.107.spread
  21.2 0.0 all-to-all-done.cells
  21.2 0.0 copy-start
  21.2 0.9 copy-done
  22.1 0.7 copy-done.7
  22.8 2.2 %shard_map.108 = (f32[16,2,128]{2,1,0:T(2,128)S(1)}, f32[16,72,128]{2,1,0:T(8,128)S(1)}) custom-call(s32[16,8,128]{2,1,0:T(8,128)S(1)} %all-to-all-done.cells, f32[16,2048]{1,0:T(8,128)S(1)} %copy-done, f32[16,128]{1,0:T(8,128)S(1)} %bitcast.5, f32[64,512]{1,0:T(8,128)S(1)} %shard_map.107.spread, s32[16]{0:T(128)S(1)} %get-tuple-element.34.order.slot.rest_0_), custom_call_target="tpu_custom_call" | custom-call | flops 1 | bytes 1 | tf_op jit(solution)/shard_map/pallas_call | solution.py:24
  25.0 22.9 %all_to_all.25.got = f32[16,72,128]{2,1,0:T(8,128)S(1)} all-to-all(f32[16,72,128]{2,1,0:T(8,128)S(1)} %get-tuple-element.43.looked), channel_id=1, replica_groups=mesh['seg'=2,'bundle'=16] {'bundle'}, dimensions={0} | all-to-all | bytes 1179648 | tf_op jit(solution)/shard_map/all_to_all | solution.py:430
  47.9 1.2 shard_map.109
  49.2 1.6 %collective-permute-start.1 = (f32[1,64,128]{2,1,0:T(8,128)S(1)}, f32[1,64,128]{2,1,0:T(8,128)S(1)}, u32[]{:S(2)}, u32[]{:S(2)}) collective-permute-start(f32[1,64,128]{2,1,0:T(8,128)S(1)} %get-tuple-element.47.end_offset), channel_id=1, source_target_pairs={{0,16},{16,0},{1,17},{17,1},{2,18},{18,2},{3,19},{19,3},{4,20},{20... | collective-permute-start | bytes 98312 | tf_op jit(solution)/shard_map/ppermute | solution.py:425
  50.7 1.8 %shard_map.111.onehot = bf16[4096,256]{1,0:T(8,128)(2,1)S(1)} custom-call(s32[16,8,128]{2,1,0:T(8,128)S(1)} %all-to-all-done.cells), custom_call_target="tpu_custom_call" | custom-call | flops 1 | bytes 1 | tf_op jit(solution)/shard_map/pallas_call | solution.py:24
  52.5 0.7 shard_map.110.local
  53.3 0.0 copy-done.1
  53.3 2.2 %shard_map.112 = (f32[16,2048]{1,0:T(8,128)S(1)}, f32[16,32,128]{2,1,0:T(8,128)S(1)}) custom-call(s32[16,8,128]{2,1,0:T(8,128)S(1)} %all-to-all-done.cells, f32[16,72,128]{2,1,0:T(8,128)S(1)} %all_to_all.25.got, f32[16,72,128]{2,1,0:T(8,128)S(1)} %get-tuple-element.43.looked, f32[16,2,128]{2,1,0:T(2,128)S(1)} %get-tuple-element.48.rates, ...), custom_call_target="tpu_custom_call" | custom-call | flops 1 | bytes 1 | tf_op jit(solution)/shard_map/pallas_call | solution.py:24
  55.5 0.0 collective-permute-done.1.other_offset
  55.5 0.8 shard_map.113
  56.4 17.3 %all_to_all.26.got = f32[16,64,128]{2,1,0:T(8,128)S(1)} all-to-all(f32[16,64,128]{2,1,0:T(8,128)S(1)} %get-tuple-element.51), channel_id=1, replica_groups=mesh['seg'=2,'bundle'=16] {'bundle'}, dimensions={0} | all-to-all | bytes 1048576 | tf_op jit(solution)/shard_map/all_to_all | solution.py:430
  73.6 1.2 shard_map.114
  74.9 0.6 collective-permute-start.2
  75.5 0.7 shard_map.115.local
  76.2 2.2 %shard_map.116 = (f32[16,2048]{1,0:T(8,128)S(1)}, f32[16,32,128]{2,1,0:T(8,128)S(1)}) custom-call(s32[16,8,128]{2,1,0:T(8,128)S(1)} %all-to-all-done.cells, f32[16,64,128]{2,1,0:T(8,128)S(1)} %all_to_all.26.got, f32[16,32,128]{2,1,0:T(8,128)S(1)} %get-tuple-element.49.rest_1_.looked, f32[16,2,128]{2,1,0:T(2,128)S(1)} %get-tuple-element.48.rates, ...), custom_call_target="tpu_custom_call" | custom-call | flops 1 | bytes 1 | tf_op jit(solution)/shard_map/pallas_call | solution.py:24
  78.4 0.4 collective-permute-done.2.other_offset
  78.9 0.8 shard_map.117
  79.7 18.4 %all_to_all.27.got = f32[16,64,128]{2,1,0:T(8,128)S(1)} all-to-all(f32[16,64,128]{2,1,0:T(8,128)S(1)} %get-tuple-element.58), channel_id=1, replica_groups=mesh['seg'=2,'bundle'=16] {'bundle'}, dimensions={0} | all-to-all | bytes 1048576 | tf_op jit(solution)/shard_map/all_to_all | solution.py:430
  98.1 1.2 shard_map.118
  99.3 1.2 collective-permute-start.3
  100.5 0.7 shard_map.119.local
  101.2 2.2 %shard_map.120 = (f32[16,2048]{1,0:T(8,128)S(1)}, f32[16,32,128]{2,1,0:T(8,128)S(1)}) custom-call(s32[16,8,128]{2,1,0:T(8,128)S(1)} %all-to-all-done.cells, f32[16,64,128]{2,1,0:T(8,128)S(1)} %all_to_all.27.got, f32[16,32,128]{2,1,0:T(8,128)S(1)} %get-tuple-element.56.rest_1_.looked, f32[16,2,128]{2,1,0:T(2,128)S(1)} %get-tuple-element.48.rates, ...), custom_call_target="tpu_custom_call" | custom-call | flops 1 | bytes 1 | tf_op jit(solution)/shard_map/pallas_call | solution.py:24
  103.5 0.0 collective-permute-done.3.other_offset
  103.5 0.8 shard_map.121
  104.3 18.4 %all_to_all.28.got = f32[16,64,128]{2,1,0:T(8,128)S(1)} all-to-all(f32[16,64,128]{2,1,0:T(8,128)S(1)} %get-tuple-element.64), channel_id=1, replica_groups=mesh['seg'=2,'bundle'=16] {'bundle'}, dimensions={0} | all-to-all | bytes 1048576 | tf_op jit(solution)/shard_map/all_to_all | solution.py:430
  122.7 1.4 %shard_map.123 = f32[16,2048]{1,0:T(8,128)} custom-call(s32[16,8,128]{2,1,0:T(8,128)S(1)} %all-to-all-done.cells, f32[16,64,128]{2,1,0:T(8,128)S(1)} %all_to_all.28.got, f32[16,32,128]{2,1,0:T(8,128)S(1)} %get-tuple-element.62.rest_1_.looked, f32[16,2,128]{2,1,0:T(2,128)S(1)} %get-tuple-element.48.rates, bf16[4096,256]{1,0:T(8,128)(2,1)S(1)} %shard_map.111.onehot, ...), custom_call_target="tpu_custom_call" | custom-call | flops 1 | bytes 1 | tf_op jit(solution)/shard_map/pallas_call | solution.py:24
  124.1 1.3 %shard_map.122 = f32[4,16,512]{2,1,0:T(8,128)} custom-call(f32[64,512]{1,0:T(8,128)S(1)} %get-tuple-element.63.spread, f32[16,64,128]{2,1,0:T(8,128)S(1)} %all_to_all.28.got, f32[16,128]{1,0:T(8,128)S(1)} %get-tuple-element.52.coupling, f32[64,512]{1,0:T(8,128)S(1)} %get-tuple-element.44.retain, f32[9,64,512]{2,1,0:T(8,128)S(1)} %get-tuple-element.45.levels, ...), custom_call_target="tpu_custom_call" | custom-call | flops 1 | bytes 1 | tf_op jit(solution)/shard_map/pallas_call | solution.py:24
  (8 shorter events, 0.0 us)
Async XLA Ops:
  0.6 47.3 %copy-start.4 = (f32[4,512]{1,0:T(4,128)S(1)}, f32[4,512]{1,0:T(4,128)}, u32[]{:S(2)}) copy-start(f32[4,512]{1,0:T(4,128)} %coupling.1) | copy-start | bytes 24580
  0.6 0.7 copy-start.6
  1.3 0.7 copy-start.9
  3.3 17.9 %all-to-all-start = ((s32[16,8,128]{2,1,0:T(8,128)}), s32[16,8,128]{2,1,0:T(8,128)S(1)}, u32[]{:S(2)}, u32[]{:S(2)}) async-start(s32[16,8,128]{2,1,0:T(8,128)} %get-tuple-element.42), calls=%async_computation | async-start | bytes 131072 | tf_op jit(solution)/shard_map/all_to_all | solution.py:430
  10.7 0.9 copy-start.2
  11.6 0.7 copy-start.3
  12.3 0.7 copy-start.5
  13.0 0.7 copy-start.8
  13.7 0.7 copy-start.10
  16.3 4.5 %collective-permute-start = (f32[2,64,128]{2,1,0:T(8,128)S(1)}, f32[2,64,128]{2,1,0:T(8,128)S(1)}, u32[]{:S(2)}, u32[]{:S(2)}) collective-permute-start(f32[2,64,128]{2,1,0:T(8,128)S(1)} %get-tuple-element.40.end_offset.end_factor), channel_id=1, source_target_pairs={{0,16},{16,0},{1,17},{17,1},{2,18},{18,2},{3,19},{19,3},{4,20},{20... | collective-permute-start | bytes 196616 | tf_op jit(solution)/shard_map/ppermute | solution.py:425
  21.2 0.9 copy-start
  22.1 0.7 copy-start.7
  47.9 5.4 %copy-start.1 = (f32[16,2048]{1,0:T(8,128)S(1)}, f32[16,2048]{1,0:T(8,128)}, u32[]{:S(2)}) copy-start(f32[16,2048]{1,0:T(8,128)} %grid.3) | copy-start | bytes 393220
  49.2 6.4 %collective-permute-start.1 = (f32[1,64,128]{2,1,0:T(8,128)S(1)}, f32[1,64,128]{2,1,0:T(8,128)S(1)}, u32[]{:S(2)}, u32[]{:S(2)}) collective-permute-start(f32[1,64,128]{2,1,0:T(8,128)S(1)} %get-tuple-element.47.end_offset), channel_id=1, source_target_pairs={{0,16},{16,0},{1,17},{17,1},{2,18},{18,2},{3,19},{19,3},{4,20},{20... | collective-permute-start | bytes 98312 | tf_op jit(solution)/shard_map/ppermute | solution.py:425
  74.9 4.0 %collective-permute-start.2 = (f32[1,64,128]{2,1,0:T(8,128)S(1)}, f32[1,64,128]{2,1,0:T(8,128)S(1)}, u32[]{:S(2)}, u32[]{:S(2)}) collective-permute-start(f32[1,64,128]{2,1,0:T(8,128)S(1)} %get-tuple-element.54.end_offset), channel_id=1, source_target_pairs={{0,16},{16,0},{1,17},{17,1},{2,18},{18,2},{3,19},{19,3},{4,20},{20... | collective-permute-start | bytes 98312 | tf_op jit(solution)/shard_map/ppermute | solution.py:425
  99.3 4.2 %collective-permute-start.3 = (f32[1,64,128]{2,1,0:T(8,128)S(1)}, f32[1,64,128]{2,1,0:T(8,128)S(1)}, u32[]{:S(2)}, u32[]{:S(2)}) collective-permute-start(f32[1,64,128]{2,1,0:T(8,128)S(1)} %get-tuple-element.60.end_offset), channel_id=1, source_target_pairs={{0,16},{16,0},{1,17},{17,1},{2,18},{18,2},{3,19},{19,3},{4,20},{20... | collective-permute-start | bytes 98312 | tf_op jit(solution)/shard_map/ppermute | solution.py:425

commit v3 on v2

--- a/solution.py
+++ b/solution.py
@@ -19,7 +19,7 @@
 ANY = pl.BlockSpec(memory_space=pl.ANY)
 
 
-def call(kernel, outs, ins, out_specs=None, scratch=()):
+def call(kernel, outs, ins, out_specs=None, scratch=(), flops=1e8):
     args = [a for a, _ in ins]
     return pl.pallas_call(
         kernel,
@@ -27,7 +27,7 @@
         in_specs=[s for _, s in ins],
         out_specs=out_specs or [VMEM] * len(outs),
         scratch_shapes=list(scratch),
-        cost_estimate=pl.CostEstimate(flops=1, bytes_accessed=1, transcendentals=0),
+        cost_estimate=pl.CostEstimate(flops=int(flops), bytes_accessed=1, transcendentals=0),
         compiler_params=pltpu.CompilerParams(vmem_limit_bytes=40 * 1024 * 1024),
     )(*args)
 
@@ -47,14 +47,14 @@
         owner = owners[0, line, 0, group]
         rank = count[owner]
         count[owner] = rank + 1
-        slot[b] = owner * cap + rank
+        slot[b : b + 1, :] = jnp.full((1, LANES), owner * cap + rank, jnp.int32)
         send[owner, pl.ds(rank, 1), :] = cells[
             pl.ds(line, 1), group * LANES : (group + 1) * LANES
         ]
 
 
 def where_slot(slot, b, cap):
-    s = slot[b]
+    s = slot[b, 0]
     return s // cap, s % cap
 
 
@@ -167,12 +167,24 @@
     return out
 
 
+def pack_ends(line, lane, first, last):
+    at = 2 * HALF * line
+    both = jnp.where(lane < LANES // 2, first, last)
+    both = pltpu.roll(both, (HALF + at) % LANES, 1)
+    return both, (lane >= at) & (lane < at + 2 * HALF)
+
+
+def unpack_ends(line, packed):
+    return pltpu.roll(packed, (-(HALF + 2 * HALF * line)) % LANES, 1)
+
+
 def first_kernel(
     lines, comps, groups, conc, slowness, retard, taps, inlet, order,
     retain, levels, offset, factor, ends, wide_taps, wide_inlet,
 ):
     lane = lax.broadcasted_iota(jnp.int32, (comps, LANES), 1)
     slow_by = column(retard[...], comps)
+    packed = [jnp.zeros((comps, LANES), F32)] * 2
     for t in range(taps.shape[1]):
         wide_taps[t] = jnp.broadcast_to(taps[:, t : t + 1], (comps, LANES))
     for line in range(lines):
@@ -204,8 +216,12 @@
         offsets = scan_line(levels, retain, values, line, comps, groups)
         for group in range(groups):
             put(offset, line, comps, group, offsets[group])
-        ends[0, pl.ds(line * comps, comps), :] = jnp.where(lane < 64, offsets[0], offsets[-1])
-        ends[1, pl.ds(line * comps, comps), :] = jnp.where(lane < 64, whole[0], whole[-1])
+        part, inside = pack_ends(line, lane, offsets[0], offsets[-1])
+        packed[0] = jnp.where(inside, part, packed[0])
+        part, inside = pack_ends(line, lane, whole[0], whole[-1])
+        packed[1] = jnp.where(inside, part, packed[1])
+    ends[0] = packed[0]
+    ends[1] = packed[1]
 
 
 def taps_kernel(lines, comps, groups, sources, taps, *refs):
@@ -231,9 +247,7 @@
     if first:
         (spread,) = rest
     else:
-        slot_in, looked, spread, send, slot, done = rest
-        copy = pltpu.make_async_copy(slot_in, slot, done)
-        copy.start()
+        slot, looked, spread, send = rest
     me = lax.axis_index("seg")
     lane = lax.broadcasted_iota(jnp.int32, (comps, LANES), 1)
     columns = tap_columns(taps)
@@ -242,12 +256,14 @@
 
         def part(s):
             if has_gather:
-                return other_offset[s, rows, :], other_factor[s, rows, :]
-            mine = me == s
-            return (
-                jnp.where(mine, end_offset[0, rows, :], other_offset[0, rows, :]),
-                jnp.where(mine, end_factor[1, rows, :], other_factor[1, rows, :]),
-            )
+                pair = other_offset[s], other_factor[s]
+            else:
+                mine = me == s
+                pair = (
+                    jnp.where(mine, end_offset[0], other_offset[0]),
+                    jnp.where(mine, end_factor[1], other_factor[1]),
+                )
+            return [unpack_ends(line, x) for x in pair]
 
         flow = inlet[rows, :]
         zero = jnp.zeros((comps, LANES), F32)
@@ -273,7 +289,6 @@
     if first:
         return
     send[:, 0 : cap * comps, :] = looked[...]
-    copy.wait()
     for b in range(lines * groups):
         place(send, slot, b, cap, comps, tile(spread, b // groups, comps, b % groups))
 
@@ -282,6 +297,7 @@
     lane = lax.broadcasted_iota(jnp.int32, (comps, LANES), 1)
     outs = list(outs)
     coupling_out = outs.pop() if first else None
+    packed = jnp.zeros((comps, LANES), F32)
     for line in range(lines):
         values = []
         for group in range(groups):
@@ -303,7 +319,10 @@
         offsets = scan_line(levels, retain, values, line, comps, groups)
         for group in range(groups):
             put(outs[0], line, comps, group, offsets[group])
-        outs[1][0, pl.ds(line * comps, comps), :] = jnp.where(lane < 64, offsets[0], offsets[-1])
+        part, inside = pack_ends(line, lane, offsets[0], offsets[-1])
+        packed = jnp.where(inside, part, packed)
+    if not last:
+        outs[1][0] = packed
 
 
 def gather_cells(grid, cell, comps, high_total):
@@ -323,9 +342,9 @@
     high_total = grid.shape[1] // LANES
     row = lax.broadcasted_iota(jnp.int32, (high_total, LANES), 0)
 
-    def one(owner, carry):
+    for owner in range(cells.shape[0]):
         for rank in range(cap):
-            cell = cells[owner, pl.ds(rank, 1), :]
+            cell = cells[owner, rank : rank + 1, :]
             valid = cell >= 0
             cell = jnp.maximum(cell, 0)
             send[owner, rank * comps : (rank + 1) * comps, :] = gather_cells(
@@ -335,37 +354,35 @@
             k = jnp.take_along_axis(kappa[...], low, axis=1, mode="promise_in_bounds")
             rate = jnp.sum(jnp.where(row == (cell >> 7), k, 0.0), axis=0, keepdims=True)
             rate = jnp.where(valid, rate, 0.0)
-            rates[owner, pl.ds(rank, 1), :] = rate
-            send[owner, pl.ds(2 * cap * comps + rank, 1), :] = rate
-        return carry
-
-    lax.fori_loop(0, cells.shape[0], one, 0, unroll=4)
+            rates[owner, rank : rank + 1, :] = rate
+            at = 2 * cap * comps + rank
+            send[owner, at : at + 1, :] = rate
     for b in range(slot.shape[0]):
         place(send, slot, b, cap, comps, tile(spread, b // groups, comps, b % groups))
 
 
-def onehot_kernel(cap, cells, onehot):
-    wide = onehot.shape[1]
+def onehot_kernel(cap, cells, order, onehot):
+    wide = onehot.shape[0]
     row = lax.broadcasted_iota(jnp.int32, (wide, LANES), 0)
-
-    def one(owner, carry):
+    for owner in range(cells.shape[0]):
         for rank in range(cap):
-            cell = cells[owner, pl.ds(rank, 1), :]
-            hit = jnp.where(row == (cell & (wide - 1)), 1.0, 0.0).astype(F32)
-            at = pl.multiple_of((owner * cap + rank) * LANES, LANES)
-            onehot[pl.ds(at, LANES), :] = hit.T.astype(BF16)
-        return carry
-
-    lax.fori_loop(0, cells.shape[0], one, 0)
+            cell = cells[owner, rank : rank + 1, :]
+            at = (owner * cap + rank) * LANES
+            onehot[:, at : at + LANES] = jnp.where(row == (cell & (wide - 1)), 1.0, 0.0).astype(BF16)
+
+
+def in_two(x):
+    coarse = x.astype(BF16)
+    return coarse, (x - coarse.astype(F32)).astype(BF16)
 
 
 def update_kernel(cap, chunk, last, cells, got, looked, rates, onehot, grid, *rest):
     if last:
         grid_out, masked = rest
     else:
-        grid_out, looked_out, masked = rest
+        grid_out, looked_out, masked, stack = rest
     comps = grid.shape[0]
-    wide = onehot.shape[1]
+    wide = onehot.shape[0]
     bits = wide.bit_length() - 1
     high_total = grid.shape[1] // wide
     owners_total = cells.shape[0]
@@ -385,8 +402,7 @@
                 span = slice(rank * comps, (rank + 1) * comps)
                 came = slice((cap + rank) * comps, (cap + rank + 1) * comps)
                 flux = jnp.where(valid, rate * (looked[owner, span, :] - got[owner, came, :]), 0.0)
-                coarse = flux.astype(BF16)
-                fine = (flux - coarse.astype(F32)).astype(BF16)
+                coarse, fine = in_two(flux)
                 high = jnp.broadcast_to((cell >> bits).astype(F32), (comps, LANES)).astype(BF16)
                 for h in range(high_total):
                     hit = high == jnp.asarray(h, BF16)
@@ -397,8 +413,9 @@
                         jnp.where(hit, fine, jnp.zeros_like(fine))
                     )
         first = start * cap * LANES
-        part = jnp.dot(
-            masked[turn], onehot[first : first + width, :], preferred_element_type=F32
+        part = lax.dot_general(
+            masked[turn], onehot[:, first : first + width], (((1,), (1,)), ((), ())),
+            preferred_element_type=F32,
         )
         total = part if total is None else total + part
     for h in range(high_total):
@@ -409,15 +426,25 @@
     if last:
         return
 
-    def one(owner, carry):
-        for rank in range(cap):
-            cell = jnp.maximum(cells[owner, pl.ds(rank, 1), :], 0)
-            looked_out[owner, rank * comps : (rank + 1) * comps, :] = gather_cells(
-                grid_out, cell, comps, grid.shape[1] // LANES
-            )
-        return carry
-
-    lax.fori_loop(0, owners_total, one, 0, unroll=4)
+    for h in range(high_total):
+        coarse, fine = in_two(grid_out[:, h * wide : (h + 1) * wide])
+        stack[h * comps : (h + 1) * comps, :] = coarse
+        stack[rows + h * comps : rows + (h + 1) * comps, :] = fine
+    for first in range(0, owners_total * cap, 4):
+        part = jnp.dot(
+            stack[...], onehot[:, first * LANES : (first + 4) * LANES], preferred_element_type=F32
+        )
+        for i in range(4):
+            owner, rank = (first + i) // cap, (first + i) % cap
+            cell = jnp.maximum(cells[owner, rank : rank + 1, :], 0)
+            high = jnp.broadcast_to(cell >> bits, (comps, LANES))
+            span = slice(i * LANES, (i + 1) * LANES)
+            found = jnp.zeros((comps, LANES), F32)
+            for h in range(high_total):
+                at = slice(h * comps, (h + 1) * comps)
+                at2 = slice(rows + h * comps, rows + (h + 1) * comps)
+                found = jnp.where(high == h, part[at, span] + part[at2, span], found)
+            looked_out[owner, rank * comps : (rank + 1) * comps, :] = found
 
 
 def swap(x, segs):
@@ -445,10 +472,10 @@
 
     slot, cell_send = call(
         functools.partial(route_kernel, groups, cap),
-        [sds((blocks,), jnp.int32), sds((owners_total, 8 * (-(-cap // 8)), LANES), jnp.int32)],
-        [(jnp.swapaxes(owners, 2, 3), SMEM), (cells, VMEM)],
-        out_specs=[SMEM, VMEM],
+        [sds((blocks, LANES), jnp.int32), sds((owners_total, 8 * (-(-cap // 8)), LANES), jnp.int32)],
+        [(jnp.swapaxes(owners, 2, 3), VMEM), (cells, VMEM)],
         scratch=[pltpu.SMEM((owners_total,), jnp.int32)],
+        flops=1e9,
     )
     cell_recv = exchange(cell_send)
 
@@ -456,7 +483,7 @@
         functools.partial(first_kernel, lines, comps, groups),
         [
             sds((rows, nodes)), sds((LEVELS + 2, rows, nodes)), sds((rows, nodes)),
-            sds((rows, nodes)), sds((2, rows, LANES)), sds((taps.shape[1], comps, LANES)),
+            sds((rows, nodes)), sds((2, comps, LANES)), sds((taps.shape[1], comps, LANES)),
             sds((rows, LANES)),
         ],
         [
@@ -482,14 +509,13 @@
             (local, VMEM), (carried, VMEM), (ends, VMEM), (first_ends, VMEM),
             (other_offset, VMEM), (other_factor, VMEM), (taps, VMEM), (inlet, VMEM),
         ]
-        outs, scratch = [sds((rows, nodes))], []
+        outs = [sds((rows, nodes))]
         if not first:
             ins += [(slot, VMEM), (looked, VMEM)]
             outs.append(sds((owners_total, 2 * half, LANES)))
-            scratch = [pltpu.SMEM((blocks,), jnp.int32), pltpu.SemaphoreType.DMA]
         return call(
             functools.partial(finish_kernel, lines, comps, groups, cap, segs, segs != 2, first),
-            outs, ins, scratch=scratch,
+            outs, ins,
         )
 
     (spread,) = finish(None)
@@ -500,21 +526,16 @@
         ],
         [
             (cell_recv, VMEM), (grid, VMEM), (kappa.reshape(cell_count // LANES, LANES), VMEM),
-            (spread, VMEM), (slot, SMEM),
+            (spread, VMEM), (slot, VMEM),
         ],
     )
     looked = send
     wide = 256 if cell_count % 256 == 0 else LANES
-    (onehot,) = call(
-        functools.partial(onehot_kernel, cap),
-        [sds((owners_total * cap * LANES, wide), BF16)],
-        [(cell_recv, VMEM)],
-    )
     coupling = slowness
     for step in range(STEPS):
         last = step == STEPS - 1
         got = exchange(send)
-        outs = [sds(conc.shape)] if last else [sds((rows, nodes)), sds((1, rows, LANES))]
+        outs = [sds(conc.shape)] if last else [sds((rows, nodes)), sds((1, comps, LANES))]
         if step == 0:
             outs.append(sds((blocks, LANES)))
         result = call(
@@ -522,7 +543,7 @@
             outs,
             [
                 (spread, VMEM), (got, VMEM), (coupling, VMEM), (retain, VMEM), (levels, VMEM),
-                (slot, SMEM),
+                (slot, VMEM),
             ],
         )
         if step == 0:
@@ -533,6 +554,12 @@
             offset, ends = result[0], result[1]
             got_ends = swap(ends, segs)
             other_offset = got_ends if segs == 2 else got_ends[:, 0]
+        if step == 0:
+            (onehot,) = call(
+                functools.partial(onehot_kernel, cap),
+                [sds((wide, owners_total * cap * LANES), BF16)],
+                [(cell_recv, VMEM), (ends, ANY)],
+            )
         outs = [sds(grid.shape)]
         if not last:
             outs.append(sds((owners_total, half, LANES)))
@@ -552,7 +579,8 @@
                     ),
                     BF16,
                 )
-            ],
+            ]
+            + ([] if last else [pltpu.VMEM((2 * (cell_count // wide) * comps, wide), BF16)]),
         )
         grid = result[0]
         if not last:

time: 126 us -> 116 us (0.921)
  local copies, waits for them, and re-layouts: 6.61 us -> 1.43 us
  Pallas kernels: 26.9 us -> 22.2 us
    unnamed x22 -> x18, local copies, waits for them, and re-layouts: 6.61 us -> 1.43 us
    pallas_call x20, Pallas kernels: 26.9 us -> 22.2 us  [call(): pl.pallas_call(kernel, out_shape=outs, in_specs=[s for _, s in ins], out_...]
  transfers between devices with their start and end apart: 5 -> 5, of which waited for: 2 -> 4; matrix products, arithmetic and copies ran while one was open for 0% -> 0% of each run, Pallas kernels for 12% -> 10%
where the time goes in v3:
time: 116 us; the launch traced here: 115 us
  blocking collectives  76.3 us (66%)
  Pallas kernels  22.2 us (19%)
  starting transfers between devices  12.1 us (10%)
  waiting for transfers between devices  2.5 us (2%)
  local copies, waits for them, and re-layouts  1.43 us (1%)
    all_to_all x4, blocking collectives, exchange(): return lax.all_to_all(x, 'bundle', split_axis=0, concat_axis=0, tiled=True)  76.3 us
    pallas_call x20, Pallas kernels, call(): pl.pallas_call(kernel, out_shape=outs, in_specs=[s for _, s in ins], out_...  22.2 us
    all_to_all x1, starting transfers between devices, exchange(): return lax.all_to_all(x, 'bundle', split_axis=0, concat_axis=0, tiled=True)  7.36 us
    ppermute x4, starting transfers between devices, swap(): return lax.ppermute(x, 'seg', [(0, 1), (1, 0)])  4.71 us
  transfers between devices with their start and end apart: 5, of which 4 were waited for; matrix products, arithmetic and copies ran while one was open for 0% of the time, Pallas kernels for 10%

profile of v3, /device:TPU:0, one launch (start us, length us, event | category | flops | bytes accessed | tf_op | source)
XLA Modules:
  0.0 115.3 jit_solution(12126916084040468308)
XLA Ops:
  0.6 0.0 copy-start.1
  0.6 0.0 copy-start.2
  0.7 0.0 copy-start.3
  0.7 0.7 copy-done.3
  1.4 0.0 copy-start.6
  1.4 0.7 copy-done.6
  2.1 0.0 copy-start.5
  2.1 0.8 shard_map.104
  2.9 7.4 %all-to-all-start = ((s32[16,8,128]{2,1,0:T(8,128)}), s32[16,8,128]{2,1,0:T(8,128)S(1)}, u32[]{:S(2)}, u32[]{:S(2)}) async-start(s32[16,8,128]{2,1,0:T(8,128)} %get-tuple-element.42), calls=%async_computation | async-start | bytes 131072 | tf_op jit(solution)/shard_map/all_to_all | solution.py:457
  10.3 0.0 copy-done.1
  10.3 0.0 copy-done.2
  10.3 0.0 copy-done.4
  10.3 0.0 copy-done.7
  10.3 0.0 copy-done.8
  10.3 1.8 %shard_map.105 = (f32[64,512]{1,0:T(8,128)S(1)}, f32[9,64,512]{2,1,0:T(8,128)S(1)}, f32[64,512]{1,0:T(8,128)S(1)}, f32[64,512]{1,0:T(8,128)S(1)}, f32[2,16,128]{...) custom-call(f32[4,16,512]{2,1,0:T(8,128)S(1)} %copy-done.2, f32[4,512]{1,0:T(4,128)S(1)} %copy-done.1, ...), custom_call_target="tpu_custom_call" | custom-call | flops 100000000 | bytes 1 | tf_op jit(solution)/shard_map/pallas_call | solution.py:24
  12.1 1.6 %collective-permute-start = (f32[2,16,128]{2,1,0:T(8,128)S(1)}, f32[2,16,128]{2,1,0:T(8,128)S(1)}, u32[]{:S(2)}, u32[]{:S(2)}) collective-permute-start(f32[2,16,128]{2,1,0:T(8,128)S(1)} %get-tuple-element.40.end_offset.end_factor), channel_id=1, source_target_pairs={{0,16},{16,0},{1,17},{17,1},{2,18},{18,2},{3,19},{19,3},{4,20},{20... | collective-permute-start | bytes 49160 | tf_op jit(solution)/shard_map/ppermute | solution.py:452
  13.6 1.4 %shard_map.106 = (f32[64,512]{1,0:T(8,128)S(1)}, f32[64,512]{1,0:T(8,128)S(1)}) custom-call(f32[33,16,128]{2,1,0:T(8,128)S(1)} %get-tuple-element.35.taps, f32[64,512]{1,0:T(8,128)S(1)} %get-tuple-element.36.refs_0_, f32[64,512]{1,0:T(8,128)S(1)} %get-tuple-element.37.refs_1_), custom_call_target="tpu_custom_call" | custom-call | flops 100000000 | bytes 1 | tf_op jit(solution)/shard_map/pallas_call | solution.py:24
  15.1 0.8 collective-permute-done.other_offset.other_factor
  15.9 0.5 shard_map.107.spread
  16.4 0.8 all-to-all-done.cells
  17.1 0.0 copy-done
  17.2 0.0 copy-done.5
  17.2 1.4 %shard_map.108 = (f32[16,2,128]{2,1,0:T(2,128)S(1)}, f32[16,72,128]{2,1,0:T(8,128)S(1)}) custom-call(s32[16,8,128]{2,1,0:T(8,128)S(1)} %all-to-all-done.cells, f32[16,2048]{1,0:T(8,128)S(1)} %copy-done, f32[16,128]{1,0:T(8,128)S(1)} %bitcast.5, f32[64,512]{1,0:T(8,128)S(1)} %shard_map.107.spread, s32[16,128]{1,0:T(8,128)S(1)} %get-tuple-element.34.order.slot.rest_0_), custom_call_target="tpu_custom_call" | custom-call | flops 100000000 | bytes 1 | tf_op jit(solution)/shard_map/pallas_call | solution.py:24
  18.5 22.3 %all_to_all.25.got = f32[16,72,128]{2,1,0:T(8,128)S(1)} all-to-all(f32[16,72,128]{2,1,0:T(8,128)S(1)} %get-tuple-element.43.looked), channel_id=1, replica_groups=mesh['seg'=2,'bundle'=16] {'bundle'}, dimensions={0} | all-to-all | bytes 1179648 | tf_op jit(solution)/shard_map/all_to_all | solution.py:457
  40.9 0.8 shard_map.109
  41.7 0.7 shard_map.110.local
  42.4 1.6 %collective-permute-start.1 = (f32[1,16,128]{2,1,0:T(8,128)S(1)}, f32[1,16,128]{2,1,0:T(8,128)S(1)}, u32[]{:S(2)}, u32[]{:S(2)}) collective-permute-start(f32[1,16,128]{2,1,0:T(8,128)S(1)} %get-tuple-element.47.order.end_offset), channel_id=1, source_target_pairs={{0,16},{16,0},{1,17},{17,1},{2,18},{18,2},{3,19},{19,3},{4,20},{20... | collective-permute-start | bytes 24584 | tf_op jit(solution)/shard_map/ppermute | solution.py:452
  44.0 0.6 shard_map.111.onehot
  44.6 2.5 %shard_map.112 = (f32[16,2048]{1,0:T(8,128)S(1)}, f32[16,32,128]{2,1,0:T(8,128)S(1)}) custom-call(s32[16,8,128]{2,1,0:T(8,128)S(1)} %all-to-all-done.cells, f32[16,72,128]{2,1,0:T(8,128)S(1)} %all_to_all.25.got, f32[16,72,128]{2,1,0:T(8,128)S(1)} %get-tuple-element.43.looked, f32[16,2,128]{2,1,0:T(2,128)S(1)} %get-tuple-element.48.rates, ...), custom_call_target="tpu_custom_call" | custom-call | flops 100000000 | bytes 1 | tf_op jit(solution)/shard_map/pallas_call | solution.py:24
  47.1 0.0 collective-permute-done.1.other_offset
  47.1 0.5 shard_map.113
  47.6 17.3 %all_to_all.26.got = f32[16,64,128]{2,1,0:T(8,128)S(1)} all-to-all(f32[16,64,128]{2,1,0:T(8,128)S(1)} %get-tuple-element.51), channel_id=1, replica_groups=mesh['seg'=2,'bundle'=16] {'bundle'}, dimensions={0} | all-to-all | bytes 1048576 | tf_op jit(solution)/shard_map/all_to_all | solution.py:457
  64.8 0.8 shard_map.114
  65.6 0.7 shard_map.115.local
  66.4 0.6 collective-permute-start.2
  67.0 2.5 %shard_map.116 = (f32[16,2048]{1,0:T(8,128)S(1)}, f32[16,32,128]{2,1,0:T(8,128)S(1)}) custom-call(s32[16,8,128]{2,1,0:T(8,128)S(1)} %all-to-all-done.cells, f32[16,64,128]{2,1,0:T(8,128)S(1)} %all_to_all.26.got, f32[16,32,128]{2,1,0:T(8,128)S(1)} %get-tuple-element.49.rest_1_.looked, f32[16,2,128]{2,1,0:T(2,128)S(1)} %get-tuple-element.48.rates, ...), custom_call_target="tpu_custom_call" | custom-call | flops 100000000 | bytes 1 | tf_op jit(solution)/shard_map/pallas_call | solution.py:24
  69.5 0.6 collective-permute-done.2.other_offset
  70.1 0.5 shard_map.117
  70.6 18.4 %all_to_all.27.got = f32[16,64,128]{2,1,0:T(8,128)S(1)} all-to-all(f32[16,64,128]{2,1,0:T(8,128)S(1)} %get-tuple-element.58), channel_id=1, replica_groups=mesh['seg'=2,'bundle'=16] {'bundle'}, dimensions={0} | all-to-all | bytes 1048576 | tf_op jit(solution)/shard_map/all_to_all | solution.py:457
  89.0 0.8 shard_map.118
  89.8 0.7 shard_map.119.local
  90.5 0.9 collective-permute-start.3
  91.4 2.5 %shard_map.120 = (f32[16,2048]{1,0:T(8,128)S(1)}, f32[16,32,128]{2,1,0:T(8,128)S(1)}) custom-call(s32[16,8,128]{2,1,0:T(8,128)S(1)} %all-to-all-done.cells, f32[16,64,128]{2,1,0:T(8,128)S(1)} %all_to_all.27.got, f32[16,32,128]{2,1,0:T(8,128)S(1)} %get-tuple-element.56.rest_1_.looked, f32[16,2,128]{2,1,0:T(2,128)S(1)} %get-tuple-element.48.rates, ...), custom_call_target="tpu_custom_call" | custom-call | flops 100000000 | bytes 1 | tf_op jit(solution)/shard_map/pallas_call | solution.py:24
  93.9 0.3 collective-permute-done.3.other_offset
  94.2 0.5 shard_map.121
  94.7 18.4 %all_to_all.28.got = f32[16,64,128]{2,1,0:T(8,128)S(1)} all-to-all(f32[16,64,128]{2,1,0:T(8,128)S(1)} %get-tuple-element.64), channel_id=1, replica_groups=mesh['seg'=2,'bundle'=16] {'bundle'}, dimensions={0} | all-to-all | bytes 1048576 | tf_op jit(solution)/shard_map/all_to_all | solution.py:457
  113.1 1.4 %shard_map.123 = f32[16,2048]{1,0:T(8,128)} custom-call(s32[16,8,128]{2,1,0:T(8,128)S(1)} %all-to-all-done.cells, f32[16,64,128]{2,1,0:T(8,128)S(1)} %all_to_all.28.got, f32[16,32,128]{2,1,0:T(8,128)S(1)} %get-tuple-element.62.rest_1_.looked, f32[16,2,128]{2,1,0:T(2,128)S(1)} %get-tuple-element.48.rates, bf16[256,4096]{1,0:T(8,128)(2,1)S(1)} %shard_map.111.onehot, ...), custom_call_target="tpu_custom_call" | custom-call | flops 100000000 | bytes 1 | tf_op jit(solution)/shard_map/pallas_call | solution.py:24
  114.5 0.8 shard_map.122
  (4 shorter events, 0.0 us)
Async XLA Ops:
  0.6 9.6 %copy-start.1 = (f32[4,512]{1,0:T(4,128)S(1)}, f32[4,512]{1,0:T(4,128)}, u32[]{:S(2)}) copy-start(f32[4,512]{1,0:T(4,128)} %coupling.1) | copy-start | bytes 24580
  0.6 9.6 %copy-start.2 = (f32[4,16,512]{2,1,0:T(8,128)S(1)}, f32[4,16,512]{2,1,0:T(8,128)}, u32[]{:S(2)}) copy-start(f32[4,16,512]{2,1,0:T(8,128)} %conc.1) | copy-start | bytes 393220
  0.7 0.7 copy-start.3
  1.4 0.7 copy-start.6
  2.1 8.2 %copy-start.4 = (f32[16,33]{1,0:T(8,128)S(1)}, f32[16,33]{1,0:T(8,128)}, u32[]{:S(2)}) copy-start(f32[16,33]{1,0:T(8,128)} %taps.1) | copy-start | bytes 6340
  2.1 8.2 %copy-start.7 = (f32[4,16]{1,0:T(4,128)S(1)}, f32[4,16]{1,0:T(4,128)}, u32[]{:S(2)}) copy-start(f32[4,16]{1,0:T(4,128)} %inlet.1) | copy-start | bytes 772
  2.1 8.2 %copy-start.8 = (f32[16]{0:T(128)S(1)}, f32[16]{0:T(128)}, u32[]{:S(2)}) copy-start(f32[16]{0:T(128)} %param.11) | copy-start | bytes 196
  2.1 15.1 %copy-start = (f32[16,2048]{1,0:T(8,128)S(1)}, f32[16,2048]{1,0:T(8,128)}, u32[]{:S(2)}) copy-start(f32[16,2048]{1,0:T(8,128)} %grid.3) | copy-start | bytes 393220
  2.1 15.1 %copy-start.5 = (f32[2048]{0:T(1024)S(1)}, f32[2048]{0:T(1024)}, u32[]{:S(2)}) copy-start(f32[2048]{0:T(1024)} %param.15) | copy-start | bytes 24580
  2.9 14.3 %all-to-all-start = ((s32[16,8,128]{2,1,0:T(8,128)}), s32[16,8,128]{2,1,0:T(8,128)S(1)}, u32[]{:S(2)}, u32[]{:S(2)}) async-start(s32[16,8,128]{2,1,0:T(8,128)} %get-tuple-element.42), calls=%async_computation | async-start | bytes 131072 | tf_op jit(solution)/shard_map/all_to_all | solution.py:457
  12.1 3.8 %collective-permute-start = (f32[2,16,128]{2,1,0:T(8,128)S(1)}, f32[2,16,128]{2,1,0:T(8,128)S(1)}, u32[]{:S(2)}, u32[]{:S(2)}) collective-permute-start(f32[2,16,128]{2,1,0:T(8,128)S(1)} %get-tuple-element.40.end_offset.end_factor), channel_id=1, source_target_pairs={{0,16},{16,0},{1,17},{17,1},{2,18},{18,2},{3,19},{19,3},{4,20},{20... | collective-permute-start | bytes 49160 | tf_op jit(solution)/shard_map/ppermute | solution.py:452
  42.4 4.7 %collective-permute-start.1 = (f32[1,16,128]{2,1,0:T(8,128)S(1)}, f32[1,16,128]{2,1,0:T(8,128)S(1)}, u32[]{:S(2)}, u32[]{:S(2)}) collective-permute-start(f32[1,16,128]{2,1,0:T(8,128)S(1)} %get-tuple-element.47.order.end_offset), channel_id=1, source_target_pairs={{0,16},{16,0},{1,17},{17,1},{2,18},{18,2},{3,19},{19,3},{4,20},{20... | collective-permute-start | bytes 24584 | tf_op jit(solution)/shard_map/ppermute | solution.py:452
  66.4 3.7 %collective-permute-start.2 = (f32[1,16,128]{2,1,0:T(8,128)S(1)}, f32[1,16,128]{2,1,0:T(8,128)S(1)}, u32[]{:S(2)}, u32[]{:S(2)}) collective-permute-start(f32[1,16,128]{2,1,0:T(8,128)S(1)} %get-tuple-element.54.end_offset), channel_id=1, source_target_pairs={{0,16},{16,0},{1,17},{17,1},{2,18},{18,2},{3,19},{19,3},{4,20},{20... | collective-permute-start | bytes 24584 | tf_op jit(solution)/shard_map/ppermute | solution.py:452
  90.5 3.7 %collective-permute-start.3 = (f32[1,16,128]{2,1,0:T(8,128)S(1)}, f32[1,16,128]{2,1,0:T(8,128)S(1)}, u32[]{:S(2)}, u32[]{:S(2)}) collective-permute-start(f32[1,16,128]{2,1,0:T(8,128)S(1)} %get-tuple-element.60.end_offset), channel_id=1, source_target_pairs={{0,16},{16,0},{1,17},{17,1},{2,18},{18,2},{3,19},{19,3},{4,20},{20... | collective-permute-start | bytes 24584 | tf_op jit(solution)/shard_map/ppermute | solution.py:452

commit v4 on v3

--- a/solution.py
+++ b/solution.py
@@ -19,7 +19,7 @@
 ANY = pl.BlockSpec(memory_space=pl.ANY)
 
 
-def call(kernel, outs, ins, out_specs=None, scratch=(), flops=1e8):
+def call(kernel, outs, ins, out_specs=None, scratch=(), flops=1):
     args = [a for a, _ in ins]
     return pl.pallas_call(
         kernel,
@@ -376,11 +376,7 @@
     return coarse, (x - coarse.astype(F32)).astype(BF16)
 
 
-def update_kernel(cap, chunk, last, cells, got, looked, rates, onehot, grid, *rest):
-    if last:
-        grid_out, masked = rest
-    else:
-        grid_out, looked_out, masked, stack = rest
+def update_kernel(cap, chunk, cells, got, looked, rates, onehot, grid, grid_out, masked):
     comps = grid.shape[0]
     wide = onehot.shape[0]
     bits = wide.bit_length() - 1
@@ -423,11 +419,17 @@
         at = slice(h * comps, (h + 1) * comps)
         at2 = slice(rows + h * comps, rows + (h + 1) * comps)
         grid_out[:, span] = grid[:, span] - 0.25 * (total[at, :] + total[at2, :])
-    if last:
-        return
-
+
+
+def look_kernel(cap, cells, onehot, grid, looked, stack):
+    comps = grid.shape[0]
+    wide = onehot.shape[0]
+    bits = wide.bit_length() - 1
+    high_total = grid.shape[1] // wide
+    owners_total = cells.shape[0]
+    rows = high_total * comps
     for h in range(high_total):
-        coarse, fine = in_two(grid_out[:, h * wide : (h + 1) * wide])
+        coarse, fine = in_two(grid[:, h * wide : (h + 1) * wide])
         stack[h * comps : (h + 1) * comps, :] = coarse
         stack[rows + h * comps : rows + (h + 1) * comps, :] = fine
     for first in range(0, owners_total * cap, 4):
@@ -444,7 +446,7 @@
                 at = slice(h * comps, (h + 1) * comps)
                 at2 = slice(rows + h * comps, rows + (h + 1) * comps)
                 found = jnp.where(high == h, part[at, span] + part[at2, span], found)
-            looked_out[owner, rank * comps : (rank + 1) * comps, :] = found
+            looked[owner, rank * comps : (rank + 1) * comps, :] = found
 
 
 def swap(x, segs):
@@ -472,7 +474,7 @@
 
     slot, cell_send = call(
         functools.partial(route_kernel, groups, cap),
-        [sds((blocks, LANES), jnp.int32), sds((owners_total, 8 * (-(-cap // 8)), LANES), jnp.int32)],
+        [sds((blocks, LANES), jnp.int32), sds((owners_total, cap, LANES), jnp.int32)],
         [(jnp.swapaxes(owners, 2, 3), VMEM), (cells, VMEM)],
         scratch=[pltpu.SMEM((owners_total,), jnp.int32)],
         flops=1e9,
@@ -490,6 +492,7 @@
             (conc, VMEM), (slowness, VMEM), (retard.reshape(1, comps), VMEM), (taps, VMEM),
             (inlet, VMEM), (slot, ANY),
         ],
+        flops=1e8,
     )
     first_ends = ends
     other = swap(ends, segs)
@@ -501,6 +504,7 @@
         functools.partial(taps_kernel, lines, comps, groups, 2),
         [sds((rows, nodes))] * 2,
         [(taps, VMEM), (offset, VMEM), (factor, VMEM)],
+        flops=1e8,
     )
 
     def finish(looked):
@@ -515,7 +519,7 @@
             outs.append(sds((owners_total, 2 * half, LANES)))
         return call(
             functools.partial(finish_kernel, lines, comps, groups, cap, segs, segs != 2, first),
-            outs, ins,
+            outs, ins, flops=1e8 if first else 1,
         )
 
     (spread,) = finish(None)
@@ -528,6 +532,7 @@
             (cell_recv, VMEM), (grid, VMEM), (kappa.reshape(cell_count // LANES, LANES), VMEM),
             (spread, VMEM), (slot, VMEM),
         ],
+        flops=1e8,
     )
     looked = send
     wide = 256 if cell_count % 256 == 0 else LANES
@@ -560,12 +565,9 @@
                 [sds((wide, owners_total * cap * LANES), BF16)],
                 [(cell_recv, VMEM), (ends, ANY)],
             )
-        outs = [sds(grid.shape)]
-        if not last:
-            outs.append(sds((owners_total, half, LANES)))
-        result = call(
-            functools.partial(update_kernel, cap, chunk, last),
-            outs,
+        (grid,) = call(
+            functools.partial(update_kernel, cap, chunk),
+            [sds(grid.shape)],
             [
                 (cell_recv, VMEM), (got, VMEM), (looked, VMEM), (rates, VMEM), (onehot, VMEM),
                 (grid, VMEM),
@@ -579,12 +581,15 @@
                     ),
                     BF16,
                 )
-            ]
-            + ([] if last else [pltpu.VMEM((2 * (cell_count // wide) * comps, wide), BF16)]),
+            ],
         )
-        grid = result[0]
         if not last:
-            looked = result[1]
+            (looked,) = call(
+                functools.partial(look_kernel, cap),
+                [sds((owners_total, half, LANES))],
+                [(cell_recv, VMEM), (onehot, VMEM), (grid, VMEM)],
+                scratch=[pltpu.VMEM((2 * (cell_count // wide) * comps, wide), BF16)],
+            )
             (local,) = call(
                 functools.partial(taps_kernel, lines, comps, groups, 1),
                 [sds((rows, nodes))],

time: 116 us -> 113 us (0.974)
  Pallas kernels: 22.2 us -> 19.2 us
    pallas_call x20 -> x23, Pallas kernels: 22.2 us -> 19.2 us  [call(): pl.pallas_call(kernel, out_shape=outs, in_specs=[s for _, s in ins], out_...]
where the time goes in v4:
time: 113 us
  blocking collectives  76.7 us (68%)
  Pallas kernels  19.2 us (17%)
  starting transfers between devices  12.1 us (11%)
  waiting for transfers between devices  2.4 us (2%)
  local copies, waits for them, and re-layouts  1.43 us (1%)
    all_to_all x4, blocking collectives, exchange(): return lax.all_to_all(x, 'bundle', split_axis=0, concat_axis=0, tiled=True)  76.7 us
    pallas_call x23, Pallas kernels, call(): pl.pallas_call(kernel, out_shape=outs, in_specs=[s for _, s in ins], out_...  19.2 us
    all_to_all x1, starting transfers between devices, exchange(): return lax.all_to_all(x, 'bundle', split_axis=0, concat_axis=0, tiled=True)  7.36 us
    ppermute x4, starting transfers between devices, swap(): return lax.ppermute(x, 'seg', [(0, 1), (1, 0)])  4.74 us
  transfers between devices with their start and end apart: 5, of which 4 were waited for; matrix products, arithmetic and copies ran while one was open for 0% of the time, Pallas kernels for 10%

profile of v4, /device:TPU:0, one launch (start us, length us, event | category | flops | bytes accessed | tf_op | source)
XLA Modules:
  0.0 112.7 jit_solution(10239608982603057640)
XLA Ops:
  0.6 0.0 copy-start.1
  0.6 0.0 copy-start.2
  0.7 0.0 copy-start.3
  0.7 0.7 copy-done.3
  1.4 0.7 copy-done.6
  2.1 0.0 copy-start.5
  2.1 0.8 shard_map.104
  2.9 7.4 %all-to-all-start = ((s32[16,2,128]{2,1,0:T(2,128)}), s32[16,2,128]{2,1,0:T(2,128)S(1)}, u32[]{:S(2)}, u32[]{:S(2)}) async-start(s32[16,2,128]{2,1,0:T(2,128)} %get-tuple-element.36), calls=%async_computation | async-start | bytes 32768 | tf_op jit(solution)/shard_map/all_to_all | solution.py:459
  10.2 0.0 copy-done.1
  10.2 0.0 copy-done.2
  10.2 0.0 copy-done.4
  10.3 0.0 copy-done.7
  10.3 1.8 %shard_map.105 = (f32[64,512]{1,0:T(8,128)S(1)}, f32[9,64,512]{2,1,0:T(8,128)S(1)}, f32[64,512]{1,0:T(8,128)S(1)}, f32[64,512]{1,0:T(8,128)S(1)}, f32[2,16,128]{...) custom-call(f32[4,16,512]{2,1,0:T(8,128)S(1)} %copy-done.2, f32[4,512]{1,0:T(4,128)S(1)} %copy-done.1, ...), custom_call_target="tpu_custom_call" | custom-call | flops 100000000 | bytes 1 | tf_op jit(solution)/shard_map/pallas_call | solution.py:24
  12.0 1.6 %collective-permute-start = (f32[2,16,128]{2,1,0:T(8,128)S(1)}, f32[2,16,128]{2,1,0:T(8,128)S(1)}, u32[]{:S(2)}, u32[]{:S(2)}) collective-permute-start(f32[2,16,128]{2,1,0:T(8,128)S(1)} %get-tuple-element.34.end_offset.end_factor), channel_id=1, source_target_pairs={{0,16},{16,0},{1,17},{17,1},{2,18},{18,2},{3,19},{19,3},{4,20},{20... | collective-permute-start | bytes 49160 | tf_op jit(solution)/shard_map/ppermute | solution.py:454
  13.6 1.4 %shard_map.106 = (f32[64,512]{1,0:T(8,128)S(1)}, f32[64,512]{1,0:T(8,128)S(1)}) custom-call(f32[33,16,128]{2,1,0:T(8,128)S(1)} %get-tuple-element.29.taps, f32[64,512]{1,0:T(8,128)S(1)} %get-tuple-element.30.refs_0_, f32[64,512]{1,0:T(8,128)S(1)} %get-tuple-element.31.refs_1_), custom_call_target="tpu_custom_call" | custom-call | flops 100000000 | bytes 1 | tf_op jit(solution)/shard_map/pallas_call | solution.py:24
  15.0 0.8 collective-permute-done.other_offset.other_factor
  15.8 0.5 shard_map.107.spread
  16.3 0.4 all-to-all-done.cells
  16.7 0.0 copy-done
  16.7 1.4 %shard_map.108 = (f32[16,2,128]{2,1,0:T(2,128)S(1)}, f32[16,72,128]{2,1,0:T(8,128)S(1)}) custom-call(s32[16,2,128]{2,1,0:T(2,128)S(1)} %all-to-all-done.cells, f32[16,2048]{1,0:T(8,128)S(1)} %copy-done, f32[16,128]{1,0:T(8,128)S(1)} %bitcast.5, f32[64,512]{1,0:T(8,128)S(1)} %shard_map.107.spread, s32[16,128]{1,0:T(8,128)S(1)} %get-tuple-element.28.order.slot.rest_0_), custom_call_target="tpu_custom_call" | custom-call | flops 100000000 | bytes 1 | tf_op jit(solution)/shard_map/pallas_call | solution.py:24
  18.1 22.7 %all_to_all.25.got = f32[16,72,128]{2,1,0:T(8,128)S(1)} all-to-all(f32[16,72,128]{2,1,0:T(8,128)S(1)} %get-tuple-element.37.looked), channel_id=1, replica_groups=mesh['seg'=2,'bundle'=16] {'bundle'}, dimensions={0} | all-to-all | bytes 1179648 | tf_op jit(solution)/shard_map/all_to_all | solution.py:459
  40.8 0.8 shard_map.109
  41.6 1.6 %collective-permute-start.1 = (f32[1,16,128]{2,1,0:T(8,128)S(1)}, f32[1,16,128]{2,1,0:T(8,128)S(1)}, u32[]{:S(2)}, u32[]{:S(2)}) collective-permute-start(f32[1,16,128]{2,1,0:T(8,128)S(1)} %get-tuple-element.41.order.end_offset), channel_id=1, source_target_pairs={{0,16},{16,0},{1,17},{17,1},{2,18},{18,2},{3,19},{19,3},{4,20},{20... | collective-permute-start | bytes 24584 | tf_op jit(solution)/shard_map/ppermute | solution.py:454
  43.2 0.6 shard_map.111.onehot
  43.8 0.8 shard_map.112.grid
  44.6 0.7 shard_map.110.local
  45.3 0.7 shard_map.113.rest_1_.looked
  46.0 0.0 collective-permute-done.1.other_offset
  46.1 0.5 shard_map.114
  46.6 17.3 %all_to_all.26.got = f32[16,64,128]{2,1,0:T(8,128)S(1)} all-to-all(f32[16,64,128]{2,1,0:T(8,128)S(1)} %get-tuple-element.44), channel_id=1, replica_groups=mesh['seg'=2,'bundle'=16] {'bundle'}, dimensions={0} | all-to-all | bytes 1048576 | tf_op jit(solution)/shard_map/all_to_all | solution.py:459
  63.8 0.8 shard_map.115
  64.6 0.8 collective-permute-start.2
  65.4 0.8 shard_map.117.grid
  66.2 0.7 shard_map.116.local
  67.0 0.7 shard_map.118.rest_1_.looked
  67.7 0.6 collective-permute-done.2.other_offset
  68.3 0.5 shard_map.119
  68.8 18.4 %all_to_all.27.got = f32[16,64,128]{2,1,0:T(8,128)S(1)} all-to-all(f32[16,64,128]{2,1,0:T(8,128)S(1)} %get-tuple-element.49), channel_id=1, replica_groups=mesh['seg'=2,'bundle'=16] {'bundle'}, dimensions={0} | all-to-all | bytes 1048576 | tf_op jit(solution)/shard_map/all_to_all | solution.py:459
  87.1 0.8 shard_map.120
  87.9 0.8 collective-permute-start.3
  88.7 0.8 shard_map.122.grid
  89.5 0.7 shard_map.121.local
  90.3 0.7 shard_map.123.rest_1_.looked
  91.0 0.6 collective-permute-done.3.other_offset
  91.6 0.5 shard_map.124
  92.1 18.4 %all_to_all.28.got = f32[16,64,128]{2,1,0:T(8,128)S(1)} all-to-all(f32[16,64,128]{2,1,0:T(8,128)S(1)} %get-tuple-element.53), channel_id=1, replica_groups=mesh['seg'=2,'bundle'=16] {'bundle'}, dimensions={0} | all-to-all | bytes 1048576 | tf_op jit(solution)/shard_map/all_to_all | solution.py:459
  110.5 1.4 %shard_map.126 = f32[16,2048]{1,0:T(8,128)} custom-call(s32[16,2,128]{2,1,0:T(2,128)S(1)} %all-to-all-done.cells, f32[16,64,128]{2,1,0:T(8,128)S(1)} %all_to_all.28.got, f32[16,32,128]{2,1,0:T(8,128)S(1)} %shard_map.123.rest_1_.looked, f32[16,2,128]{2,1,0:T(2,128)S(1)} %get-tuple-element.42.rates, bf16[256,4096]{1,0:T(8,128)(2,1)S(1)} %shard_map.111.onehot, ...), custom_call_target="tpu_custom_call" | custom-call | flops 1 | bytes 1 | tf_op jit(solution)/shard_map/pallas_call | solution.py:24
  111.9 0.8 shard_map.125
  (7 shorter events, 0.0 us)
Async XLA Ops:
  0.6 9.6 %copy-start.1 = (f32[4,512]{1,0:T(4,128)S(1)}, f32[4,512]{1,0:T(4,128)}, u32[]{:S(2)}) copy-start(f32[4,512]{1,0:T(4,128)} %coupling.1) | copy-start | bytes 24580
  0.6 9.6 %copy-start.2 = (f32[4,16,512]{2,1,0:T(8,128)S(1)}, f32[4,16,512]{2,1,0:T(8,128)}, u32[]{:S(2)}) copy-start(f32[4,16,512]{2,1,0:T(8,128)} %conc.1) | copy-start | bytes 393220
  0.7 0.7 copy-start.3
  1.4 0.7 copy-start.6
  2.1 8.2 %copy-start.4 = (f32[16,33]{1,0:T(8,128)S(1)}, f32[16,33]{1,0:T(8,128)}, u32[]{:S(2)}) copy-start(f32[16,33]{1,0:T(8,128)} %taps.1) | copy-start | bytes 6340
  2.1 8.2 %copy-start.7 = (f32[4,16]{1,0:T(4,128)S(1)}, f32[4,16]{1,0:T(4,128)}, u32[]{:S(2)}) copy-start(f32[4,16]{1,0:T(4,128)} %inlet.1) | copy-start | bytes 772
  2.1 8.2 %copy-start.8 = (f32[16]{0:T(128)S(1)}, f32[16]{0:T(128)}, u32[]{:S(2)}) copy-start(f32[16]{0:T(128)} %param.11) | copy-start | bytes 196
  2.1 14.7 %copy-start = (f32[16,2048]{1,0:T(8,128)S(1)}, f32[16,2048]{1,0:T(8,128)}, u32[]{:S(2)}) copy-start(f32[16,2048]{1,0:T(8,128)} %grid.3) | copy-start | bytes 393220
  2.1 14.6 %copy-start.5 = (f32[2048]{0:T(1024)S(1)}, f32[2048]{0:T(1024)}, u32[]{:S(2)}) copy-start(f32[2048]{0:T(1024)} %param.15) | copy-start | bytes 24580
  2.9 13.9 %all-to-all-start = ((s32[16,2,128]{2,1,0:T(2,128)}), s32[16,2,128]{2,1,0:T(2,128)S(1)}, u32[]{:S(2)}, u32[]{:S(2)}) async-start(s32[16,2,128]{2,1,0:T(2,128)} %get-tuple-element.36), calls=%async_computation | async-start | bytes 32768 | tf_op jit(solution)/shard_map/all_to_all | solution.py:459
  12.0 3.8 %collective-permute-start = (f32[2,16,128]{2,1,0:T(8,128)S(1)}, f32[2,16,128]{2,1,0:T(8,128)S(1)}, u32[]{:S(2)}, u32[]{:S(2)}) collective-permute-start(f32[2,16,128]{2,1,0:T(8,128)S(1)} %get-tuple-element.34.end_offset.end_factor), channel_id=1, source_target_pairs={{0,16},{16,0},{1,17},{17,1},{2,18},{18,2},{3,19},{19,3},{4,20},{20... | collective-permute-start | bytes 49160 | tf_op jit(solution)/shard_map/ppermute | solution.py:454
  41.6 4.4 %collective-permute-start.1 = (f32[1,16,128]{2,1,0:T(8,128)S(1)}, f32[1,16,128]{2,1,0:T(8,128)S(1)}, u32[]{:S(2)}, u32[]{:S(2)}) collective-permute-start(f32[1,16,128]{2,1,0:T(8,128)S(1)} %get-tuple-element.41.order.end_offset), channel_id=1, source_target_pairs={{0,16},{16,0},{1,17},{17,1},{2,18},{18,2},{3,19},{19,3},{4,20},{20... | collective-permute-start | bytes 24584 | tf_op jit(solution)/shard_map/ppermute | solution.py:454
  64.6 3.7 %collective-permute-start.2 = (f32[1,16,128]{2,1,0:T(8,128)S(1)}, f32[1,16,128]{2,1,0:T(8,128)S(1)}, u32[]{:S(2)}, u32[]{:S(2)}) collective-permute-start(f32[1,16,128]{2,1,0:T(8,128)S(1)} %get-tuple-element.47.end_offset), channel_id=1, source_target_pairs={{0,16},{16,0},{1,17},{17,1},{2,18},{18,2},{3,19},{19,3},{4,20},{20... | collective-permute-start | bytes 24584 | tf_op jit(solution)/shard_map/ppermute | solution.py:454
  87.9 3.7 %collective-permute-start.3 = (f32[1,16,128]{2,1,0:T(8,128)S(1)}, f32[1,16,128]{2,1,0:T(8,128)S(1)}, u32[]{:S(2)}, u32[]{:S(2)}) collective-permute-start(f32[1,16,128]{2,1,0:T(8,128)S(1)} %get-tuple-element.51.end_offset), channel_id=1, source_target_pairs={{0,16},{16,0},{1,17},{17,1},{2,18},{18,2},{3,19},{19,3},{4,20},{20... | collective-permute-start | bytes 24584 | tf_op jit(solution)/shard_map/ppermute | solution.py:454

commit v5 on v4

--- a/solution.py
+++ b/solution.py
@@ -19,7 +19,7 @@
 ANY = pl.BlockSpec(memory_space=pl.ANY)
 
 
-def call(kernel, outs, ins, out_specs=None, scratch=(), flops=1):
+def call(kernel, outs, ins, out_specs=None, scratch=(), flops=1, grant=40):
     args = [a for a, _ in ins]
     return pl.pallas_call(
         kernel,
@@ -28,7 +28,7 @@
         out_specs=out_specs or [VMEM] * len(outs),
         scratch_shapes=list(scratch),
         cost_estimate=pl.CostEstimate(flops=int(flops), bytes_accessed=1, transcendentals=0),
-        compiler_params=pltpu.CompilerParams(vmem_limit_bytes=40 * 1024 * 1024),
+        compiler_params=pltpu.CompilerParams(vmem_limit_bytes=grant * 1024 * 1024),
     )(*args)
 
 
@@ -36,18 +36,31 @@
     return jax.ShapeDtypeStruct(shape, dtype)
 
 
-def route_kernel(groups, cap, owners, cells, slot, send, count):
-    blocks = slot.shape[0]
-    owners_total = send.shape[0]
-    send[...] = jnp.full(send.shape, -1, jnp.int32)
+def slots(owners, count, owners_total, lines, groups):
     for o in range(owners_total):
         count[o] = 0
-    for b in range(blocks):
+    out = []
+    for line in range(lines):
+        for group in range(groups):
+            owner = owners[0, line, 0, group]
+            rank = count[owner]
+            count[owner] = rank + 1
+            out.append((owner, rank))
+    return out
+
+
+def route_kernel(groups, owners_in, cells_in, send, owners, cells, count, done):
+    copies = [
+        pltpu.make_async_copy(owners_in, owners, done.at[0]),
+        pltpu.make_async_copy(cells_in, cells, done.at[1]),
+    ]
+    for copy in copies:
+        copy.start()
+    send[...] = jnp.full(send.shape, -1, jnp.int32)
+    for copy in copies:
+        copy.wait()
+    for b, (owner, rank) in enumerate(slots(owners, count, send.shape[0], cells.shape[0], groups)):
         line, group = b // groups, b % groups
-        owner = owners[0, line, 0, group]
-        rank = count[owner]
-        count[owner] = rank + 1
-        slot[b : b + 1, :] = jnp.full((1, LANES), owner * cap + rank, jnp.int32)
         send[owner, pl.ds(rank, 1), :] = cells[
             pl.ds(line, 1), group * LANES : (group + 1) * LANES
         ]
@@ -84,25 +97,32 @@
 LEVELS = 7
 
 
-def scan_line(levels, retain, values, line, comps, groups):
-    offsets = []
-    for group in range(groups):
-        offset = (1.0 - tile(retain, line, comps, group)) * values[group]
-        for level in range(LEVELS):
-            offset = offset + level_rows(levels, level, line, comps, group) * pltpu.roll(
-                offset, 1 << level, 1
-            )
-        offsets.append(offset)
-    carry = last_lane(offsets[0])
-    done = [offsets[0]]
-    for group in range(1, groups):
-        done.append(offsets[group] + level_rows(levels, LEVELS, line, comps, group) * carry)
-        if group < groups - 1:
-            carry = (
-                last_lane(offsets[group])
-                + level_rows(levels, LEVELS + 1, line, comps, group) * carry
-            )
-    return done
+def scan_lines(levels, retain, values, lines, comps, groups):
+    blocks = [(line, group) for line in range(lines) for group in range(groups)]
+    offsets = [
+        (1.0 - tile(retain, line, comps, group)) * values[line * groups + group]
+        for line, group in blocks
+    ]
+    for level in range(LEVELS):
+        offsets = [
+            offset
+            + level_rows(levels, level, line, comps, group) * pltpu.roll(offset, 1 << level, 1)
+            for offset, (line, group) in zip(offsets, blocks)
+        ]
+    out = []
+    for line in range(lines):
+        own = offsets[line * groups : (line + 1) * groups]
+        carry = last_lane(own[0])
+        done = [own[0]]
+        for group in range(1, groups):
+            done.append(own[group] + level_rows(levels, LEVELS, line, comps, group) * carry)
+            if group < groups - 1:
+                carry = (
+                    last_lane(own[group])
+                    + level_rows(levels, LEVELS + 1, line, comps, group) * carry
+                )
+        out.append(done)
+    return out
 
 
 def tap_columns(wide_taps):
@@ -179,9 +199,11 @@
 
 
 def first_kernel(
-    lines, comps, groups, conc, slowness, retard, taps, inlet, order,
-    retain, levels, offset, factor, ends, wide_taps, wide_inlet,
+    lines, comps, groups, cap, owners_total, conc, slowness, retard, taps, inlet, owners,
+    retain, levels, offset, factor, ends, wide_taps, wide_inlet, slot, count,
 ):
+    for b, (owner, rank) in enumerate(slots(owners, count, owners_total, lines, groups)):
+        slot[b : b + 1, :] = jnp.full((1, LANES), owner * cap + rank, jnp.int32)
     lane = lax.broadcasted_iota(jnp.int32, (comps, LANES), 1)
     slow_by = column(retard[...], comps)
     packed = [jnp.zeros((comps, LANES), F32)] * 2
@@ -189,8 +211,9 @@
         wide_taps[t] = jnp.broadcast_to(taps[:, t : t + 1], (comps, LANES))
     for line in range(lines):
         wide_inlet[pl.ds(line * comps, comps), :] = column(inlet[line : line + 1, :], comps)
+    values, wholes = [], []
     for line in range(lines):
-        values, whole = [], []
+        whole = []
         for group in range(groups):
             s = slowness[pl.ds(line, 1), group * LANES : (group + 1) * LANES]
             r = 1.0 / (1.0 + slow_by * s)
@@ -213,7 +236,9 @@
             put(factor, line, comps, group, f)
             whole.append(f)
             values.append(conc[line, :, span])
-        offsets = scan_line(levels, retain, values, line, comps, groups)
+        wholes.append(whole)
+    for line, offsets in enumerate(scan_lines(levels, retain, values, lines, comps, groups)):
+        whole = wholes[line]
         for group in range(groups):
             put(offset, line, comps, group, offsets[group])
         part, inside = pack_ends(line, lane, offsets[0], offsets[-1])
@@ -293,36 +318,27 @@
         place(send, slot, b, cap, comps, tile(spread, b // groups, comps, b % groups))
 
 
-def conc_kernel(lines, comps, groups, cap, first, last, spread, got, coupling, retain, levels, slot, *outs):
+def conc_kernel(lines, comps, groups, cap, first, spread, got, coupling, retain, levels, slot, *outs):
     lane = lax.broadcasted_iota(jnp.int32, (comps, LANES), 1)
-    outs = list(outs)
-    coupling_out = outs.pop() if first else None
+    values = []
+    for b in range(lines * groups):
+        line, group = b // groups, b % groups
+        owner, rank = where_slot(slot, b, cap)
+        looked = got[owner, pl.ds(pl.multiple_of(rank * comps, 8), comps), :]
+        if first:
+            rate = got[owner, pl.ds(2 * cap * comps + rank, 1), :]
+            outs[2][b : b + 1, :] = rate
+        else:
+            rate = coupling[b : b + 1, :]
+        s = tile(spread, line, comps, group)
+        values.append(s + rate * (looked - s))
     packed = jnp.zeros((comps, LANES), F32)
-    for line in range(lines):
-        values = []
-        for group in range(groups):
-            b = line * groups + group
-            owner, rank = where_slot(slot, b, cap)
-            looked = got[owner, pl.ds(pl.multiple_of(rank * comps, 8), comps), :]
-            if first:
-                rate = got[owner, pl.ds(2 * cap * comps + rank, 1), :]
-                coupling_out[pl.ds(b, 1), :] = rate
-            else:
-                rate = coupling[pl.ds(b, 1), :]
-            s = tile(spread, line, comps, group)
-            value = s + rate * (looked - s)
-            if last:
-                outs[0][line, :, group * LANES : (group + 1) * LANES] = value
-            values.append(value)
-        if last:
-            continue
-        offsets = scan_line(levels, retain, values, line, comps, groups)
+    for line, offsets in enumerate(scan_lines(levels, retain, values, lines, comps, groups)):
         for group in range(groups):
             put(outs[0], line, comps, group, offsets[group])
         part, inside = pack_ends(line, lane, offsets[0], offsets[-1])
         packed = jnp.where(inside, part, packed)
-    if not last:
-        outs[1][0] = packed
+    outs[1][0] = packed
 
 
 def gather_cells(grid, cell, comps, high_total):
@@ -337,43 +353,86 @@
     return out
 
 
-def look_first_kernel(groups, cap, cells, grid, kappa, spread, slot, rates, send):
+def look_by_matmul(cells, cap, onehot, stack, first, count, high_total, wide):
+    rows = stack.shape[0] // 2
+    comps = rows // high_total
+    bits = wide.bit_length() - 1
+    part = jnp.dot(
+        stack[...], onehot[:, first * LANES : (first + count) * LANES], preferred_element_type=F32
+    )
+    out = []
+    for i in range(count):
+        owner, rank = (first + i) // cap, (first + i) % cap
+        cell = jnp.maximum(cells[owner, rank : rank + 1, :], 0)
+        high = jnp.broadcast_to(cell >> bits, (comps, LANES))
+        span = slice(i * LANES, (i + 1) * LANES)
+        found = jnp.zeros((comps, LANES), F32)
+        for h in range(high_total):
+            at = slice(h * comps, (h + 1) * comps)
+            at2 = slice(rows + h * comps, rows + (h + 1) * comps)
+            found = jnp.where(high == h, part[at, span] + part[at2, span], found)
+        out.append(found)
+    return out
+
+
+def in_two(x):
+    coarse = x.astype(BF16)
+    return coarse, (x - coarse.astype(F32)).astype(BF16)
+
+
+def stack_grid(grid, stack, wide):
     comps = grid.shape[0]
+    rows = stack.shape[0] // 2
+    for h in range(grid.shape[1] // wide):
+        coarse, fine = in_two(grid[:, h * wide : (h + 1) * wide])
+        stack[h * comps : (h + 1) * comps, :] = coarse
+        stack[rows + h * comps : rows + (h + 1) * comps, :] = fine
+
+
+def put_onehot(onehot, at, cell):
+    wide = onehot.shape[0]
+    row = lax.broadcasted_iota(jnp.int32, (wide, LANES), 0)
+    onehot[:, at : at + LANES] = jnp.where(row == (cell & (wide - 1)), 1.0, 0.0).astype(BF16)
+
+
+def look_first_kernel(groups, cap, cells, grid, kappa, spread, slot, rates, send, onehot, stack):
+    comps = grid.shape[0]
+    wide = onehot.shape[0]
     high_total = grid.shape[1] // LANES
+    by_matmul = onehot.shape[1] // LANES
     row = lax.broadcasted_iota(jnp.int32, (high_total, LANES), 0)
-
-    for owner in range(cells.shape[0]):
-        for rank in range(cap):
-            cell = cells[owner, rank : rank + 1, :]
-            valid = cell >= 0
-            cell = jnp.maximum(cell, 0)
+    stack_grid(grid, stack, wide)
+    for s in range(by_matmul):
+        put_onehot(onehot, s * LANES, cells[s // cap, s % cap : s % cap + 1, :])
+    for s in range(cells.shape[0] * cap):
+        owner, rank = s // cap, s % cap
+        cell = cells[owner, rank : rank + 1, :]
+        valid = cell >= 0
+        cell = jnp.maximum(cell, 0)
+        if s >= by_matmul:
             send[owner, rank * comps : (rank + 1) * comps, :] = gather_cells(
                 grid, cell, comps, high_total
             )
-            low = jnp.broadcast_to(cell & (LANES - 1), (high_total, LANES))
-            k = jnp.take_along_axis(kappa[...], low, axis=1, mode="promise_in_bounds")
-            rate = jnp.sum(jnp.where(row == (cell >> 7), k, 0.0), axis=0, keepdims=True)
-            rate = jnp.where(valid, rate, 0.0)
-            rates[owner, rank : rank + 1, :] = rate
-            at = 2 * cap * comps + rank
-            send[owner, at : at + 1, :] = rate
+        low = jnp.broadcast_to(cell & (LANES - 1), (high_total, LANES))
+        k = jnp.take_along_axis(kappa[...], low, axis=1, mode="promise_in_bounds")
+        rate = jnp.sum(jnp.where(row == (cell >> 7), k, 0.0), axis=0, keepdims=True)
+        rate = jnp.where(valid, rate, 0.0)
+        rates[owner, rank : rank + 1, :] = rate
+        at = 2 * cap * comps + rank
+        send[owner, at : at + 1, :] = rate
+    for first in range(0, by_matmul, 4):
+        found = look_by_matmul(cells, cap, onehot, stack, first, 4, grid.shape[1] // wide, wide)
+        for i in range(4):
+            owner, rank = (first + i) // cap, (first + i) % cap
+            send[owner, rank * comps : (rank + 1) * comps, :] = found[i]
     for b in range(slot.shape[0]):
         place(send, slot, b, cap, comps, tile(spread, b // groups, comps, b % groups))
 
 
 def onehot_kernel(cap, cells, order, onehot):
-    wide = onehot.shape[0]
-    row = lax.broadcasted_iota(jnp.int32, (wide, LANES), 0)
     for owner in range(cells.shape[0]):
         for rank in range(cap):
-            cell = cells[owner, rank : rank + 1, :]
-            at = (owner * cap + rank) * LANES
-            onehot[:, at : at + LANES] = jnp.where(row == (cell & (wide - 1)), 1.0, 0.0).astype(BF16)
-
-
-def in_two(x):
-    coarse = x.astype(BF16)
-    return coarse, (x - coarse.astype(F32)).astype(BF16)
+            put_onehot(onehot, (owner * cap + rank) * LANES, cells[owner, rank : rank + 1, :])
 
 
 def update_kernel(cap, chunk, cells, got, looked, rates, onehot, grid, grid_out, masked):
@@ -424,29 +483,33 @@
 def look_kernel(cap, cells, onehot, grid, looked, stack):
     comps = grid.shape[0]
     wide = onehot.shape[0]
-    bits = wide.bit_length() - 1
-    high_total = grid.shape[1] // wide
-    owners_total = cells.shape[0]
-    rows = high_total * comps
-    for h in range(high_total):
-        coarse, fine = in_two(grid[:, h * wide : (h + 1) * wide])
-        stack[h * comps : (h + 1) * comps, :] = coarse
-        stack[rows + h * comps : rows + (h + 1) * comps, :] = fine
-    for first in range(0, owners_total * cap, 4):
-        part = jnp.dot(
-            stack[...], onehot[:, first * LANES : (first + 4) * LANES], preferred_element_type=F32
-        )
+    stack_grid(grid, stack, wide)
+    for first in range(0, cells.shape[0] * cap, 4):
+        found = look_by_matmul(cells, cap, onehot, stack, first, 4, grid.shape[1] // wide, wide)
         for i in range(4):
             owner, rank = (first + i) // cap, (first + i) % cap
-            cell = jnp.maximum(cells[owner, rank : rank + 1, :], 0)
-            high = jnp.broadcast_to(cell >> bits, (comps, LANES))
-            span = slice(i * LANES, (i + 1) * LANES)
-            found = jnp.zeros((comps, LANES), F32)
-            for h in range(high_total):
-                at = slice(h * comps, (h + 1) * comps)
-                at2 = slice(rows + h * comps, rows + (h + 1) * comps)
-                found = jnp.where(high == h, part[at, span] + part[at2, span], found)
-            looked[owner, rank * comps : (rank + 1) * comps, :] = found
+            looked[owner, rank * comps : (rank + 1) * comps, :] = found[i]
+
+
+def last_kernel(
+    lines, comps, groups, cap, chunk,
+    spread, came, coupling, slot, cells, looked, rates, onehot, grid,
+    conc_out, grid_out, conc, grid_new, masked, done,
+):
+    for b in range(lines * groups):
+        line, group = b // groups, b % groups
+        owner, rank = where_slot(slot, b, cap)
+        found = came[owner, pl.ds(pl.multiple_of(rank * comps, 8), comps), :]
+        s = tile(spread, line, comps, group)
+        value = s + coupling[b : b + 1, :] * (found - s)
+        conc[line, :, group * LANES : (group + 1) * LANES] = value
+    first = pltpu.make_async_copy(conc, conc_out, done.at[0])
+    first.start()
+    update_kernel(cap, chunk, cells, came, looked, rates, onehot, grid, grid_new, masked)
+    second = pltpu.make_async_copy(grid_new, grid_out, done.at[1])
+    second.start()
+    first.wait()
+    second.wait()
 
 
 def swap(x, segs):
@@ -471,27 +534,35 @@
     chunk = 4 if owners_total % 4 == 0 else owners_total
     half = cap * comps
     extra = 8 * (-(-cap // 8))
-
-    slot, cell_send = call(
-        functools.partial(route_kernel, groups, cap),
-        [sds((blocks, LANES), jnp.int32), sds((owners_total, cap, LANES), jnp.int32)],
-        [(jnp.swapaxes(owners, 2, 3), VMEM), (cells, VMEM)],
-        scratch=[pltpu.SMEM((owners_total,), jnp.int32)],
+    wide = 256 if cell_count % 256 == 0 else LANES
+    matmul_slots = owners_total * cap // 8 * 4
+
+    owners = jnp.swapaxes(owners, 2, 3)
+    (cell_send,) = call(
+        functools.partial(route_kernel, groups),
+        [sds((owners_total, cap, LANES), jnp.int32)],
+        [(owners, ANY), (cells, ANY)],
+        scratch=[
+            pltpu.VMEM((1, lines, 1, groups), jnp.int32), pltpu.VMEM((lines, nodes), jnp.int32),
+            pltpu.SMEM((owners_total,), jnp.int32), pltpu.SemaphoreType.DMA((2,)),
+        ],
+        grant=58,
         flops=1e9,
     )
     cell_recv = exchange(cell_send)
 
-    retain, levels, offset, factor, ends, taps, inlet = call(
-        functools.partial(first_kernel, lines, comps, groups),
+    retain, levels, offset, factor, ends, taps, inlet, slot = call(
+        functools.partial(first_kernel, lines, comps, groups, cap, owners_total),
         [
             sds((rows, nodes)), sds((LEVELS + 2, rows, nodes)), sds((rows, nodes)),
             sds((rows, nodes)), sds((2, comps, LANES)), sds((taps.shape[1], comps, LANES)),
-            sds((rows, LANES)),
+            sds((rows, LANES)), sds((blocks, LANES), jnp.int32),
         ],
         [
             (conc, VMEM), (slowness, VMEM), (retard.reshape(1, comps), VMEM), (taps, VMEM),
-            (inlet, VMEM), (slot, ANY),
+            (inlet, VMEM), (owners, VMEM),
         ],
+        scratch=[pltpu.SMEM((owners_total,), jnp.int32)],
         flops=1e8,
     )
     first_ends = ends
@@ -532,19 +603,44 @@
             (cell_recv, VMEM), (grid, VMEM), (kappa.reshape(cell_count // LANES, LANES), VMEM),
             (spread, VMEM), (slot, VMEM),
         ],
+        scratch=[
+            pltpu.VMEM((wide, matmul_slots * LANES), BF16),
+            pltpu.VMEM((2 * (cell_count // wide) * comps, wide), BF16),
+        ],
         flops=1e8,
     )
     looked = send
-    wide = 256 if cell_count % 256 == 0 else LANES
     coupling = slowness
     for step in range(STEPS):
         last = step == STEPS - 1
         got = exchange(send)
-        outs = [sds(conc.shape)] if last else [sds((rows, nodes)), sds((1, comps, LANES))]
+        masks = pltpu.VMEM(
+            (
+                min(4, owners_total // chunk), 2 * (cell_count // wide) * comps,
+                chunk * cap * LANES,
+            ),
+            BF16,
+        )
+        if last:
+            conc_out, grid = call(
+                functools.partial(last_kernel, lines, comps, groups, cap, chunk),
+                [sds(conc.shape), sds(grid.shape)],
+                [
+                    (spread, VMEM), (got, VMEM), (coupling, VMEM), (slot, VMEM),
+                    (cell_recv, VMEM), (looked, VMEM), (rates, VMEM), (onehot, VMEM), (grid, VMEM),
+                ],
+                out_specs=[ANY, ANY],
+                scratch=[
+                    pltpu.VMEM(conc.shape, F32), pltpu.VMEM(grid.shape, F32), masks,
+                    pltpu.SemaphoreType.DMA((2,)),
+                ],
+            )
+            break
+        outs = [sds((rows, nodes)), sds((1, comps, LANES))]
         if step == 0:
             outs.append(sds((blocks, LANES)))
         result = call(
-            functools.partial(conc_kernel, lines, comps, groups, cap, step == 0, last),
+            functools.partial(conc_kernel, lines, comps, groups, cap, step == 0),
             outs,
             [
                 (spread, VMEM), (got, VMEM), (coupling, VMEM), (retain, VMEM), (levels, VMEM),
@@ -553,12 +649,9 @@
         )
         if step == 0:
             coupling = result[-1]
-        if last:
-            conc_out = result[0]
-        else:
-            offset, ends = result[0], result[1]
-            got_ends = swap(ends, segs)
-            other_offset = got_ends if segs == 2 else got_ends[:, 0]
+        offset, ends = result[0], result[1]
+        got_ends = swap(ends, segs)
+        other_offset = got_ends if segs == 2 else got_ends[:, 0]
         if step == 0:
             (onehot,) = call(
                 functools.partial(onehot_kernel, cap),
@@ -572,30 +665,20 @@
                 (cell_recv, VMEM), (got, VMEM), (looked, VMEM), (rates, VMEM), (onehot, VMEM),
                 (grid, VMEM),
             ],
-            scratch=[
-                pltpu.VMEM(
-                    (
-                        min(4, owners_total // chunk),
-                        2 * (cell_count // wide) * comps,
-                        chunk * cap * LANES,
-                    ),
-                    BF16,
-                )
-            ],
+            scratch=[masks],
         )
-        if not last:
-            (looked,) = call(
-                functools.partial(look_kernel, cap),
-                [sds((owners_total, half, LANES))],
-                [(cell_recv, VMEM), (onehot, VMEM), (grid, VMEM)],
-                scratch=[pltpu.VMEM((2 * (cell_count // wide) * comps, wide), BF16)],
-            )
-            (local,) = call(
-                functools.partial(taps_kernel, lines, comps, groups, 1),
-                [sds((rows, nodes))],
-                [(taps, VMEM), (offset, VMEM)],
-            )
-            spread, send = finish(looked)
+        (looked,) = call(
+            functools.partial(look_kernel, cap),
+            [sds((owners_total, half, LANES))],
+            [(cell_recv, VMEM), (onehot, VMEM), (grid, VMEM)],
+            scratch=[pltpu.VMEM((2 * (cell_count // wide) * comps, wide), BF16)],
+        )
+        (local,) = call(
+            functools.partial(taps_kernel, lines, comps, groups, 1),
+            [sds((rows, nodes))],
+            [(taps, VMEM), (offset, VMEM)],
+        )
+        spread, send = finish(looked)
     return (conc_out, grid)
 
 

time: 113 us -> 112 us (level)
  local copies, waits for them, and re-layouts: 1.43 us -> 0.03 us
    unnamed x18 -> x16, local copies, waits for them, and re-layouts: 1.43 us -> 0.03 us
    pallas_call x23 -> x22, Pallas kernels: 19.2 us -> 19.8 us  [call(): pl.pallas_call(kernel, out_shape=outs, in_specs=[s for _, s in ins], out_...]
  transfers between devices with their start and end apart: 5 -> 5, of which waited for: 4 -> 3; matrix products, arithmetic and copies ran while one was open for 0% -> 0% of each run, Pallas kernels for 10% -> 10%
where the time goes in v5:
time: 112 us
  blocking collectives  77.1 us (69%)
  Pallas kernels  19.8 us (18%)
  starting transfers between devices  12.1 us (11%)
  waiting for transfers between devices  2.02 us (2%)
    all_to_all x4, blocking collectives, exchange(): return lax.all_to_all(x, 'bundle', split_axis=0, concat_axis=0, tiled=True)  77.1 us
    pallas_call x22, Pallas kernels, call(): pl.pallas_call(kernel, out_shape=outs, in_specs=[s for _, s in ins], out_...  19.8 us
    all_to_all x1, starting transfers between devices, exchange(): return lax.all_to_all(x, 'bundle', split_axis=0, concat_axis=0, tiled=True)  7.37 us
    ppermute x4, starting transfers between devices, swap(): return lax.ppermute(x, 'seg', [(0, 1), (1, 0)])  4.7 us
  transfers between devices with their start and end apart: 5, of which 3 were waited for; matrix products, arithmetic and copies ran while one was open for 0% of the time, Pallas kernels for 10%

profile of v5, /device:TPU:0, one launch (start us, length us, event | category | flops | bytes accessed | tf_op | source)
XLA Modules:
  0.0 112.0 jit_solution(11255143280475034809)
XLA Ops:
  0.6 0.0 copy-start.6
  0.6 0.0 copy-start.1
  0.7 0.0 copy-start.5
  0.7 0.0 copy-start.3
  0.7 0.0 copy-start.7
  0.7 0.0 copy-start.2
  0.7 0.0 copy-start
  0.7 0.0 copy-start.4
  0.7 1.6 %shard_map.107 = s32[16,2,128]{2,1,0:T(2,128)} custom-call(s32[1,4,1,4]{3,2,1,0:T(1,128)} %bitcast.6, s32[4,512]{1,0:T(4,128)} %cells_in.1), custom_call_target="tpu_custom_call" | custom-call | flops 1000000000 | bytes 1 | tf_op jit(solution)/shard_map/pallas_call | solution.py:24
  2.3 7.4 %all-to-all-start = ((s32[16,2,128]{2,1,0:T(2,128)}), s32[16,2,128]{2,1,0:T(2,128)S(1)}, u32[]{:S(2)}, u32[]{:S(2)}) async-start(s32[16,2,128]{2,1,0:T(2,128)} %shard_map.107), calls=%async_computation | async-start | bytes 32768 | tf_op jit(solution)/shard_map/all_to_all | solution.py:522
  9.7 0.0 copy-done.6
  9.7 0.0 copy-done.1
  9.7 0.0 copy-done.5
  9.7 0.0 copy-done.3
  9.7 2.5 %shard_map.104 = (f32[64,512]{1,0:T(8,128)S(1)}, f32[9,64,512]{2,1,0:T(8,128)S(1)}, f32[64,512]{1,0:T(8,128)S(1)}, f32[64,512]{1,0:T(8,128)S(1)}, f32[2,16,128]{...) custom-call(f32[4,16,512]{2,1,0:T(8,128)S(1)} %copy-done.2, ...), custom_call_target="tpu_custom_call" | custom-call | flops 100000000 | bytes 1 | tf_op jit(solution)/shard_map/pallas_call | solution.py:24
  12.2 1.6 %collective-permute-start = (f32[2,16,128]{2,1,0:T(8,128)S(1)}, f32[2,16,128]{2,1,0:T(8,128)S(1)}, u32[]{:S(2)}, u32[]{:S(2)}) collective-permute-start(f32[2,16,128]{2,1,0:T(8,128)S(1)} %get-tuple-element.32.end_offset.end_factor), channel_id=1, source_target_pairs={{0,16},{16,0},{1,17},{17,1},{2,18},{18,2},{3,19},{19,3},{4,20},{20... | collective-permute-start | bytes 49160 | tf_op jit(solution)/shard_map/ppermute | solution.py:517
  13.8 1.4 %shard_map.105 = (f32[64,512]{1,0:T(8,128)S(1)}, f32[64,512]{1,0:T(8,128)S(1)}) custom-call(f32[33,16,128]{2,1,0:T(8,128)S(1)} %get-tuple-element.27.taps, f32[64,512]{1,0:T(8,128)S(1)} %get-tuple-element.28.refs_0_, f32[64,512]{1,0:T(8,128)S(1)} %get-tuple-element.29.refs_1_), custom_call_target="tpu_custom_call" | custom-call | flops 100000000 | bytes 1 | tf_op jit(solution)/shard_map/pallas_call | solution.py:24
  15.3 0.8 collective-permute-done.other_offset.other_factor
  16.0 0.5 shard_map.106.spread
  16.5 0.0 all-to-all-done.cells
  16.6 1.1 shard_map.108
  17.7 23.1 %all_to_all.25.got = f32[16,72,128]{2,1,0:T(8,128)S(1)} all-to-all(f32[16,72,128]{2,1,0:T(8,128)S(1)} %get-tuple-element.35.looked), channel_id=1, replica_groups=mesh['seg'=2,'bundle'=16] {'bundle'}, dimensions={0} | all-to-all | bytes 1179648 | tf_op jit(solution)/shard_map/all_to_all | solution.py:522
  40.8 0.8 shard_map.109
  41.5 1.6 %collective-permute-start.1 = (f32[1,16,128]{2,1,0:T(8,128)S(1)}, f32[1,16,128]{2,1,0:T(8,128)S(1)}, u32[]{:S(2)}, u32[]{:S(2)}) collective-permute-start(f32[1,16,128]{2,1,0:T(8,128)S(1)} %get-tuple-element.39.order.end_offset), channel_id=1, source_target_pairs={{0,16},{16,0},{1,17},{17,1},{2,18},{18,2},{3,19},{19,3},{4,20},{20... | collective-permute-start | bytes 24584 | tf_op jit(solution)/shard_map/ppermute | solution.py:517
  43.1 0.6 shard_map.111.onehot
  43.7 0.8 shard_map.112.grid
  44.5 0.7 shard_map.110.local
  45.2 0.7 shard_map.113.rest_1_.looked
  45.9 0.0 collective-permute-done.1.other_offset
  46.0 0.5 shard_map.114
  46.5 17.3 %all_to_all.26.got = f32[16,64,128]{2,1,0:T(8,128)S(1)} all-to-all(f32[16,64,128]{2,1,0:T(8,128)S(1)} %get-tuple-element.42), channel_id=1, replica_groups=mesh['seg'=2,'bundle'=16] {'bundle'}, dimensions={0} | all-to-all | bytes 1048576 | tf_op jit(solution)/shard_map/all_to_all | solution.py:522
  63.7 0.8 shard_map.115
  64.5 0.8 collective-permute-start.2
  65.3 0.8 shard_map.117.grid
  66.1 0.7 shard_map.116.local
  66.8 0.7 shard_map.118.rest_1_.looked
  67.5 0.6 collective-permute-done.2.other_offset
  68.2 0.5 shard_map.119
  68.7 18.4 %all_to_all.27.got = f32[16,64,128]{2,1,0:T(8,128)S(1)} all-to-all(f32[16,64,128]{2,1,0:T(8,128)S(1)} %get-tuple-element.47), channel_id=1, replica_groups=mesh['seg'=2,'bundle'=16] {'bundle'}, dimensions={0} | all-to-all | bytes 1048576 | tf_op jit(solution)/shard_map/all_to_all | solution.py:522
  87.0 0.8 shard_map.120
  87.8 0.8 collective-permute-start.3
  88.6 0.8 shard_map.122.grid
  89.4 0.7 shard_map.121.local
  90.1 0.7 shard_map.123.rest_1_.looked
  90.8 0.6 collective-permute-done.3.other_offset
  91.5 0.5 shard_map.124
  92.0 18.4 %all_to_all.28.came = f32[16,64,128]{2,1,0:T(8,128)S(1)} all-to-all(f32[16,64,128]{2,1,0:T(8,128)S(1)} %get-tuple-element.51), channel_id=1, replica_groups=mesh['seg'=2,'bundle'=16] {'bundle'}, dimensions={0} | all-to-all | bytes 1048576 | tf_op jit(solution)/shard_map/all_to_all | solution.py:522
  110.3 1.5 %shard_map.125 = (f32[4,16,512]{2,1,0:T(8,128)}, f32[16,2048]{1,0:T(8,128)}) custom-call(f32[64,512]{1,0:T(8,128)S(1)} %get-tuple-element.50.spread, f32[16,64,128]{2,1,0:T(8,128)S(1)} %all_to_all.28.came, f32[16,128]{1,0:T(8,128)S(1)} %get-tuple-element.43.coupling, s32[16,128]{1,0:T(8,128)S(1)} %get-tuple-element.34.slot.rest_0_, ...), custom_call_target="tpu_custom_call" | custom-call | flops 1 | bytes 1 | tf_op jit(solution)/shard_map/pallas_call | solution.py:24
  (4 shorter events, 0.0 us)
Async XLA Ops:
  0.6 9.0 %copy-start.6 = (s32[1,4,4,1]{2,3,1,0:T(1,128)S(1)}, s32[1,4,4,1]{2,3,1,0:T(1,128)}, u32[]{:S(2)}) copy-start(s32[1,4,4,1]{2,3,1,0:T(1,128)} %param.16) | copy-start | bytes 196
  0.6 9.0 %copy-start.1 = (f32[4,512]{1,0:T(4,128)S(1)}, f32[4,512]{1,0:T(4,128)}, u32[]{:S(2)}) copy-start(f32[4,512]{1,0:T(4,128)} %coupling.1) | copy-start | bytes 24580
  0.7 9.0 %copy-start.5 = (f32[4,16]{1,0:T(4,128)S(1)}, f32[4,16]{1,0:T(4,128)}, u32[]{:S(2)}) copy-start(f32[4,16]{1,0:T(4,128)} %inlet.1) | copy-start | bytes 772
  0.7 9.0 %copy-start.3 = (f32[16,33]{1,0:T(8,128)S(1)}, f32[16,33]{1,0:T(8,128)}, u32[]{:S(2)}) copy-start(f32[16,33]{1,0:T(8,128)} %taps.1) | copy-start | bytes 6340
  0.7 9.0 %copy-start.7 = (f32[16]{0:T(128)S(1)}, f32[16]{0:T(128)}, u32[]{:S(2)}) copy-start(f32[16]{0:T(128)} %param.11) | copy-start | bytes 196
  0.7 9.0 %copy-start.2 = (f32[4,16,512]{2,1,0:T(8,128)S(1)}, f32[4,16,512]{2,1,0:T(8,128)}, u32[]{:S(2)}) copy-start(f32[4,16,512]{2,1,0:T(8,128)} %conc.1) | copy-start | bytes 393220
  0.7 15.9 %copy-start = (f32[16,2048]{1,0:T(8,128)S(1)}, f32[16,2048]{1,0:T(8,128)}, u32[]{:S(2)}) copy-start(f32[16,2048]{1,0:T(8,128)} %grid.3) | copy-start | bytes 393220
  0.7 15.9 %copy-start.4 = (f32[2048]{0:T(1024)S(1)}, f32[2048]{0:T(1024)}, u32[]{:S(2)}) copy-start(f32[2048]{0:T(1024)} %param.15) | copy-start | bytes 24580
  2.3 14.3 %all-to-all-start = ((s32[16,2,128]{2,1,0:T(2,128)}), s32[16,2,128]{2,1,0:T(2,128)S(1)}, u32[]{:S(2)}, u32[]{:S(2)}) async-start(s32[16,2,128]{2,1,0:T(2,128)} %shard_map.107), calls=%async_computation | async-start | bytes 32768 | tf_op jit(solution)/shard_map/all_to_all | solution.py:522
  12.2 3.8 %collective-permute-start = (f32[2,16,128]{2,1,0:T(8,128)S(1)}, f32[2,16,128]{2,1,0:T(8,128)S(1)}, u32[]{:S(2)}, u32[]{:S(2)}) collective-permute-start(f32[2,16,128]{2,1,0:T(8,128)S(1)} %get-tuple-element.32.end_offset.end_factor), channel_id=1, source_target_pairs={{0,16},{16,0},{1,17},{17,1},{2,18},{18,2},{3,19},{19,3},{4,20},{20... | collective-permute-start | bytes 49160 | tf_op jit(solution)/shard_map/ppermute | solution.py:517
  41.5 4.4 %collective-permute-start.1 = (f32[1,16,128]{2,1,0:T(8,128)S(1)}, f32[1,16,128]{2,1,0:T(8,128)S(1)}, u32[]{:S(2)}, u32[]{:S(2)}) collective-permute-start(f32[1,16,128]{2,1,0:T(8,128)S(1)} %get-tuple-element.39.order.end_offset), channel_id=1, source_target_pairs={{0,16},{16,0},{1,17},{17,1},{2,18},{18,2},{3,19},{19,3},{4,20},{20... | collective-permute-start | bytes 24584 | tf_op jit(solution)/shard_map/ppermute | solution.py:517
  64.5 3.7 %collective-permute-start.2 = (f32[1,16,128]{2,1,0:T(8,128)S(1)}, f32[1,16,128]{2,1,0:T(8,128)S(1)}, u32[]{:S(2)}, u32[]{:S(2)}) collective-permute-start(f32[1,16,128]{2,1,0:T(8,128)S(1)} %get-tuple-element.45.end_offset), channel_id=1, source_target_pairs={{0,16},{16,0},{1,17},{17,1},{2,18},{18,2},{3,19},{19,3},{4,20},{20... | collective-permute-start | bytes 24584 | tf_op jit(solution)/shard_map/ppermute | solution.py:517
  87.8 3.7 %collective-permute-start.3 = (f32[1,16,128]{2,1,0:T(8,128)S(1)}, f32[1,16,128]{2,1,0:T(8,128)S(1)}, u32[]{:S(2)}, u32[]{:S(2)}) collective-permute-start(f32[1,16,128]{2,1,0:T(8,128)S(1)} %get-tuple-element.49.end_offset), channel_id=1, source_target_pairs={{0,16},{16,0},{1,17},{17,1},{2,18},{18,2},{3,19},{19,3},{4,20},{20... | collective-permute-start | bytes 24584 | tf_op jit(solution)/shard_map/ppermute | solution.py:517

commit v6 on v5

--- a/solution.py
+++ b/solution.py
@@ -199,18 +199,11 @@
 
 
 def first_kernel(
-    lines, comps, groups, cap, owners_total, conc, slowness, retard, taps, inlet, owners,
-    retain, levels, offset, factor, ends, wide_taps, wide_inlet, slot, count,
+    lines, comps, groups, conc, slowness, retard, retain, levels, offset, factor, ends
 ):
-    for b, (owner, rank) in enumerate(slots(owners, count, owners_total, lines, groups)):
-        slot[b : b + 1, :] = jnp.full((1, LANES), owner * cap + rank, jnp.int32)
     lane = lax.broadcasted_iota(jnp.int32, (comps, LANES), 1)
     slow_by = column(retard[...], comps)
     packed = [jnp.zeros((comps, LANES), F32)] * 2
-    for t in range(taps.shape[1]):
-        wide_taps[t] = jnp.broadcast_to(taps[:, t : t + 1], (comps, LANES))
-    for line in range(lines):
-        wide_inlet[pl.ds(line * comps, comps), :] = column(inlet[line : line + 1, :], comps)
     values, wholes = [], []
     for line in range(lines):
         whole = []
@@ -263,6 +256,25 @@
 def place(send, slot, b, cap, comps, value):
     owner, rank = where_slot(slot, b, cap)
     send[owner, pl.ds(pl.multiple_of((cap + rank) * comps, 8), comps), :] = value
+
+
+def first_taps_kernel(
+    lines, comps, groups, cap, taps, inlet, owners, offset, factor,
+    local, carried, wide_taps, wide_inlet, slot,
+):
+    for t in range(taps.shape[1]):
+        wide_taps[t] = jnp.broadcast_to(taps[:, t : t + 1], (comps, LANES))
+    for line in range(lines):
+        wide_inlet[pl.ds(line * comps, comps), :] = column(inlet[line : line + 1, :], comps)
+    blocks = lines * groups
+    square = (blocks, blocks)
+    row = jnp.concatenate([owners[0, line].astype(F32) for line in range(lines)], axis=1)
+    own = column(row, blocks)[:, :blocks]
+    earlier = lax.broadcasted_iota(jnp.int32, square, 1) < lax.broadcasted_iota(jnp.int32, square, 0)
+    same = jnp.where(earlier & (own == jnp.broadcast_to(row, square)), 1.0, 0.0)
+    at = own[:, :1] * cap + jnp.sum(same, axis=1, keepdims=True)
+    slot[...] = jnp.broadcast_to(at, (blocks, LANES)).astype(jnp.int32)
+    taps_kernel(lines, comps, groups, 2, wide_taps, offset, factor, local, carried)
 
 
 def finish_kernel(
@@ -551,18 +563,13 @@
     )
     cell_recv = exchange(cell_send)
 
-    retain, levels, offset, factor, ends, taps, inlet, slot = call(
-        functools.partial(first_kernel, lines, comps, groups, cap, owners_total),
+    retain, levels, offset, factor, ends = call(
+        functools.partial(first_kernel, lines, comps, groups),
         [
             sds((rows, nodes)), sds((LEVELS + 2, rows, nodes)), sds((rows, nodes)),
-            sds((rows, nodes)), sds((2, comps, LANES)), sds((taps.shape[1], comps, LANES)),
-            sds((rows, LANES)), sds((blocks, LANES), jnp.int32),
+            sds((rows, nodes)), sds((2, comps, LANES)),
         ],
-        [
-            (conc, VMEM), (slowness, VMEM), (retard.reshape(1, comps), VMEM), (taps, VMEM),
-            (inlet, VMEM), (owners, VMEM),
-        ],
-        scratch=[pltpu.SMEM((owners_total,), jnp.int32)],
+        [(conc, VMEM), (slowness, VMEM), (retard.reshape(1, comps), VMEM)],
         flops=1e8,
     )
     first_ends = ends
@@ -571,10 +578,13 @@
         other_offset = other_factor = other
     else:
         other_offset, other_factor = other[:, 0], other[:, 1]
-    local, carried = call(
-        functools.partial(taps_kernel, lines, comps, groups, 2),
-        [sds((rows, nodes))] * 2,
-        [(taps, VMEM), (offset, VMEM), (factor, VMEM)],
+    local, carried, taps, inlet, slot = call(
+        functools.partial(first_taps_kernel, lines, comps, groups, cap),
+        [
+            sds((rows, nodes)), sds((rows, nodes)), sds((taps.shape[1], comps, LANES)),
+            sds((rows, LANES)), sds((blocks, LANES), jnp.int32),
+        ],
+        [(taps, VMEM), (inlet, VMEM), (owners, VMEM), (offset, VMEM), (factor, VMEM)],
         flops=1e8,
     )
 

time: 112 us -> 111 us (level)
  Pallas kernels: 19.8 us -> 18.4 us
  blocking collectives: 77.1 us -> 75.8 us
    pallas_call x22, Pallas kernels: 19.8 us -> 18.4 us  [call(): pl.pallas_call(kernel, out_shape=outs, in_specs=[s for _, s in ins], out_...]
    all_to_all x1, waiting for transfers between devices: 0.01 us -> 1.31 us  [exchange(): return lax.all_to_all(x, 'bundle', split_axis=0, concat_axis=0, tiled=True)]
    all_to_all x4, blocking collectives: 77.1 us -> 75.8 us  [exchange(): return lax.all_to_all(x, 'bundle', split_axis=0, concat_axis=0, tiled=True)]
  transfers between devices with their start and end apart: 5 -> 5, of which waited for: 3 -> 4; matrix products, arithmetic and copies ran while one was open for 0% -> 0% of each run, Pallas kernels for 10% -> 9%
where the time goes in v6:
time: 111 us; the launch traced here: 110 us
  blocking collectives  75.8 us (68%)
  Pallas kernels  18.4 us (17%)
  starting transfers between devices  12.1 us (11%)
  waiting for transfers between devices  3.03 us (3%)
    all_to_all x4, blocking collectives, exchange(): return lax.all_to_all(x, 'bundle', split_axis=0, concat_axis=0, tiled=True)  75.8 us
    pallas_call x22, Pallas kernels, call(): pl.pallas_call(kernel, out_shape=outs, in_specs=[s for _, s in ins], out_...  18.4 us
    all_to_all x1, starting transfers between devices, exchange(): return lax.all_to_all(x, 'bundle', split_axis=0, concat_axis=0, tiled=True)  7.37 us
    ppermute x4, starting transfers between devices, swap(): return lax.ppermute(x, 'seg', [(0, 1), (1, 0)])  4.71 us
  transfers between devices with their start and end apart: 5, of which 4 were waited for; matrix products, arithmetic and copies ran while one was open for 0% of the time, Pallas kernels for 9%

profile of v6, /device:TPU:0, one launch (start us, length us, event | category | flops | bytes accessed | tf_op | source)
XLA Modules:
  0.0 110.3 jit_solution(8448393892859377370)
XLA Ops:
  0.6 0.0 copy-start.6
  0.6 0.0 copy-start.1
  0.7 0.0 copy-start.7
  0.7 0.0 copy-start.2
  0.7 0.0 copy-start.5
  0.7 0.0 copy-start.3
  0.7 0.0 copy-start
  0.7 0.0 copy-start.4
  0.7 1.5 %shard_map.107 = s32[16,2,128]{2,1,0:T(2,128)} custom-call(s32[1,4,1,4]{3,2,1,0:T(1,128)} %bitcast.6, s32[4,512]{1,0:T(4,128)} %cells_in.1), custom_call_target="tpu_custom_call" | custom-call | flops 1000000000 | bytes 1 | tf_op jit(solution)/shard_map/pallas_call | solution.py:24
  2.3 7.4 %all-to-all-start = ((s32[16,2,128]{2,1,0:T(2,128)}), s32[16,2,128]{2,1,0:T(2,128)S(1)}, u32[]{:S(2)}, u32[]{:S(2)}) async-start(s32[16,2,128]{2,1,0:T(2,128)} %shard_map.107), calls=%async_computation | async-start | bytes 32768 | tf_op jit(solution)/shard_map/all_to_all | solution.py:534
  9.6 0.0 copy-done.1
  9.6 0.0 copy-done.7
  9.7 0.0 copy-done.2
  9.7 0.8 shard_map.104
  10.5 1.6 %collective-permute-start = (f32[2,16,128]{2,1,0:T(8,128)S(1)}, f32[2,16,128]{2,1,0:T(8,128)S(1)}, u32[]{:S(2)}, u32[]{:S(2)}) collective-permute-start(f32[2,16,128]{2,1,0:T(8,128)S(1)} %get-tuple-element.32.end_offset.end_factor), channel_id=1, source_target_pairs={{0,16},{16,0},{1,17},{17,1},{2,18},{18,2},{3,19},{19,3},{4,20},{20... | collective-permute-start | bytes 49160 | tf_op jit(solution)/shard_map/ppermute | solution.py:529
  12.1 1.7 %shard_map.105 = (f32[64,512]{1,0:T(8,128)S(1)}, f32[64,512]{1,0:T(8,128)S(1)}, f32[33,16,128]{2,1,0:T(8,128)S(1)}, f32[64,128]{1,0:T(8,128)S(1)}, s32[16,128]{1,0:T(8,128)S(1)}) custom-call(f32[16,33]{1,0:T(8,128)S(1)} %copy-done.3, f32[4,16]{1,0:T(4,128)S(1)} %copy-done.5, s32[1,4,1,4]{3,2,1,0:T(1,128)S(1)} %bitcast.7, ...), custom_call_target="tpu_custom_call" | custom-call | flops 100000000 | bytes 1 | tf_op jit(solution)/shard_map/pallas_call | solution.py:24
  13.8 0.5 collective-permute-done.other_offset.other_factor
  14.3 0.5 shard_map.106.spread
  14.8 1.3 %all-to-all-done.cells = s32[16,2,128]{2,1,0:T(2,128)S(1)} async-done(((s32[16,2,128]{2,1,0:T(2,128)}), s32[16,2,128]{2,1,0:T(2,128)S(1)}, u32[]{:S(2)}, u32[]{:S(2)}) %all-to-all-start) | async-done | bytes 16416 | tf_op jit(solution)/shard_map/all_to_all | solution.py:534
  16.1 0.0 copy-done
  16.1 1.1 shard_map.108
  17.2 21.8 %all_to_all.25.got = f32[16,72,128]{2,1,0:T(8,128)S(1)} all-to-all(f32[16,72,128]{2,1,0:T(8,128)S(1)} %get-tuple-element.35.looked), channel_id=1, replica_groups=mesh['seg'=2,'bundle'=16] {'bundle'}, dimensions={0} | all-to-all | bytes 1179648 | tf_op jit(solution)/shard_map/all_to_all | solution.py:534
  39.0 0.8 shard_map.109
  39.8 1.6 %collective-permute-start.1 = (f32[1,16,128]{2,1,0:T(8,128)S(1)}, f32[1,16,128]{2,1,0:T(8,128)S(1)}, u32[]{:S(2)}, u32[]{:S(2)}) collective-permute-start(f32[1,16,128]{2,1,0:T(8,128)S(1)} %get-tuple-element.39.order.end_offset), channel_id=1, source_target_pairs={{0,16},{16,0},{1,17},{17,1},{2,18},{18,2},{3,19},{19,3},{4,20},{20... | collective-permute-start | bytes 24584 | tf_op jit(solution)/shard_map/ppermute | solution.py:529
  41.4 0.6 shard_map.111.onehot
  42.0 0.8 shard_map.112.grid
  42.8 0.7 shard_map.110.local
  43.5 0.7 shard_map.113.rest_1_.looked
  44.2 0.0 collective-permute-done.1.other_offset
  44.2 0.5 shard_map.114
  44.8 17.3 %all_to_all.26.got = f32[16,64,128]{2,1,0:T(8,128)S(1)} all-to-all(f32[16,64,128]{2,1,0:T(8,128)S(1)} %get-tuple-element.42), channel_id=1, replica_groups=mesh['seg'=2,'bundle'=16] {'bundle'}, dimensions={0} | all-to-all | bytes 1048576 | tf_op jit(solution)/shard_map/all_to_all | solution.py:534
  62.0 0.8 shard_map.115
  62.8 0.8 collective-permute-start.2
  63.6 0.8 shard_map.117.grid
  64.3 0.7 shard_map.116.local
  65.1 0.7 shard_map.118.rest_1_.looked
  65.8 0.6 collective-permute-done.2.other_offset
  66.4 0.5 shard_map.119
  66.9 18.4 %all_to_all.27.got = f32[16,64,128]{2,1,0:T(8,128)S(1)} all-to-all(f32[16,64,128]{2,1,0:T(8,128)S(1)} %get-tuple-element.47), channel_id=1, replica_groups=mesh['seg'=2,'bundle'=16] {'bundle'}, dimensions={0} | all-to-all | bytes 1048576 | tf_op jit(solution)/shard_map/all_to_all | solution.py:534
  85.3 0.8 shard_map.120
  86.1 0.8 collective-permute-start.3
  86.9 0.8 shard_map.122.grid
  87.6 0.7 shard_map.121.local
  88.4 0.7 shard_map.123.rest_1_.looked
  89.1 0.6 collective-permute-done.3.other_offset
  89.7 0.5 shard_map.124
  90.2 18.4 %all_to_all.28.came = f32[16,64,128]{2,1,0:T(8,128)S(1)} all-to-all(f32[16,64,128]{2,1,0:T(8,128)S(1)} %get-tuple-element.51), channel_id=1, replica_groups=mesh['seg'=2,'bundle'=16] {'bundle'}, dimensions={0} | all-to-all | bytes 1048576 | tf_op jit(solution)/shard_map/all_to_all | solution.py:534
  108.6 1.5 %shard_map.125 = (f32[4,16,512]{2,1,0:T(8,128)}, f32[16,2048]{1,0:T(8,128)}) custom-call(f32[64,512]{1,0:T(8,128)S(1)} %get-tuple-element.50.spread, f32[16,64,128]{2,1,0:T(8,128)S(1)} %all_to_all.28.came, f32[16,128]{1,0:T(8,128)S(1)} %get-tuple-element.43.coupling, s32[16,128]{1,0:T(8,128)S(1)} %get-tuple-element.34.slot.rest_0_, ...), custom_call_target="tpu_custom_call" | custom-call | flops 1 | bytes 1 | tf_op jit(solution)/shard_map/pallas_call | solution.py:24
  (4 shorter events, 0.0 us)
Async XLA Ops:
  0.6 11.5 %copy-start.6 = (s32[1,4,4,1]{2,3,1,0:T(1,128)S(1)}, s32[1,4,4,1]{2,3,1,0:T(1,128)}, u32[]{:S(2)}) copy-start(s32[1,4,4,1]{2,3,1,0:T(1,128)} %param.16) | copy-start | bytes 196
  0.6 9.0 %copy-start.1 = (f32[4,512]{1,0:T(4,128)S(1)}, f32[4,512]{1,0:T(4,128)}, u32[]{:S(2)}) copy-start(f32[4,512]{1,0:T(4,128)} %coupling.1) | copy-start | bytes 24580
  0.7 9.0 %copy-start.7 = (f32[16]{0:T(128)S(1)}, f32[16]{0:T(128)}, u32[]{:S(2)}) copy-start(f32[16]{0:T(128)} %param.11) | copy-start | bytes 196
  0.7 9.0 %copy-start.2 = (f32[4,16,512]{2,1,0:T(8,128)S(1)}, f32[4,16,512]{2,1,0:T(8,128)}, u32[]{:S(2)}) copy-start(f32[4,16,512]{2,1,0:T(8,128)} %conc.1) | copy-start | bytes 393220
  0.7 11.4 %copy-start.5 = (f32[4,16]{1,0:T(4,128)S(1)}, f32[4,16]{1,0:T(4,128)}, u32[]{:S(2)}) copy-start(f32[4,16]{1,0:T(4,128)} %inlet.1) | copy-start | bytes 772
  0.7 11.4 %copy-start.3 = (f32[16,33]{1,0:T(8,128)S(1)}, f32[16,33]{1,0:T(8,128)}, u32[]{:S(2)}) copy-start(f32[16,33]{1,0:T(8,128)} %taps.1) | copy-start | bytes 6340
  0.7 15.4 %copy-start = (f32[16,2048]{1,0:T(8,128)S(1)}, f32[16,2048]{1,0:T(8,128)}, u32[]{:S(2)}) copy-start(f32[16,2048]{1,0:T(8,128)} %grid.3) | copy-start | bytes 393220
  0.7 15.4 %copy-start.4 = (f32[2048]{0:T(1024)S(1)}, f32[2048]{0:T(1024)}, u32[]{:S(2)}) copy-start(f32[2048]{0:T(1024)} %param.15) | copy-start | bytes 24580
  2.3 13.9 %all-to-all-start = ((s32[16,2,128]{2,1,0:T(2,128)}), s32[16,2,128]{2,1,0:T(2,128)S(1)}, u32[]{:S(2)}, u32[]{:S(2)}) async-start(s32[16,2,128]{2,1,0:T(2,128)} %shard_map.107), calls=%async_computation | async-start | bytes 32768 | tf_op jit(solution)/shard_map/all_to_all | solution.py:534
  10.5 3.8 %collective-permute-start = (f32[2,16,128]{2,1,0:T(8,128)S(1)}, f32[2,16,128]{2,1,0:T(8,128)S(1)}, u32[]{:S(2)}, u32[]{:S(2)}) collective-permute-start(f32[2,16,128]{2,1,0:T(8,128)S(1)} %get-tuple-element.32.end_offset.end_factor), channel_id=1, source_target_pairs={{0,16},{16,0},{1,17},{17,1},{2,18},{18,2},{3,19},{19,3},{4,20},{20... | collective-permute-start | bytes 49160 | tf_op jit(solution)/shard_map/ppermute | solution.py:529
  39.8 4.4 %collective-permute-start.1 = (f32[1,16,128]{2,1,0:T(8,128)S(1)}, f32[1,16,128]{2,1,0:T(8,128)S(1)}, u32[]{:S(2)}, u32[]{:S(2)}) collective-permute-start(f32[1,16,128]{2,1,0:T(8,128)S(1)} %get-tuple-element.39.order.end_offset), channel_id=1, source_target_pairs={{0,16},{16,0},{1,17},{17,1},{2,18},{18,2},{3,19},{19,3},{4,20},{20... | collective-permute-start | bytes 24584 | tf_op jit(solution)/shard_map/ppermute | solution.py:529
  62.8 3.7 %collective-permute-start.2 = (f32[1,16,128]{2,1,0:T(8,128)S(1)}, f32[1,16,128]{2,1,0:T(8,128)S(1)}, u32[]{:S(2)}, u32[]{:S(2)}) collective-permute-start(f32[1,16,128]{2,1,0:T(8,128)S(1)} %get-tuple-element.45.end_offset), channel_id=1, source_target_pairs={{0,16},{16,0},{1,17},{17,1},{2,18},{18,2},{3,19},{19,3},{4,20},{20... | collective-permute-start | bytes 24584 | tf_op jit(solution)/shard_map/ppermute | solution.py:529
  86.1 3.7 %collective-permute-start.3 = (f32[1,16,128]{2,1,0:T(8,128)S(1)}, f32[1,16,128]{2,1,0:T(8,128)S(1)}, u32[]{:S(2)}, u32[]{:S(2)}) collective-permute-start(f32[1,16,128]{2,1,0:T(8,128)S(1)} %get-tuple-element.49.end_offset), channel_id=1, source_target_pairs={{0,16},{16,0},{1,17},{17,1},{2,18},{18,2},{3,19},{19,3},{4,20},{20... | collective-permute-start | bytes 24584 | tf_op jit(solution)/shard_map/ppermute | solution.py:529

commit v7 on v6

--- a/solution.py
+++ b/solution.py
@@ -353,18 +353,6 @@
     outs[1][0] = packed
 
 
-def gather_cells(grid, cell, comps, high_total):
-    low = jnp.broadcast_to(cell & (LANES - 1), (comps, LANES))
-    high = jnp.broadcast_to(cell >> 7, (comps, LANES))
-    out = jnp.zeros((comps, LANES), F32)
-    for h in range(high_total):
-        g = jnp.take_along_axis(
-            grid[:, h * LANES : (h + 1) * LANES], low, axis=1, mode="promise_in_bounds"
-        )
-        out = jnp.where(high == h, g, out)
-    return out
-
-
 def look_by_matmul(cells, cap, onehot, stack, first, count, high_total, wide):
     rows = stack.shape[0] // 2
     comps = rows // high_total
@@ -411,20 +399,16 @@
     comps = grid.shape[0]
     wide = onehot.shape[0]
     high_total = grid.shape[1] // LANES
-    by_matmul = onehot.shape[1] // LANES
+    slots_total = cells.shape[0] * cap
     row = lax.broadcasted_iota(jnp.int32, (high_total, LANES), 0)
     stack_grid(grid, stack, wide)
-    for s in range(by_matmul):
+    for s in range(slots_total):
         put_onehot(onehot, s * LANES, cells[s // cap, s % cap : s % cap + 1, :])
-    for s in range(cells.shape[0] * cap):
+    for s in range(slots_total):
         owner, rank = s // cap, s % cap
         cell = cells[owner, rank : rank + 1, :]
         valid = cell >= 0
         cell = jnp.maximum(cell, 0)
-        if s >= by_matmul:
-            send[owner, rank * comps : (rank + 1) * comps, :] = gather_cells(
-                grid, cell, comps, high_total
-            )
         low = jnp.broadcast_to(cell & (LANES - 1), (high_total, LANES))
         k = jnp.take_along_axis(kappa[...], low, axis=1, mode="promise_in_bounds")
         rate = jnp.sum(jnp.where(row == (cell >> 7), k, 0.0), axis=0, keepdims=True)
@@ -432,19 +416,13 @@
         rates[owner, rank : rank + 1, :] = rate
         at = 2 * cap * comps + rank
         send[owner, at : at + 1, :] = rate
-    for first in range(0, by_matmul, 4):
+    for first in range(0, slots_total, 4):
         found = look_by_matmul(cells, cap, onehot, stack, first, 4, grid.shape[1] // wide, wide)
         for i in range(4):
             owner, rank = (first + i) // cap, (first + i) % cap
             send[owner, rank * comps : (rank + 1) * comps, :] = found[i]
     for b in range(slot.shape[0]):
         place(send, slot, b, cap, comps, tile(spread, b // groups, comps, b % groups))
-
-
-def onehot_kernel(cap, cells, order, onehot):
-    for owner in range(cells.shape[0]):
-        for rank in range(cap):
-            put_onehot(onehot, (owner * cap + rank) * LANES, cells[owner, rank : rank + 1, :])
 
 
 def update_kernel(cap, chunk, cells, got, looked, rates, onehot, grid, grid_out, masked):
@@ -547,7 +525,6 @@
     half = cap * comps
     extra = 8 * (-(-cap // 8))
     wide = 256 if cell_count % 256 == 0 else LANES
-    matmul_slots = owners_total * cap // 8 * 4
 
     owners = jnp.swapaxes(owners, 2, 3)
     (cell_send,) = call(
@@ -604,17 +581,17 @@
         )
 
     (spread,) = finish(None)
-    rates, send = call(
+    rates, send, onehot = call(
         functools.partial(look_first_kernel, groups, cap),
         [
             sds((owners_total, cap, LANES)), sds((owners_total, 2 * half + extra, LANES)),
+            sds((wide, owners_total * cap * LANES), BF16),
         ],
         [
             (cell_recv, VMEM), (grid, VMEM), (kappa.reshape(cell_count // LANES, LANES), VMEM),
             (spread, VMEM), (slot, VMEM),
         ],
         scratch=[
-            pltpu.VMEM((wide, matmul_slots * LANES), BF16),
             pltpu.VMEM((2 * (cell_count // wide) * comps, wide), BF16),
         ],
         flops=1e8,
@@ -662,12 +639,6 @@
         offset, ends = result[0], result[1]
         got_ends = swap(ends, segs)
         other_offset = got_ends if segs == 2 else got_ends[:, 0]
-        if step == 0:
-            (onehot,) = call(
-                functools.partial(onehot_kernel, cap),
-                [sds((wide, owners_total * cap * LANES), BF16)],
-                [(cell_recv, VMEM), (ends, ANY)],
-            )
         (grid,) = call(
             functools.partial(update_kernel, cap, chunk),
             [sds(grid.shape)],

time: 111 us -> 110 us (level)
  starting transfers between devices: 12.1 us -> 13.3 us
  waiting for transfers between devices: 3.03 us -> 1.83 us
    ppermute x4, starting transfers between devices: 4.71 us -> 5.95 us  [swap(): return lax.ppermute(x, 'seg', [(0, 1), (1, 0)])]
    ppermute x4, waiting for transfers between devices: 1.72 us -> 0.52 us  [swap(): return lax.ppermute(x, 'seg', [(0, 1), (1, 0)])]
    pallas_call x22 -> x21, Pallas kernels: 18.4 us -> 17.9 us  [call(): pl.pallas_call(kernel, out_shape=outs, in_specs=[s for _, s in ins], out_...]
  transfers between devices with their start and end apart: 5 -> 5, of which waited for: 4 -> 2; matrix products, arithmetic and copies ran while one was open for 0% -> 0% of each run, Pallas kernels for 9% -> 9%
where the time goes in v7:
time: 110 us
  blocking collectives  75.8 us (69%)
  Pallas kernels  17.9 us (16%)
  starting transfers between devices  13.3 us (12%)
  waiting for transfers between devices  1.83 us (2%)
    all_to_all x4, blocking collectives, exchange(): return lax.all_to_all(x, 'bundle', split_axis=0, concat_axis=0, tiled=True)  75.8 us
    pallas_call x21, Pallas kernels, call(): pl.pallas_call(kernel, out_shape=outs, in_specs=[s for _, s in ins], out_...  17.9 us
    all_to_all x1, starting transfers between devices, exchange(): return lax.all_to_all(x, 'bundle', split_axis=0, concat_axis=0, tiled=True)  7.37 us
    ppermute x4, starting transfers between devices, swap(): return lax.ppermute(x, 'seg', [(0, 1), (1, 0)])  5.95 us
  transfers between devices with their start and end apart: 5, of which 2 were waited for; matrix products, arithmetic and copies ran while one was open for 0% of the time, Pallas kernels for 9%

profile of v7, /device:TPU:0, one launch (start us, length us, event | category | flops | bytes accessed | tf_op | source)
XLA Modules:
  0.0 109.8 jit_solution(6172530055889749101)
XLA Ops:
  0.6 0.0 copy-start.6
  0.6 0.0 copy-start.1
  0.7 0.0 copy-start.7
  0.7 0.0 copy-start.2
  0.7 0.0 copy-start.5
  0.7 0.0 copy-start.3
  0.7 0.0 copy-start
  0.7 0.0 copy-start.4
  0.7 1.5 %shard_map.107 = s32[16,2,128]{2,1,0:T(2,128)} custom-call(s32[1,4,1,4]{3,2,1,0:T(1,128)} %bitcast.6, s32[4,512]{1,0:T(4,128)} %cells_in.1), custom_call_target="tpu_custom_call" | custom-call | flops 1000000000 | bytes 1 | tf_op jit(solution)/shard_map/pallas_call | solution.py:24
  2.3 7.4 %all-to-all-start = ((s32[16,2,128]{2,1,0:T(2,128)}), s32[16,2,128]{2,1,0:T(2,128)S(1)}, u32[]{:S(2)}, u32[]{:S(2)}) async-start(s32[16,2,128]{2,1,0:T(2,128)} %shard_map.107), calls=%async_computation | async-start | bytes 32768 | tf_op jit(solution)/shard_map/all_to_all | solution.py:512
  9.6 0.0 copy-done.1
  9.6 0.0 copy-done.7
  9.7 0.0 copy-done.2
  9.7 0.8 shard_map.104
  10.5 1.6 %collective-permute-start = (f32[2,16,128]{2,1,0:T(8,128)S(1)}, f32[2,16,128]{2,1,0:T(8,128)S(1)}, u32[]{:S(2)}, u32[]{:S(2)}) collective-permute-start(f32[2,16,128]{2,1,0:T(8,128)S(1)} %get-tuple-element.33.end_offset.end_factor), channel_id=1, source_target_pairs={{0,16},{16,0},{1,17},{17,1},{2,18},{18,2},{3,19},{19,3},{4,20},{20... | collective-permute-start | bytes 49160 | tf_op jit(solution)/shard_map/ppermute | solution.py:507
  12.1 0.0 copy-done.5
  12.1 1.7 %shard_map.105 = (f32[64,512]{1,0:T(8,128)S(1)}, f32[64,512]{1,0:T(8,128)S(1)}, f32[33,16,128]{2,1,0:T(8,128)S(1)}, f32[64,128]{1,0:T(8,128)S(1)}, s32[16,128]{1,0:T(8,128)S(1)}) custom-call(f32[16,33]{1,0:T(8,128)S(1)} %copy-done.3, f32[4,16]{1,0:T(4,128)S(1)} %copy-done.5, s32[1,4,1,4]{3,2,1,0:T(1,128)S(1)} %bitcast.7, ...), custom_call_target="tpu_custom_call" | custom-call | flops 100000000 | bytes 1 | tf_op jit(solution)/shard_map/pallas_call | solution.py:24
  13.8 0.5 collective-permute-done.other_offset.other_factor
  14.3 0.5 shard_map.106.spread
  14.8 1.3 %all-to-all-done.cells = s32[16,2,128]{2,1,0:T(2,128)S(1)} async-done(((s32[16,2,128]{2,1,0:T(2,128)}), s32[16,2,128]{2,1,0:T(2,128)S(1)}, u32[]{:S(2)}, u32[]{:S(2)}) %all-to-all-start) | async-done | bytes 16416 | tf_op jit(solution)/shard_map/all_to_all | solution.py:512
  16.1 0.0 copy-done.4
  16.1 1.2 %shard_map.108 = (f32[16,2,128]{2,1,0:T(2,128)S(1)}, f32[16,72,128]{2,1,0:T(8,128)S(1)}, bf16[256,4096]{1,0:T(8,128)(2,1)S(1)}) custom-call(s32[16,2,128]{2,1,0:T(2,128)S(1)} %all-to-all-done.cells, f32[16,2048]{1,0:T(8,128)S(1)} %copy-done, f32[16,128]{1,0:T(8,128)S(1)} %bitcast.5, f32[64,512]{1,0:T(8,128)S(1)} %shard_map.106.spread, ...), custom_call_target="tpu_custom_call" | custom-call | flops 100000000 | bytes 1 | tf_op jit(solution)/shard_map/pallas_call | solution.py:24
  17.4 21.8 %all_to_all.25.got = f32[16,72,128]{2,1,0:T(8,128)S(1)} all-to-all(f32[16,72,128]{2,1,0:T(8,128)S(1)} %get-tuple-element.36.looked), channel_id=1, replica_groups=mesh['seg'=2,'bundle'=16] {'bundle'}, dimensions={0} | all-to-all | bytes 1179648 | tf_op jit(solution)/shard_map/all_to_all | solution.py:512
  39.2 0.8 shard_map.109
  40.0 1.6 %collective-permute-start.1 = (f32[1,16,128]{2,1,0:T(8,128)S(1)}, f32[1,16,128]{2,1,0:T(8,128)S(1)}, u32[]{:S(2)}, u32[]{:S(2)}) collective-permute-start(f32[1,16,128]{2,1,0:T(8,128)S(1)} %get-tuple-element.40.end_offset), channel_id=1, source_target_pairs={{0,16},{16,0},{1,17},{17,1},{2,18},{18,2},{3,19},{19,3},{4,20},{20... | collective-permute-start | bytes 24584 | tf_op jit(solution)/shard_map/ppermute | solution.py:507
  41.5 0.8 shard_map.111.grid
  42.3 0.7 shard_map.110.local
  43.0 0.7 shard_map.112.rest_1_.looked
  43.8 0.0 collective-permute-done.1.other_offset
  43.8 0.5 shard_map.113
  44.3 17.3 %all_to_all.26.got = f32[16,64,128]{2,1,0:T(8,128)S(1)} all-to-all(f32[16,64,128]{2,1,0:T(8,128)S(1)} %get-tuple-element.44), channel_id=1, replica_groups=mesh['seg'=2,'bundle'=16] {'bundle'}, dimensions={0} | all-to-all | bytes 1048576 | tf_op jit(solution)/shard_map/all_to_all | solution.py:512
  61.5 0.8 shard_map.114
  62.3 1.4 %collective-permute-start.2 = (f32[1,16,128]{2,1,0:T(8,128)S(1)}, f32[1,16,128]{2,1,0:T(8,128)S(1)}, u32[]{:S(2)}, u32[]{:S(2)}) collective-permute-start(f32[1,16,128]{2,1,0:T(8,128)S(1)} %get-tuple-element.47.end_offset), channel_id=1, source_target_pairs={{0,16},{16,0},{1,17},{17,1},{2,18},{18,2},{3,19},{19,3},{4,20},{20... | collective-permute-start | bytes 24584 | tf_op jit(solution)/shard_map/ppermute | solution.py:507
  63.7 0.8 shard_map.116.grid
  64.5 0.7 shard_map.115.local
  65.2 0.7 shard_map.117.rest_1_.looked
  66.0 0.0 collective-permute-done.2.other_offset
  66.0 0.5 shard_map.118
  66.5 18.4 %all_to_all.27.got = f32[16,64,128]{2,1,0:T(8,128)S(1)} all-to-all(f32[16,64,128]{2,1,0:T(8,128)S(1)} %get-tuple-element.49), channel_id=1, replica_groups=mesh['seg'=2,'bundle'=16] {'bundle'}, dimensions={0} | all-to-all | bytes 1048576 | tf_op jit(solution)/shard_map/all_to_all | solution.py:512
  84.8 0.8 shard_map.119
  85.6 1.4 %collective-permute-start.3 = (f32[1,16,128]{2,1,0:T(8,128)S(1)}, f32[1,16,128]{2,1,0:T(8,128)S(1)}, u32[]{:S(2)}, u32[]{:S(2)}) collective-permute-start(f32[1,16,128]{2,1,0:T(8,128)S(1)} %get-tuple-element.51.end_offset), channel_id=1, source_target_pairs={{0,16},{16,0},{1,17},{17,1},{2,18},{18,2},{3,19},{19,3},{4,20},{20... | collective-permute-start | bytes 24584 | tf_op jit(solution)/shard_map/ppermute | solution.py:507
  87.0 0.8 shard_map.121.grid
  87.8 0.7 shard_map.120.local
  88.5 0.7 shard_map.122.rest_1_.looked
  89.3 0.0 collective-permute-done.3.other_offset
  89.3 0.5 shard_map.123
  89.8 18.4 %all_to_all.28.came = f32[16,64,128]{2,1,0:T(8,128)S(1)} all-to-all(f32[16,64,128]{2,1,0:T(8,128)S(1)} %get-tuple-element.53), channel_id=1, replica_groups=mesh['seg'=2,'bundle'=16] {'bundle'}, dimensions={0} | all-to-all | bytes 1048576 | tf_op jit(solution)/shard_map/all_to_all | solution.py:512
  108.1 1.5 %shard_map.124 = (f32[4,16,512]{2,1,0:T(8,128)}, f32[16,2048]{1,0:T(8,128)}) custom-call(f32[64,512]{1,0:T(8,128)S(1)} %get-tuple-element.52.spread, f32[16,64,128]{2,1,0:T(8,128)S(1)} %all_to_all.28.came, f32[16,128]{1,0:T(8,128)S(1)} %get-tuple-element.45.coupling, s32[16,128]{1,0:T(8,128)S(1)} %get-tuple-element.35.slot.rest_0_, ...), custom_call_target="tpu_custom_call" | custom-call | flops 1 | bytes 1 | tf_op jit(solution)/shard_map/pallas_call | solution.py:24
  (3 shorter events, 0.0 us)
Async XLA Ops:
  0.6 11.5 %copy-start.6 = (s32[1,4,4,1]{2,3,1,0:T(1,128)S(1)}, s32[1,4,4,1]{2,3,1,0:T(1,128)}, u32[]{:S(2)}) copy-start(s32[1,4,4,1]{2,3,1,0:T(1,128)} %param.16) | copy-start | bytes 196
  0.6 9.0 %copy-start.1 = (f32[4,512]{1,0:T(4,128)S(1)}, f32[4,512]{1,0:T(4,128)}, u32[]{:S(2)}) copy-start(f32[4,512]{1,0:T(4,128)} %coupling.1) | copy-start | bytes 24580
  0.7 9.0 %copy-start.7 = (f32[16]{0:T(128)S(1)}, f32[16]{0:T(128)}, u32[]{:S(2)}) copy-start(f32[16]{0:T(128)} %param.11) | copy-start | bytes 196
  0.7 9.0 %copy-start.2 = (f32[4,16,512]{2,1,0:T(8,128)S(1)}, f32[4,16,512]{2,1,0:T(8,128)}, u32[]{:S(2)}) copy-start(f32[4,16,512]{2,1,0:T(8,128)} %conc.1) | copy-start | bytes 393220
  0.7 11.4 %copy-start.5 = (f32[4,16]{1,0:T(4,128)S(1)}, f32[4,16]{1,0:T(4,128)}, u32[]{:S(2)}) copy-start(f32[4,16]{1,0:T(4,128)} %inlet.1) | copy-start | bytes 772
  0.7 11.4 %copy-start.3 = (f32[16,33]{1,0:T(8,128)S(1)}, f32[16,33]{1,0:T(8,128)}, u32[]{:S(2)}) copy-start(f32[16,33]{1,0:T(8,128)} %taps.1) | copy-start | bytes 6340
  0.7 15.4 %copy-start = (f32[16,2048]{1,0:T(8,128)S(1)}, f32[16,2048]{1,0:T(8,128)}, u32[]{:S(2)}) copy-start(f32[16,2048]{1,0:T(8,128)} %grid.3) | copy-start | bytes 393220
  0.7 15.4 %copy-start.4 = (f32[2048]{0:T(1024)S(1)}, f32[2048]{0:T(1024)}, u32[]{:S(2)}) copy-start(f32[2048]{0:T(1024)} %param.15) | copy-start | bytes 24580
  2.3 13.9 %all-to-all-start = ((s32[16,2,128]{2,1,0:T(2,128)}), s32[16,2,128]{2,1,0:T(2,128)S(1)}, u32[]{:S(2)}, u32[]{:S(2)}) async-start(s32[16,2,128]{2,1,0:T(2,128)} %shard_map.107), calls=%async_computation | async-start | bytes 32768 | tf_op jit(solution)/shard_map/all_to_all | solution.py:512
  10.5 3.8 %collective-permute-start = (f32[2,16,128]{2,1,0:T(8,128)S(1)}, f32[2,16,128]{2,1,0:T(8,128)S(1)}, u32[]{:S(2)}, u32[]{:S(2)}) collective-permute-start(f32[2,16,128]{2,1,0:T(8,128)S(1)} %get-tuple-element.33.end_offset.end_factor), channel_id=1, source_target_pairs={{0,16},{16,0},{1,17},{17,1},{2,18},{18,2},{3,19},{19,3},{4,20},{20... | collective-permute-start | bytes 49160 | tf_op jit(solution)/shard_map/ppermute | solution.py:507
  40.0 3.8 %collective-permute-start.1 = (f32[1,16,128]{2,1,0:T(8,128)S(1)}, f32[1,16,128]{2,1,0:T(8,128)S(1)}, u32[]{:S(2)}, u32[]{:S(2)}) collective-permute-start(f32[1,16,128]{2,1,0:T(8,128)S(1)} %get-tuple-element.40.end_offset), channel_id=1, source_target_pairs={{0,16},{16,0},{1,17},{17,1},{2,18},{18,2},{3,19},{19,3},{4,20},{20... | collective-permute-start | bytes 24584 | tf_op jit(solution)/shard_map/ppermute | solution.py:507
  62.3 3.7 %collective-permute-start.2 = (f32[1,16,128]{2,1,0:T(8,128)S(1)}, f32[1,16,128]{2,1,0:T(8,128)S(1)}, u32[]{:S(2)}, u32[]{:S(2)}) collective-permute-start(f32[1,16,128]{2,1,0:T(8,128)S(1)} %get-tuple-element.47.end_offset), channel_id=1, source_target_pairs={{0,16},{16,0},{1,17},{17,1},{2,18},{18,2},{3,19},{19,3},{4,20},{20... | collective-permute-start | bytes 24584 | tf_op jit(solution)/shard_map/ppermute | solution.py:507
  85.6 3.7 %collective-permute-start.3 = (f32[1,16,128]{2,1,0:T(8,128)S(1)}, f32[1,16,128]{2,1,0:T(8,128)S(1)}, u32[]{:S(2)}, u32[]{:S(2)}) collective-permute-start(f32[1,16,128]{2,1,0:T(8,128)S(1)} %get-tuple-element.51.end_offset), channel_id=1, source_target_pairs={{0,16},{16,0},{1,17},{17,1},{2,18},{18,2},{3,19},{19,3},{4,20},{20... | collective-permute-start | bytes 24584 | tf_op jit(solution)/shard_map/ppermute | solution.py:507

commit v8 on v7

--- a/solution.py
+++ b/solution.py
@@ -95,6 +95,12 @@
 
 
 LEVELS = 7
+TOGETHER = (
+    ((0, 1), (1, 2), (LEVELS + 2, 3)),
+    ((2, 4), (3, 8), (LEVELS + 3, 12)),
+    ((4, 16), (5, 32), (LEVELS + 4, 48)),
+    ((6, 64),),
+)
 
 
 def scan_lines(levels, retain, values, lines, comps, groups):
@@ -103,10 +109,13 @@
         (1.0 - tile(retain, line, comps, group)) * values[line * groups + group]
         for line, group in blocks
     ]
-    for level in range(LEVELS):
+    for terms in TOGETHER:
         offsets = [
             offset
-            + level_rows(levels, level, line, comps, group) * pltpu.roll(offset, 1 << level, 1)
+            + sum(
+                level_rows(levels, at, line, comps, group) * pltpu.roll(offset, shift, 1)
+                for at, shift in terms
+            )
             for offset, (line, group) in zip(offsets, blocks)
         ]
     out = []
@@ -216,7 +225,13 @@
             f = r
             for level in range(LEVELS):
                 inside = lane >= (1 << level)
-                levels[level, rows, span] = jnp.where(inside, f, 0.0)
+                masked = jnp.where(inside, f, 0.0)
+                levels[level, rows, span] = masked
+                if level % 2:
+                    levels[LEVELS + 2 + level // 2, rows, span] = masked * pltpu.roll(
+                        shorter, 1 << level, 1
+                    )
+                shorter = masked
                 f = jnp.where(inside, f * pltpu.roll(f, 1 << level, 1), f)
             levels[LEVELS, rows, span] = f
             end = last_lane(f)
@@ -543,7 +558,7 @@
     retain, levels, offset, factor, ends = call(
         functools.partial(first_kernel, lines, comps, groups),
         [
-            sds((rows, nodes)), sds((LEVELS + 2, rows, nodes)), sds((rows, nodes)),
+            sds((rows, nodes)), sds((LEVELS + 5, rows, nodes)), sds((rows, nodes)),
             sds((rows, nodes)), sds((2, comps, LANES)),
         ],
         [(conc, VMEM), (slowness, VMEM), (retard.reshape(1, comps), VMEM)],

time: 110 us -> 110 us (level)
  no operation moved by 1% of the time
where the time goes in v8:
time: 110 us
  blocking collectives  76.1 us (69%)
  Pallas kernels  17.7 us (16%)
  starting transfers between devices  13.3 us (12%)
  waiting for transfers between devices  1.58 us (1%)
    all_to_all x4, blocking collectives, exchange(): return lax.all_to_all(x, 'bundle', split_axis=0, concat_axis=0, tiled=True)  76.1 us
    pallas_call x21, Pallas kernels, call(): pl.pallas_call(kernel, out_shape=outs, in_specs=[s for _, s in ins], out_...  17.7 us
    all_to_all x1, starting transfers between devices, exchange(): return lax.all_to_all(x, 'bundle', split_axis=0, concat_axis=0, tiled=True)  7.37 us
    ppermute x4, starting transfers between devices, swap(): return lax.ppermute(x, 'seg', [(0, 1), (1, 0)])  5.96 us
  transfers between devices with their start and end apart: 5, of which 2 were waited for; matrix products, arithmetic and copies ran while one was open for 0% of the time, Pallas kernels for 9%

profile of v8, /device:TPU:0, one launch (start us, length us, event | category | flops | bytes accessed | tf_op | source)
XLA Modules:
  0.0 109.7 jit_solution(16971798853260498730)
XLA Ops:
  0.6 0.0 copy-start.6
  0.6 0.0 copy-start.1
  0.7 0.0 copy-start.7
  0.7 0.0 copy-start.2
  0.7 0.0 copy-start.5
  0.7 0.0 copy-start.3
  0.7 0.0 copy-start
  0.7 0.0 copy-start.4
  0.7 1.5 %shard_map.107 = s32[16,2,128]{2,1,0:T(2,128)} custom-call(s32[1,4,1,4]{3,2,1,0:T(1,128)} %bitcast.6, s32[4,512]{1,0:T(4,128)} %cells_in.1), custom_call_target="tpu_custom_call" | custom-call | flops 1000000000 | bytes 1 | tf_op jit(solution)/shard_map/pallas_call | solution.py:24
  2.3 7.4 %all-to-all-start = ((s32[16,2,128]{2,1,0:T(2,128)}), s32[16,2,128]{2,1,0:T(2,128)S(1)}, u32[]{:S(2)}, u32[]{:S(2)}) async-start(s32[16,2,128]{2,1,0:T(2,128)} %shard_map.107), calls=%async_computation | async-start | bytes 32768 | tf_op jit(solution)/shard_map/all_to_all | solution.py:527
  9.6 0.0 copy-done.1
  9.6 0.0 copy-done.7
  9.7 0.0 copy-done.2
  9.7 1.1 %shard_map.104 = (f32[64,512]{1,0:T(8,128)S(1)}, f32[12,64,512]{2,1,0:T(8,128)S(1)}, f32[64,512]{1,0:T(8,128)S(1)}, f32[64,512]{1,0:T(8,128)S(1)}, f32[2,16,128]{2,1,0:T(8,128)S(1)}) custom-call(f32[4,16,512]{2,1,0:T(8,128)S(1)} %copy-done.2, f32[4,512]{1,0:T(4,128)S(1)} %copy-done.1, f32[1,16]{1,0:T(1,128)S(1)} %bitcast.8), custom_call_target="tpu_custom_call" | custom-call | flops 100000000 | bytes 1 | tf_op jit(solution)/shard_map/pallas_call | solution.py:24
  10.8 1.6 %collective-permute-start = (f32[2,16,128]{2,1,0:T(8,128)S(1)}, f32[2,16,128]{2,1,0:T(8,128)S(1)}, u32[]{:S(2)}, u32[]{:S(2)}) collective-permute-start(f32[2,16,128]{2,1,0:T(8,128)S(1)} %get-tuple-element.33.end_offset.end_factor), channel_id=1, source_target_pairs={{0,16},{16,0},{1,17},{17,1},{2,18},{18,2},{3,19},{19,3},{4,20},{20... | collective-permute-start | bytes 49160 | tf_op jit(solution)/shard_map/ppermute | solution.py:522
  12.4 0.0 copy-done.6
  12.4 1.7 %shard_map.105 = (f32[64,512]{1,0:T(8,128)S(1)}, f32[64,512]{1,0:T(8,128)S(1)}, f32[33,16,128]{2,1,0:T(8,128)S(1)}, f32[64,128]{1,0:T(8,128)S(1)}, s32[16,128]{1,0:T(8,128)S(1)}) custom-call(f32[16,33]{1,0:T(8,128)S(1)} %copy-done.3, f32[4,16]{1,0:T(4,128)S(1)} %copy-done.5, s32[1,4,1,4]{3,2,1,0:T(1,128)S(1)} %bitcast.7, ...), custom_call_target="tpu_custom_call" | custom-call | flops 100000000 | bytes 1 | tf_op jit(solution)/shard_map/pallas_call | solution.py:24
  14.1 0.5 collective-permute-done.other_offset.other_factor
  14.6 0.5 shard_map.106.spread
  15.1 1.0 all-to-all-done.cells
  16.1 0.0 copy-done.4
  16.1 1.2 %shard_map.108 = (f32[16,2,128]{2,1,0:T(2,128)S(1)}, f32[16,72,128]{2,1,0:T(8,128)S(1)}, bf16[256,4096]{1,0:T(8,128)(2,1)S(1)}) custom-call(s32[16,2,128]{2,1,0:T(2,128)S(1)} %all-to-all-done.cells, f32[16,2048]{1,0:T(8,128)S(1)} %copy-done, f32[16,128]{1,0:T(8,128)S(1)} %bitcast.5, f32[64,512]{1,0:T(8,128)S(1)} %shard_map.106.spread, ...), custom_call_target="tpu_custom_call" | custom-call | flops 100000000 | bytes 1 | tf_op jit(solution)/shard_map/pallas_call | solution.py:24
  17.4 22.1 %all_to_all.25.got = f32[16,72,128]{2,1,0:T(8,128)S(1)} all-to-all(f32[16,72,128]{2,1,0:T(8,128)S(1)} %get-tuple-element.36.looked), channel_id=1, replica_groups=mesh['seg'=2,'bundle'=16] {'bundle'}, dimensions={0} | all-to-all | bytes 1179648 | tf_op jit(solution)/shard_map/all_to_all | solution.py:527
  39.5 0.6 shard_map.109
  40.1 1.6 %collective-permute-start.1 = (f32[1,16,128]{2,1,0:T(8,128)S(1)}, f32[1,16,128]{2,1,0:T(8,128)S(1)}, u32[]{:S(2)}, u32[]{:S(2)}) collective-permute-start(f32[1,16,128]{2,1,0:T(8,128)S(1)} %get-tuple-element.40.end_offset), channel_id=1, source_target_pairs={{0,16},{16,0},{1,17},{17,1},{2,18},{18,2},{3,19},{19,3},{4,20},{20... | collective-permute-start | bytes 24584 | tf_op jit(solution)/shard_map/ppermute | solution.py:522
  41.7 0.8 shard_map.111.grid
  42.4 0.7 shard_map.110.local
  43.2 0.7 shard_map.112.rest_1_.looked
  43.9 0.0 collective-permute-done.1.other_offset
  43.9 0.5 shard_map.113
  44.4 17.3 %all_to_all.26.got = f32[16,64,128]{2,1,0:T(8,128)S(1)} all-to-all(f32[16,64,128]{2,1,0:T(8,128)S(1)} %get-tuple-element.44), channel_id=1, replica_groups=mesh['seg'=2,'bundle'=16] {'bundle'}, dimensions={0} | all-to-all | bytes 1048576 | tf_op jit(solution)/shard_map/all_to_all | solution.py:527
  61.7 0.6 shard_map.114
  62.3 1.4 %collective-permute-start.2 = (f32[1,16,128]{2,1,0:T(8,128)S(1)}, f32[1,16,128]{2,1,0:T(8,128)S(1)}, u32[]{:S(2)}, u32[]{:S(2)}) collective-permute-start(f32[1,16,128]{2,1,0:T(8,128)S(1)} %get-tuple-element.47.end_offset), channel_id=1, source_target_pairs={{0,16},{16,0},{1,17},{17,1},{2,18},{18,2},{3,19},{19,3},{4,20},{20... | collective-permute-start | bytes 24584 | tf_op jit(solution)/shard_map/ppermute | solution.py:522
  63.7 0.8 shard_map.116.grid
  64.5 0.7 shard_map.115.local
  65.2 0.7 shard_map.117.rest_1_.looked
  65.9 0.0 collective-permute-done.2.other_offset
  66.0 0.5 shard_map.118
  66.5 18.4 %all_to_all.27.got = f32[16,64,128]{2,1,0:T(8,128)S(1)} all-to-all(f32[16,64,128]{2,1,0:T(8,128)S(1)} %get-tuple-element.49), channel_id=1, replica_groups=mesh['seg'=2,'bundle'=16] {'bundle'}, dimensions={0} | all-to-all | bytes 1048576 | tf_op jit(solution)/shard_map/all_to_all | solution.py:527
  84.8 0.6 shard_map.119
  85.5 1.4 %collective-permute-start.3 = (f32[1,16,128]{2,1,0:T(8,128)S(1)}, f32[1,16,128]{2,1,0:T(8,128)S(1)}, u32[]{:S(2)}, u32[]{:S(2)}) collective-permute-start(f32[1,16,128]{2,1,0:T(8,128)S(1)} %get-tuple-element.51.end_offset), channel_id=1, source_target_pairs={{0,16},{16,0},{1,17},{17,1},{2,18},{18,2},{3,19},{19,3},{4,20},{20... | collective-permute-start | bytes 24584 | tf_op jit(solution)/shard_map/ppermute | solution.py:522
  86.9 0.8 shard_map.121.grid
  87.6 0.7 shard_map.120.local
  88.4 0.7 shard_map.122.rest_1_.looked
  89.1 0.0 collective-permute-done.3.other_offset
  89.1 0.5 shard_map.123
  89.6 18.4 %all_to_all.28.came = f32[16,64,128]{2,1,0:T(8,128)S(1)} all-to-all(f32[16,64,128]{2,1,0:T(8,128)S(1)} %get-tuple-element.53), channel_id=1, replica_groups=mesh['seg'=2,'bundle'=16] {'bundle'}, dimensions={0} | all-to-all | bytes 1048576 | tf_op jit(solution)/shard_map/all_to_all | solution.py:527
  108.0 1.5 %shard_map.124 = (f32[4,16,512]{2,1,0:T(8,128)}, f32[16,2048]{1,0:T(8,128)}) custom-call(f32[64,512]{1,0:T(8,128)S(1)} %get-tuple-element.52.spread, f32[16,64,128]{2,1,0:T(8,128)S(1)} %all_to_all.28.came, f32[16,128]{1,0:T(8,128)S(1)} %get-tuple-element.45.coupling, s32[16,128]{1,0:T(8,128)S(1)} %get-tuple-element.35.slot.rest_0_, ...), custom_call_target="tpu_custom_call" | custom-call | flops 1 | bytes 1 | tf_op jit(solution)/shard_map/pallas_call | solution.py:24
  (3 shorter events, 0.0 us)
Async XLA Ops:
  0.6 11.7 %copy-start.6 = (s32[1,4,4,1]{2,3,1,0:T(1,128)S(1)}, s32[1,4,4,1]{2,3,1,0:T(1,128)}, u32[]{:S(2)}) copy-start(s32[1,4,4,1]{2,3,1,0:T(1,128)} %param.16) | copy-start | bytes 196
  0.6 9.0 %copy-start.1 = (f32[4,512]{1,0:T(4,128)S(1)}, f32[4,512]{1,0:T(4,128)}, u32[]{:S(2)}) copy-start(f32[4,512]{1,0:T(4,128)} %coupling.1) | copy-start | bytes 24580
  0.7 9.0 %copy-start.7 = (f32[16]{0:T(128)S(1)}, f32[16]{0:T(128)}, u32[]{:S(2)}) copy-start(f32[16]{0:T(128)} %param.11) | copy-start | bytes 196
  0.7 9.0 %copy-start.2 = (f32[4,16,512]{2,1,0:T(8,128)S(1)}, f32[4,16,512]{2,1,0:T(8,128)}, u32[]{:S(2)}) copy-start(f32[4,16,512]{2,1,0:T(8,128)} %conc.1) | copy-start | bytes 393220
  0.7 11.7 %copy-start.5 = (f32[4,16]{1,0:T(4,128)S(1)}, f32[4,16]{1,0:T(4,128)}, u32[]{:S(2)}) copy-start(f32[4,16]{1,0:T(4,128)} %inlet.1) | copy-start | bytes 772
  0.7 11.7 %copy-start.3 = (f32[16,33]{1,0:T(8,128)S(1)}, f32[16,33]{1,0:T(8,128)}, u32[]{:S(2)}) copy-start(f32[16,33]{1,0:T(8,128)} %taps.1) | copy-start | bytes 6340
  0.7 15.4 %copy-start = (f32[16,2048]{1,0:T(8,128)S(1)}, f32[16,2048]{1,0:T(8,128)}, u32[]{:S(2)}) copy-start(f32[16,2048]{1,0:T(8,128)} %grid.3) | copy-start | bytes 393220
  0.7 15.4 %copy-start.4 = (f32[2048]{0:T(1024)S(1)}, f32[2048]{0:T(1024)}, u32[]{:S(2)}) copy-start(f32[2048]{0:T(1024)} %param.15) | copy-start | bytes 24580
  2.3 13.9 %all-to-all-start = ((s32[16,2,128]{2,1,0:T(2,128)}), s32[16,2,128]{2,1,0:T(2,128)S(1)}, u32[]{:S(2)}, u32[]{:S(2)}) async-start(s32[16,2,128]{2,1,0:T(2,128)} %shard_map.107), calls=%async_computation | async-start | bytes 32768 | tf_op jit(solution)/shard_map/all_to_all | solution.py:527
  10.8 3.8 %collective-permute-start = (f32[2,16,128]{2,1,0:T(8,128)S(1)}, f32[2,16,128]{2,1,0:T(8,128)S(1)}, u32[]{:S(2)}, u32[]{:S(2)}) collective-permute-start(f32[2,16,128]{2,1,0:T(8,128)S(1)} %get-tuple-element.33.end_offset.end_factor), channel_id=1, source_target_pairs={{0,16},{16,0},{1,17},{17,1},{2,18},{18,2},{3,19},{19,3},{4,20},{20... | collective-permute-start | bytes 49160 | tf_op jit(solution)/shard_map/ppermute | solution.py:522
  40.1 3.8 %collective-permute-start.1 = (f32[1,16,128]{2,1,0:T(8,128)S(1)}, f32[1,16,128]{2,1,0:T(8,128)S(1)}, u32[]{:S(2)}, u32[]{:S(2)}) collective-permute-start(f32[1,16,128]{2,1,0:T(8,128)S(1)} %get-tuple-element.40.end_offset), channel_id=1, source_target_pairs={{0,16},{16,0},{1,17},{17,1},{2,18},{18,2},{3,19},{19,3},{4,20},{20... | collective-permute-start | bytes 24584 | tf_op jit(solution)/shard_map/ppermute | solution.py:522
  62.3 3.7 %collective-permute-start.2 = (f32[1,16,128]{2,1,0:T(8,128)S(1)}, f32[1,16,128]{2,1,0:T(8,128)S(1)}, u32[]{:S(2)}, u32[]{:S(2)}) collective-permute-start(f32[1,16,128]{2,1,0:T(8,128)S(1)} %get-tuple-element.47.end_offset), channel_id=1, source_target_pairs={{0,16},{16,0},{1,17},{17,1},{2,18},{18,2},{3,19},{19,3},{4,20},{20... | collective-permute-start | bytes 24584 | tf_op jit(solution)/shard_map/ppermute | solution.py:522
  85.5 3.7 %collective-permute-start.3 = (f32[1,16,128]{2,1,0:T(8,128)S(1)}, f32[1,16,128]{2,1,0:T(8,128)S(1)}, u32[]{:S(2)}, u32[]{:S(2)}) collective-permute-start(f32[1,16,128]{2,1,0:T(8,128)S(1)} %get-tuple-element.51.end_offset), channel_id=1, source_target_pairs={{0,16},{16,0},{1,17},{17,1},{2,18},{18,2},{3,19},{19,3},{4,20},{20... | collective-permute-start | bytes 24584 | tf_op jit(solution)/shard_map/ppermute | solution.py:522
